TPU v7x, 256 devices: a whole 4x4x8 slice. The times are simulated.
256 devices in a mesh: ex: 2 (over x_hi), ey: 2 (over x_lo), lin: 64 (over z, y, core).
Axes of the slice: x: 4 (x_hi: 2, x_lo: 2; x = x_hi * 2 + x_lo), y: 4, z: 8, core: 2. Of those that a mesh axis runs over, the one named last changes fastest.
Arguments:
- load: float32 [5, 5, 5, 4, 128, 256], P(None, None, None, None, ('ey', 'lin'), 'ex'), may hold values from -6 to 6
- kappa: float32 [4, 128, 256], P(None, ('ey', 'lin'), 'ex'), may hold values from 0.3 to 3
- wet: int32 [4, 128, 256], P(None, ('ey', 'lin'), 'ex'), may hold values 0 or 1
Outputs:
- solution: float32 [5, 5, 5, 4, 128, 256], P(None, None, None, None, ('ey', 'lin'), 'ex')
- residual: float32 [5, 5, 5, 4, 128, 256], P(None, None, None, None, ('ey', 'lin'), 'ex')
All inputs are finite; a program needn't handle non-finite values. No bound on the sum of `wet` on one device may be relied on, other than what follows from the above.
Results may differ from a plain program's by a relative error of at most 0.00016.
Values sent between devices are 32-bit elements; how exact they have to be, the bound alone decides.
No kernel may reach another device: no remote copies, remote signals or barrier semaphores. Data moves between devices by JAX's collectives and lax.ppermute only.
A program may use at most 64 MiB of HBM per device.

v0:
```python
import math

import jax
import jax.numpy as jnp
import numpy as np
from jax import lax
from jax.sharding import PartitionSpec as P

LOBATTO_NODES = 5
CYCLES = 2
NPRE = 2
NPOST = 2
NC = 4


fine_relax = 0.25
coarse_relax = 0.4


def padded_2(cells, sides, width):
    for axis, dim in sides:
        count = lax.axis_size(axis)
        ends = count - 1
        head = lax.slice_in_dim(cells, 0, width, axis=dim)
        tail = lax.slice_in_dim(cells, cells.shape[dim] - width, cells.shape[dim], axis=dim)
        cells = jnp.concatenate(
            [
                lax.ppermute(tail, axis, [(i, (i + 1) % count) for i in range(ends)]),
                cells,
                lax.ppermute(head, axis, [((i + 1) % count, i) for i in range(ends)]),
            ],
            axis=dim,
        )
    return cells


def node_tables():
    points = np.array([-1.0, -math.sqrt(3.0 / 7.0), 0.0, math.sqrt(3.0 / 7.0), 1.0])
    weights = np.array([0.1, 49.0 / 90.0, 32.0 / 45.0, 49.0 / 90.0, 0.1])
    eye_table = np.eye(points.shape[0])
    spread = points[:, None] - points[None, :] + eye_table
    factors = np.prod(spread, axis=1)
    deriv = factors[:, None] / (factors[None, :] * spread)
    deriv = np.where(eye_table > 0, (np.sum(1.0 / spread, axis=1) - 1.0)[:, None], deriv)
    stiff = deriv.T @ (weights[:, None] * deriv)
    mass = eye_table * weights[:, None]
    interp = np.stack([(1.0 - points) / 2.0, (1.0 + points) / 2.0], axis=1)
    coarse_stiff = interp.T @ stiff @ interp
    coarse_mass = interp.T @ mass @ interp
    return [
        jnp.asarray(table, jnp.float32)
        for table in (stiff, mass, interp, coarse_stiff, coarse_mass)
    ]


def along(matrix, field, axis):
    if axis == 0:
        return jnp.einsum("pa,a...->p...", matrix, field, precision=lax.Precision.HIGHEST)
    if axis == 1:
        return jnp.einsum("qb,ab...->aq...", matrix, field, precision=lax.Precision.HIGHEST)
    return jnp.einsum("rc,abc...->abr...", matrix, field, precision=lax.Precision.HIGHEST)


def element_apply(field, coeff, stiff, mass):
    mass_c = along(mass, field, 2)
    mass_bc = along(mass, mass_c, 1)
    first_term = along(stiff, mass_bc, 0)
    second_term = along(mass, along(stiff, mass_c, 1), 0)
    third_term = along(mass, along(mass, along(stiff, field, 2), 1), 0)
    return coeff * (first_term + second_term + third_term)


def element_diagonal(coeff, stiff, mass):
    stiff_diag = jnp.diagonal(stiff)
    mass_diag = jnp.diagonal(mass)
    local = (
        stiff_diag[:, None, None] * mass_diag[None, :, None] * mass_diag[None, None, :]
        + mass_diag[:, None, None] * stiff_diag[None, :, None] * mass_diag[None, None, :]
        + mass_diag[:, None, None] * mass_diag[None, :, None] * stiff_diag[None, None, :]
    )
    return local[:, :, :, None, None, None] * coeff[None, None, None]


def pair_sum(field, node_axis, fetch):
    count = field.shape[node_axis]
    lower = lax.index_in_dim(field, 0, node_axis, keepdims=False)
    upper = lax.index_in_dim(field, count - 1, node_axis, keepdims=False)
    elem_axis = node_axis + 2
    length = lower.shape[elem_axis]
    lower_first = lax.slice_in_dim(lower, 0, 1, axis=elem_axis)
    upper_last = lax.slice_in_dim(upper, length - 1, length, axis=elem_axis)
    outer = fetch(jnp.concatenate([lower_first, upper_last], axis=elem_axis))
    inner = lax.slice_in_dim(upper, 0, length - 1, axis=elem_axis) + lax.slice_in_dim(
        lower, 1, length, axis=elem_axis
    )
    head = lower_first + lax.slice_in_dim(outer, 0, 1, axis=elem_axis)
    tail = upper_last + lax.slice_in_dim(outer, 3, 4, axis=elem_axis)
    new_lower = jnp.concatenate([head, inner], axis=elem_axis)
    new_upper = jnp.concatenate([inner, tail], axis=elem_axis)
    middle = lax.slice_in_dim(field, 1, count - 1, axis=node_axis)
    return jnp.concatenate(
        [jnp.expand_dims(new_lower, node_axis), middle, jnp.expand_dims(new_upper, node_axis)],
        axis=node_axis,
    )


def pad_edge(axis):

    def padded(edge):
        widths = [(1, 1) if dim == axis else (0, 0) for dim in range(edge.ndim)]
        return jnp.pad(edge, widths)

    return padded


def along_shore(edge):
    return padded_2(edge, (("ex", 4),), 1)


def across_shore(edge):
    return padded_2(edge, ((("ey", "lin"), 3),), 1)


def assemble(field, fetch_x, fetch_y, fetch_z):
    field = pair_sum(field, 2, fetch_x)
    field = pair_sum(field, 1, fetch_y)
    return pair_sum(field, 0, fetch_z)


def surface_mask(count, layers, total):
    node = jnp.arange(count, dtype=jnp.int32)[:, None]
    layer = jnp.arange(layers, dtype=jnp.int32)[None, :]
    keep = jnp.where((node == count - 1) & (layer == total - 1), jnp.float32(0.0), jnp.float32(1.0))
    return keep.reshape(count, 1, 1, layers, 1, 1)


def coarse_sweeps(local, coeff, coarse_sum, keep, inverse, coarse_stiff, coarse_mass):
    restricted = keep * coarse_sum(local)
    correction = inverse * restricted
    for sweep in range(NC - 1):
        image = keep * coarse_sum(element_apply(correction, coeff, coarse_stiff, coarse_mass))
        correction = correction + inverse * (restricted - image)
    return correction


def multigrid(load, coeff, fine_sum, keep, coarse_correct, tables):
    stiff, mass, interp, coarse_stiff, coarse_mass = tables
    inverse = fine_relax / fine_sum(element_diagonal(coeff, stiff, mass))
    rhs = keep * fine_sum(load)
    solution = jnp.zeros_like(load)

    def sweep_once(solution):
        change = keep * fine_sum(load - element_apply(solution, coeff, stiff, mass))
        return solution + inverse * change

    transpose = interp.T
    for cycle in range(CYCLES):
        for sweep in range(NPRE):
            if cycle == 0 and sweep == 0:
                solution = solution + inverse * rhs
            else:
                solution = sweep_once(solution)
        local = load - element_apply(solution, coeff, stiff, mass)
        local = along(transpose, along(transpose, along(transpose, local, 2), 1), 0)
        correction = coarse_correct(local)
        solution = solution + along(interp, along(interp, along(interp, correction, 2), 1), 0)
        for sweep in range(NPOST):
            solution = sweep_once(solution)
    residual = keep * fine_sum(load - element_apply(solution, coeff, stiff, mass))
    return (solution, residual)


def per_device(load, kappa, wet):
    tables = node_tables()
    stiff, mass, interp, coarse_stiff, coarse_mass = tables
    coeff = kappa * jnp.where(wet == 1, jnp.float32(1.0), jnp.float32(0.05))
    layers = coeff.shape[0]

    def block_sum(field):
        return assemble(field, along_shore, across_shore, pad_edge(2))

    fine_retain_mask = surface_mask(LOBATTO_NODES, layers, layers)
    coarse_retain_mask = surface_mask(2, layers, layers)
    coarse_inverse = coarse_relax / block_sum(element_diagonal(coeff, coarse_stiff, coarse_mass))

    def coarse_correct(local):
        return coarse_sweeps(
            local, coeff, block_sum, coarse_retain_mask, coarse_inverse, coarse_stiff, coarse_mass
        )

    return multigrid(load, coeff, block_sum, fine_retain_mask, coarse_correct, tables)


def solution(mesh):
    in_specs = (
        P(None, None, None, None, ("ey", "lin"), "ex"),
        P(None, ("ey", "lin"), "ex"),
        P(None, ("ey", "lin"), "ex"),
    )
    out_specs = (
        P(None, None, None, None, ("ey", "lin"), "ex"),
        P(None, None, None, None, ("ey", "lin"), "ex"),
    )
    return jax.shard_map(
        per_device, mesh=mesh, in_specs=in_specs, out_specs=out_specs, check_vma=False
    )
```

profile of v0, /device:TPU:2, one launch (start us, length us, event | category | flops | bytes accessed | tf_op | source)
XLA Modules:
  0.0 502.3 jit_solution(9532024850963704284)
XLA Ops:
  3.0 4.0 collective-permute-start.12
  13.6 5.7 %collective-permute-done.13 = f32[2,2,4,1,1]{4,2,0,1,3:T(4,128)S(1)} collective-permute-done((f32[2,2,4,1,1]{4,2,0,1,3:T(4,128)S(1)}, f32[2,2,4,1,1]{4,2,0,1,3:T(4,128)S(1)}, u32[]{:S(2)}, u32[]{:S(2)}) %collective-permute-start.13) | collective-permute-done | bytes 96 | tf_op jit(solution)/shard_map/ppermute | solution.py:30
  22.1 4.9 collective-permute-done.1
  27.3 1.9 collective-permute-start.2
  29.4 3.6 collective-permute-start.6
  33.0 4.0 collective-permute-done.2
  37.0 4.1 collective-permute-start.3
  41.2 4.8 collective-permute-start.7
  55.3 1.9 collective-permute-start.14
  58.8 6.4 %collective-permute-done.9 = f32[5,5,4,1,1]{4,0,2,1,3:T(8,128)S(1)} collective-permute-done((f32[5,5,4,1,1]{4,0,2,1,3:T(8,128)S(1)}, f32[5,5,4,1,1]{4,0,2,1,3:T(8,128)S(1)}, u32[]{:S(2)}, u32[]{:S(2)}) %collective-permute-start.9) | collective-permute-done | bytes 432 | tf_op jit(solution)/shard_map/ppermute | solution.py:30
  66.4 1.9 collective-permute-start.10
  68.3 7.9 %collective-permute-start.11 = (f32[5,5,4,1,128]{4,0,2,1,3:T(8,128)S(1)}, f32[5,5,4,1,128]{4,0,2,1,3:T(8,128)S(1)}, u32[]{:S(2)}, u32[]{:S(2)}) collective-permute-start(f32[5,5,4,1,128]{4,0,2,1,3:T(8,128)S(1)} %get-tuple-element.49), channel_id=1, source_target_pairs={{1,0},{2,1},{3,2},{4,3},{5,4},{6,5},{7,6},{8,7},{9,8},{10,9},{11,1... | collective-permute-start | bytes 153608 | tf_op jit(solution)/shard_map/ppermute | solution.py:30
  76.2 2.8 collective-permute-start.15
  90.3 5.7 %collective-permute-done.17 = f32[2,2,4,1,1]{4,0,2,1,3:T(2,128)S(1)} collective-permute-done((f32[2,2,4,1,1]{4,0,2,1,3:T(2,128)S(1)}, f32[2,2,4,1,1]{4,0,2,1,3:T(2,128)S(1)}, u32[]{:S(2)}, u32[]{:S(2)}) %collective-permute-start.17) | collective-permute-done | bytes 96 | tf_op jit(solution)/shard_map/ppermute | solution.py:30
  96.2 1.9 collective-permute-start.18
  98.1 7.2 %collective-permute-done.18 = f32[2,2,4,1,128]{4,0,2,1,3:T(2,128)S(1)} collective-permute-done((f32[2,2,4,1,128]{4,0,2,1,3:T(2,128)S(1)}, f32[2,2,4,1,128]{4,0,2,1,3:T(2,128)S(1)}, u32[]{:S(2)}, u32[]{:S(2)}) %collective-permute-start.18) | collective-permute-done | bytes 8224 | tf_op jit(solution)/shard_map/ppermute | solution.py:28
  105.4 1.9 collective-permute-start.19
  116.0 5.7 %collective-permute-done.21 = f32[2,2,4,1,1]{4,2,0,1,3:T(4,128)S(1)} collective-permute-done((f32[2,2,4,1,1]{4,2,0,1,3:T(4,128)S(1)}, f32[2,2,4,1,1]{4,2,0,1,3:T(4,128)S(1)}, u32[]{:S(2)}, u32[]{:S(2)}) %collective-permute-start.21) | collective-permute-done | bytes 96 | tf_op jit(solution)/shard_map/ppermute | solution.py:30
  121.8 1.9 collective-permute-start.22
  123.7 7.3 %collective-permute-done.22 = f32[2,2,4,1,128]{4,2,1,0,3:T(4,128)S(1)} collective-permute-done((f32[2,2,4,1,128]{4,2,1,0,3:T(4,128)S(1)}, f32[2,2,4,1,128]{4,2,1,0,3:T(4,128)S(1)}, u32[]{:S(2)}, u32[]{:S(2)}) %collective-permute-start.22) | collective-permute-done | bytes 8224 | tf_op jit(solution)/shard_map/ppermute | solution.py:28
  140.5 5.7 %collective-permute-done.25 = f32[2,2,4,1,1]{4,2,0,1,3:T(4,128)S(1)} collective-permute-done((f32[2,2,4,1,1]{4,2,0,1,3:T(4,128)S(1)}, f32[2,2,4,1,1]{4,2,0,1,3:T(4,128)S(1)}, u32[]{:S(2)}, u32[]{:S(2)}) %collective-permute-start.25) | collective-permute-done | bytes 96 | tf_op jit(solution)/shard_map/ppermute | solution.py:30
  146.3 1.9 collective-permute-start.26
  148.2 7.3 %collective-permute-done.26 = f32[2,2,4,1,128]{4,2,1,0,3:T(4,128)S(1)} collective-permute-done((f32[2,2,4,1,128]{4,2,1,0,3:T(4,128)S(1)}, f32[2,2,4,1,128]{4,2,1,0,3:T(4,128)S(1)}, u32[]{:S(2)}, u32[]{:S(2)}) %collective-permute-start.26) | collective-permute-done | bytes 8224 | tf_op jit(solution)/shard_map/ppermute | solution.py:28
  165.0 5.7 %collective-permute-done.29 = f32[2,2,4,1,1]{4,2,0,1,3:T(4,128)S(1)} collective-permute-done((f32[2,2,4,1,1]{4,2,0,1,3:T(4,128)S(1)}, f32[2,2,4,1,1]{4,2,0,1,3:T(4,128)S(1)}, u32[]{:S(2)}, u32[]{:S(2)}) %collective-permute-start.29) | collective-permute-done | bytes 96 | tf_op jit(solution)/shard_map/ppermute | solution.py:30
  170.8 1.9 collective-permute-start.30
  172.7 7.3 %collective-permute-done.30 = f32[2,2,4,1,128]{4,2,1,0,3:T(4,128)S(1)} collective-permute-done((f32[2,2,4,1,128]{4,2,1,0,3:T(4,128)S(1)}, f32[2,2,4,1,128]{4,2,1,0,3:T(4,128)S(1)}, u32[]{:S(2)}, u32[]{:S(2)}) %collective-permute-start.30) | collective-permute-done | bytes 8224 | tf_op jit(solution)/shard_map/ppermute | solution.py:28
  180.0 2.1 collective-permute-start.31
  194.7 6.1 %collective-permute-done.33 = f32[5,5,4,1,1]{4,2,0,1,3:T(4,128)S(1)} collective-permute-done((f32[5,5,4,1,1]{4,2,0,1,3:T(4,128)S(1)}, f32[5,5,4,1,1]{4,2,0,1,3:T(4,128)S(1)}, u32[]{:S(2)}, u32[]{:S(2)}) %collective-permute-start.33) | collective-permute-done | bytes 432 | tf_op jit(solution)/shard_map/ppermute | solution.py:30
  201.1 1.9 collective-permute-start.34
  203.0 7.8 %collective-permute-done.34 = f32[5,5,4,1,128]{4,2,1,0,3:T(4,128)S(1)} collective-permute-done((f32[5,5,4,1,128]{4,2,1,0,3:T(4,128)S(1)}, f32[5,5,4,1,128]{4,2,1,0,3:T(4,128)S(1)}, u32[]{:S(2)}, u32[]{:S(2)}) %collective-permute-start.34) | collective-permute-done | bytes 51232 | tf_op jit(solution)/shard_map/ppermute | solution.py:28
  210.9 2.1 collective-permute-start.35
  224.9 6.1 %collective-permute-done.37 = f32[5,5,4,1,1]{4,2,0,1,3:T(4,128)S(1)} collective-permute-done((f32[5,5,4,1,1]{4,2,0,1,3:T(4,128)S(1)}, f32[5,5,4,1,1]{4,2,0,1,3:T(4,128)S(1)}, u32[]{:S(2)}, u32[]{:S(2)}) %collective-permute-start.37) | collective-permute-done | bytes 432 | tf_op jit(solution)/shard_map/ppermute | solution.py:30
  231.3 1.9 collective-permute-start.38
  233.2 7.7 %collective-permute-done.38 = f32[5,5,4,1,128]{4,2,1,0,3:T(4,128)S(1)} collective-permute-done((f32[5,5,4,1,128]{4,2,1,0,3:T(4,128)S(1)}, f32[5,5,4,1,128]{4,2,1,0,3:T(4,128)S(1)}, u32[]{:S(2)}, u32[]{:S(2)}) %collective-permute-start.38) | collective-permute-done | bytes 51232 | tf_op jit(solution)/shard_map/ppermute | solution.py:28
  240.9 1.9 collective-permute-start.39
  255.5 5.7 %collective-permute-done.41 = f32[5,5,4,1,1]{4,2,0,1,3:T(4,128)S(1)} collective-permute-done((f32[5,5,4,1,1]{4,2,0,1,3:T(4,128)S(1)}, f32[5,5,4,1,1]{4,2,0,1,3:T(4,128)S(1)}, u32[]{:S(2)}, u32[]{:S(2)}) %collective-permute-start.41) | collective-permute-done | bytes 432 | tf_op jit(solution)/shard_map/ppermute | solution.py:30
  261.4 1.9 collective-permute-start.42
  263.4 7.7 %collective-permute-done.42 = f32[5,5,4,1,128]{4,2,1,0,3:T(4,128)S(1)} collective-permute-done((f32[5,5,4,1,128]{4,2,1,0,3:T(4,128)S(1)}, f32[5,5,4,1,128]{4,2,1,0,3:T(4,128)S(1)}, u32[]{:S(2)}, u32[]{:S(2)}) %collective-permute-start.42) | collective-permute-done | bytes 51232 | tf_op jit(solution)/shard_map/ppermute | solution.py:28
  271.1 1.9 collective-permute-start.43
  285.2 6.1 %collective-permute-done.45 = f32[5,5,4,1,1]{4,2,0,1,3:T(4,128)S(1)} collective-permute-done((f32[5,5,4,1,1]{4,2,0,1,3:T(4,128)S(1)}, f32[5,5,4,1,1]{4,2,0,1,3:T(4,128)S(1)}, u32[]{:S(2)}, u32[]{:S(2)}) %collective-permute-start.45) | collective-permute-done | bytes 432 | tf_op jit(solution)/shard_map/ppermute | solution.py:30
  291.6 1.9 collective-permute-start.46
  293.5 7.7 %collective-permute-done.46 = f32[5,5,4,1,128]{4,2,1,0,3:T(4,128)S(1)} collective-permute-done((f32[5,5,4,1,128]{4,2,1,0,3:T(4,128)S(1)}, f32[5,5,4,1,128]{4,2,1,0,3:T(4,128)S(1)}, u32[]{:S(2)}, u32[]{:S(2)}) %collective-permute-start.46) | collective-permute-done | bytes 51232 | tf_op jit(solution)/shard_map/ppermute | solution.py:28
  301.3 1.9 collective-permute-start.47
  315.9 5.7 %collective-permute-done.49 = f32[2,2,4,1,1]{4,2,0,1,3:T(4,128)S(1)} collective-permute-done((f32[2,2,4,1,1]{4,2,0,1,3:T(4,128)S(1)}, f32[2,2,4,1,1]{4,2,0,1,3:T(4,128)S(1)}, u32[]{:S(2)}, u32[]{:S(2)}) %collective-permute-start.49) | collective-permute-done | bytes 96 | tf_op jit(solution)/shard_map/ppermute | solution.py:30
  321.7 1.9 collective-permute-start.50
  323.7 7.3 %collective-permute-done.50 = f32[2,2,4,1,128]{4,2,1,0,3:T(4,128)S(1)} collective-permute-done((f32[2,2,4,1,128]{4,2,1,0,3:T(4,128)S(1)}, f32[2,2,4,1,128]{4,2,1,0,3:T(4,128)S(1)}, u32[]{:S(2)}, u32[]{:S(2)}) %collective-permute-start.50) | collective-permute-done | bytes 8224 | tf_op jit(solution)/shard_map/ppermute | solution.py:28
  340.4 5.7 %collective-permute-done.53 = f32[2,2,4,1,1]{4,2,0,1,3:T(4,128)S(1)} collective-permute-done((f32[2,2,4,1,1]{4,2,0,1,3:T(4,128)S(1)}, f32[2,2,4,1,1]{4,2,0,1,3:T(4,128)S(1)}, u32[]{:S(2)}, u32[]{:S(2)}) %collective-permute-start.53) | collective-permute-done | bytes 96 | tf_op jit(solution)/shard_map/ppermute | solution.py:30
  346.2 1.9 collective-permute-start.54
  348.2 7.3 %collective-permute-done.54 = f32[2,2,4,1,128]{4,2,1,0,3:T(4,128)S(1)} collective-permute-done((f32[2,2,4,1,128]{4,2,1,0,3:T(4,128)S(1)}, f32[2,2,4,1,128]{4,2,1,0,3:T(4,128)S(1)}, u32[]{:S(2)}, u32[]{:S(2)}) %collective-permute-start.54) | collective-permute-done | bytes 8224 | tf_op jit(solution)/shard_map/ppermute | solution.py:28
  364.9 5.7 %collective-permute-done.57 = f32[2,2,4,1,1]{4,2,0,1,3:T(4,128)S(1)} collective-permute-done((f32[2,2,4,1,1]{4,2,0,1,3:T(4,128)S(1)}, f32[2,2,4,1,1]{4,2,0,1,3:T(4,128)S(1)}, u32[]{:S(2)}, u32[]{:S(2)}) %collective-permute-start.57) | collective-permute-done | bytes 96 | tf_op jit(solution)/shard_map/ppermute | solution.py:30
  372.7 7.3 %collective-permute-done.58 = f32[2,2,4,1,128]{4,2,1,0,3:T(4,128)S(1)} collective-permute-done((f32[2,2,4,1,128]{4,2,1,0,3:T(4,128)S(1)}, f32[2,2,4,1,128]{4,2,1,0,3:T(4,128)S(1)}, u32[]{:S(2)}, u32[]{:S(2)}) %collective-permute-start.58) | collective-permute-done | bytes 8224 | tf_op jit(solution)/shard_map/ppermute | solution.py:28
  389.4 5.7 %collective-permute-done.61 = f32[2,2,4,1,1]{4,2,0,1,3:T(4,128)S(1)} collective-permute-done((f32[2,2,4,1,1]{4,2,0,1,3:T(4,128)S(1)}, f32[2,2,4,1,1]{4,2,0,1,3:T(4,128)S(1)}, u32[]{:S(2)}, u32[]{:S(2)}) %collective-permute-start.61) | collective-permute-done | bytes 96 | tf_op jit(solution)/shard_map/ppermute | solution.py:30
  395.2 1.9 collective-permute-start.62
  397.2 7.3 %collective-permute-done.62 = f32[2,2,4,1,128]{4,2,0,1,3:T(4,128)S(1)} collective-permute-done((f32[2,2,4,1,128]{4,2,0,1,3:T(4,128)S(1)}, f32[2,2,4,1,128]{4,2,0,1,3:T(4,128)S(1)}, u32[]{:S(2)}, u32[]{:S(2)}) %collective-permute-start.62) | collective-permute-done | bytes 8224 | tf_op jit(solution)/shard_map/ppermute | solution.py:28
  404.4 2.1 collective-permute-start.63
  419.2 6.1 %collective-permute-done.65 = f32[5,5,4,1,1]{4,2,0,1,3:T(4,128)S(1)} collective-permute-done((f32[5,5,4,1,1]{4,2,0,1,3:T(4,128)S(1)}, f32[5,5,4,1,1]{4,2,0,1,3:T(4,128)S(1)}, u32[]{:S(2)}, u32[]{:S(2)}) %collective-permute-start.65) | collective-permute-done | bytes 432 | tf_op jit(solution)/shard_map/ppermute | solution.py:30
  425.5 1.9 collective-permute-start.66
  427.4 7.7 %collective-permute-done.66 = f32[5,5,4,1,128]{4,2,0,1,3:T(4,128)S(1)} collective-permute-done((f32[5,5,4,1,128]{4,2,0,1,3:T(4,128)S(1)}, f32[5,5,4,1,128]{4,2,0,1,3:T(4,128)S(1)}, u32[]{:S(2)}, u32[]{:S(2)}) %collective-permute-start.66) | collective-permute-done | bytes 51232 | tf_op jit(solution)/shard_map/ppermute | solution.py:28
  435.2 2.1 collective-permute-start.67
  449.4 6.1 %collective-permute-done.69 = f32[5,5,4,1,1]{4,2,0,1,3:T(4,128)S(1)} collective-permute-done((f32[5,5,4,1,1]{4,2,0,1,3:T(4,128)S(1)}, f32[5,5,4,1,1]{4,2,0,1,3:T(4,128)S(1)}, u32[]{:S(2)}, u32[]{:S(2)}) %collective-permute-start.69) | collective-permute-done | bytes 432 | tf_op jit(solution)/shard_map/ppermute | solution.py:30
  455.7 1.9 collective-permute-start.70
  457.6 7.7 %collective-permute-done.70 = f32[5,5,4,1,128]{4,2,1,0,3:T(4,128)S(1)} collective-permute-done((f32[5,5,4,1,128]{4,2,1,0,3:T(4,128)S(1)}, f32[5,5,4,1,128]{4,2,1,0,3:T(4,128)S(1)}, u32[]{:S(2)}, u32[]{:S(2)}) %collective-permute-start.70) | collective-permute-done | bytes 51232 | tf_op jit(solution)/shard_map/ppermute | solution.py:28
  479.6 6.1 %collective-permute-done.73 = f32[5,5,4,1,1]{4,2,0,1,3:T(4,128)S(1)} collective-permute-done((f32[5,5,4,1,1]{4,2,0,1,3:T(4,128)S(1)}, f32[5,5,4,1,1]{4,2,0,1,3:T(4,128)S(1)}, u32[]{:S(2)}, u32[]{:S(2)}) %collective-permute-start.73) | collective-permute-done | bytes 432 | tf_op jit(solution)/shard_map/ppermute | solution.py:30
  487.9 7.7 %collective-permute-done.74 = f32[5,5,4,1,128]{4,2,0,1,3:T(4,128)S(1)} collective-permute-done((f32[5,5,4,1,128]{4,2,0,1,3:T(4,128)S(1)}, f32[5,5,4,1,128]{4,2,0,1,3:T(4,128)S(1)}, u32[]{:S(2)}, u32[]{:S(2)}) %collective-permute-start.74) | collective-permute-done | bytes 51232 | tf_op jit(solution)/shard_map/ppermute | solution.py:28
  (628 shorter events, 202.6 us)
Async XLA Ops:
  3.0 9.2 %collective-permute-start.12 = (f32[2,2,4,1,1]{4,2,0,1,3:T(4,128)S(1)}, f32[2,2,4,1,1]{4,2,0,1,3:T(4,128)S(1)}, u32[]{:S(2)}, u32[]{:S(2)}) collective-permute-start(f32[2,2,4,1,1]{4,2,0,1,3:T(4,128)S(1)} %slice.1268), channel_id=1, source_target_pairs={{0,128},{1,129},{2,130},{3,131},{4,132},{5,133},{6,134},{7,135},{8... | collective-permute-start | bytes 200 | tf_op jit(solution)/shard_map/ppermute | solution.py:28
  8.9 10.5 %collective-permute-start = (f32[5,5,4,1,1]{4,2,0,1,3:T(4,128)S(1)}, f32[5,5,4,1,1]{4,2,0,1,3:T(4,128)S(1)}, u32[]{:S(2)}, u32[]{:S(2)}) collective-permute-start(f32[5,5,4,1,1]{4,2,0,1,3:T(4,128)S(1)} %slice.1233), channel_id=1, source_target_pairs={{0,128},{1,129},{2,130},{3,131},{4,132},{5,133},{6,134},{7,135},{8... | collective-permute-start | bytes 1208 | tf_op jit(solution)/shard_map/ppermute | solution.py:28
  10.4 10.4 %collective-permute-start.4 = (f32[5,5,4,1,1]{4,2,0,1,3:T(4,128)S(1)}, f32[5,5,4,1,1]{4,2,0,1,3:T(4,128)S(1)}, u32[]{:S(2)}, u32[]{:S(2)}) collective-permute-start(f32[5,5,4,1,1]{4,2,0,1,3:T(4,128)S(1)} %slice.1244), channel_id=1, source_target_pairs={{0,128},{1,129},{2,130},{3,131},{4,132},{5,133},{6,134},{7,135},{8... | collective-permute-start | bytes 1208 | tf_op jit(solution)/shard_map/ppermute | solution.py:28
  12.2 7.0 %collective-permute-start.13 = (f32[2,2,4,1,1]{4,2,0,1,3:T(4,128)S(1)}, f32[2,2,4,1,1]{4,2,0,1,3:T(4,128)S(1)}, u32[]{:S(2)}, u32[]{:S(2)}) collective-permute-start(f32[2,2,4,1,1]{4,2,0,1,3:T(4,128)S(1)} %get-tuple-element.231), channel_id=1, source_target_pairs={{128,0},{129,1},{130,2},{131,3},{132,4},{133,5},{134,6},{135,7},{1... | collective-permute-start | bytes 200 | tf_op jit(solution)/shard_map/ppermute | solution.py:30
  19.5 7.5 %collective-permute-start.1 = (f32[5,5,4,1,1]{4,2,0,1,3:T(4,128)S(1)}, f32[5,5,4,1,1]{4,2,0,1,3:T(4,128)S(1)}, u32[]{:S(2)}, u32[]{:S(2)}) collective-permute-start(f32[5,5,4,1,1]{4,2,0,1,3:T(4,128)S(1)} %get-tuple-element.143), channel_id=1, source_target_pairs={{128,0},{129,1},{130,2},{131,3},{132,4},{133,5},{134,6},{135,7},{1... | collective-permute-start | bytes 1208 | tf_op jit(solution)/shard_map/ppermute | solution.py:30
  20.8 8.4 %collective-permute-start.5 = (f32[5,5,4,1,1]{4,2,0,1,3:T(4,128)S(1)}, f32[5,5,4,1,1]{4,2,0,1,3:T(4,128)S(1)}, u32[]{:S(2)}, u32[]{:S(2)}) collective-permute-start(f32[5,5,4,1,1]{4,2,0,1,3:T(4,128)S(1)} %get-tuple-element.149), channel_id=1, source_target_pairs={{128,0},{129,1},{130,2},{131,3},{132,4},{133,5},{134,6},{135,7},{1... | collective-permute-start | bytes 1208 | tf_op jit(solution)/shard_map/ppermute | solution.py:30
  27.3 9.7 %collective-permute-start.2 = (f32[5,5,4,1,128]{4,2,1,0,3:T(4,128)S(1)}, f32[5,5,4,1,128]{4,2,1,0,3:T(4,128)S(1)}, u32[]{:S(2)}, u32[]{:S(2)}) collective-permute-start(f32[5,5,4,1,128]{4,2,1,0,3:T(4,128)S(1)} %maximum_bitcast_fusion.32), channel_id=1, source_target_pairs={{0,1},{1,2},{2,3},{3,4},{4,5},{5,6},{6,7},{7,8},{8,9},{9,10},{10,1... | collective-permute-start | bytes 153608 | tf_op jit(solution)/shard_map/ppermute | solution.py:28
  29.4 11.7 %collective-permute-start.6 = (f32[5,5,4,1,128]{4,2,1,0,3:T(4,128)S(1)}, f32[5,5,4,1,128]{4,2,1,0,3:T(4,128)S(1)}, u32[]{:S(2)}, u32[]{:S(2)}) collective-permute-start(f32[5,5,4,1,128]{4,2,1,0,3:T(4,128)S(1)} %maximum_bitcast_fusion.28), channel_id=1, source_target_pairs={{0,1},{1,2},{2,3},{3,4},{4,5},{5,6},{6,7},{7,8},{8,9},{9,10},{10,1... | collective-permute-start | bytes 153608 | tf_op jit(solution)/shard_map/ppermute | solution.py:28
  37.0 9.0 %collective-permute-start.3 = (f32[5,5,4,1,128]{4,2,1,0,3:T(4,128)S(1)}, f32[5,5,4,1,128]{4,2,1,0,3:T(4,128)S(1)}, u32[]{:S(2)}, u32[]{:S(2)}) collective-permute-start(f32[5,5,4,1,128]{4,2,1,0,3:T(4,128)S(1)} %get-tuple-element.43), channel_id=1, source_target_pairs={{1,0},{2,1},{3,2},{4,3},{5,4},{6,5},{7,6},{8,7},{9,8},{10,9},{11,1... | collective-permute-start | bytes 153608 | tf_op jit(solution)/shard_map/ppermute | solution.py:30
  41.2 6.6 %collective-permute-start.7 = (f32[5,5,4,1,128]{4,2,1,0,3:T(4,128)S(1)}, f32[5,5,4,1,128]{4,2,1,0,3:T(4,128)S(1)}, u32[]{:S(2)}, u32[]{:S(2)}) collective-permute-start(f32[5,5,4,1,128]{4,2,1,0,3:T(4,128)S(1)} %get-tuple-element.41), channel_id=1, source_target_pairs={{1,0},{2,1},{3,2},{4,3},{5,4},{6,5},{7,6},{8,7},{9,8},{10,9},{11,1... | collective-permute-start | bytes 153608 | tf_op jit(solution)/shard_map/ppermute | solution.py:30
  54.0 3.3 collective-permute-start.8
  55.3 20.8 %collective-permute-start.14 = (f32[2,2,4,1,128]{4,2,1,0,3:T(4,128)S(1)}, f32[2,2,4,1,128]{4,2,1,0,3:T(4,128)S(1)}, u32[]{:S(2)}, u32[]{:S(2)}) collective-permute-start(f32[2,2,4,1,128]{4,2,1,0,3:T(4,128)S(1)} %fusion.302), channel_id=1, source_target_pairs={{0,1},{1,2},{2,3},{3,4},{4,5},{5,6},{6,7},{7,8},{8,9},{9,10},{10,1... | collective-permute-start | bytes 24584 | tf_op jit(solution)/shard_map/ppermute | solution.py:28
  57.4 7.8 %collective-permute-start.9 = (f32[5,5,4,1,1]{4,0,2,1,3:T(8,128)S(1)}, f32[5,5,4,1,1]{4,0,2,1,3:T(8,128)S(1)}, u32[]{:S(2)}, u32[]{:S(2)}) collective-permute-start(f32[5,5,4,1,1]{4,0,2,1,3:T(8,128)S(1)} %get-tuple-element.93), channel_id=1, source_target_pairs={{128,0},{129,1},{130,2},{131,3},{132,4},{133,5},{134,6},{135,7},{1... | collective-permute-start | bytes 1208 | tf_op jit(solution)/shard_map/ppermute | solution.py:30
  66.4 12.7 %collective-permute-start.10 = (f32[5,5,4,1,128]{4,0,2,1,3:T(8,128)S(1)}, f32[5,5,4,1,128]{4,0,2,1,3:T(8,128)S(1)}, u32[]{:S(2)}, u32[]{:S(2)}) collective-permute-start(f32[5,5,4,1,128]{4,0,2,1,3:T(8,128)S(1)} %get-tuple-element.48), channel_id=1, source_target_pairs={{0,1},{1,2},{2,3},{3,4},{4,5},{5,6},{6,7},{7,8},{8,9},{9,10},{10,1... | collective-permute-start | bytes 153608 | tf_op jit(solution)/shard_map/ppermute | solution.py:28
  68.3 10.8 %collective-permute-start.11 = (f32[5,5,4,1,128]{4,0,2,1,3:T(8,128)S(1)}, f32[5,5,4,1,128]{4,0,2,1,3:T(8,128)S(1)}, u32[]{:S(2)}, u32[]{:S(2)}) collective-permute-start(f32[5,5,4,1,128]{4,0,2,1,3:T(8,128)S(1)} %get-tuple-element.49), channel_id=1, source_target_pairs={{1,0},{2,1},{3,2},{4,3},{5,4},{6,5},{7,6},{8,7},{9,8},{10,9},{11,1... | collective-permute-start | bytes 153608 | tf_op jit(solution)/shard_map/ppermute | solution.py:30
  76.2 11.4 %collective-permute-start.15 = (f32[2,2,4,1,128]{4,2,1,0,3:T(4,128)S(1)}, f32[2,2,4,1,128]{4,2,1,0,3:T(4,128)S(1)}, u32[]{:S(2)}, u32[]{:S(2)}) collective-permute-start(f32[2,2,4,1,128]{4,2,1,0,3:T(4,128)S(1)} %get-tuple-element.35), channel_id=1, source_target_pairs={{1,0},{2,1},{3,2},{4,3},{5,4},{6,5},{7,6},{8,7},{9,8},{10,9},{11,1... | collective-permute-start | bytes 24584 | tf_op jit(solution)/shard_map/ppermute | solution.py:30
  89.0 7.0 %collective-permute-start.17 = (f32[2,2,4,1,1]{4,0,2,1,3:T(2,128)S(1)}, f32[2,2,4,1,1]{4,0,2,1,3:T(2,128)S(1)}, u32[]{:S(2)}, u32[]{:S(2)}) collective-permute-start(f32[2,2,4,1,1]{4,0,2,1,3:T(2,128)S(1)} %get-tuple-element.237), channel_id=1, source_target_pairs={{128,0},{129,1},{130,2},{131,3},{132,4},{133,5},{134,6},{135,7},{1... | collective-permute-start | bytes 200 | tf_op jit(solution)/shard_map/ppermute | solution.py:30
  96.2 9.2 %collective-permute-start.18 = (f32[2,2,4,1,128]{4,0,2,1,3:T(2,128)S(1)}, f32[2,2,4,1,128]{4,0,2,1,3:T(2,128)S(1)}, u32[]{:S(2)}, u32[]{:S(2)}) collective-permute-start(f32[2,2,4,1,128]{4,0,2,1,3:T(2,128)S(1)} %fusion.300), channel_id=1, source_target_pairs={{0,1},{1,2},{2,3},{3,4},{4,5},{5,6},{6,7},{7,8},{8,9},{9,10},{10,1... | collective-permute-start | bytes 24584 | tf_op jit(solution)/shard_map/ppermute | solution.py:28
  105.4 3.3 collective-permute-start.19
  114.6 7.0 %collective-permute-start.21 = (f32[2,2,4,1,1]{4,2,0,1,3:T(4,128)S(1)}, f32[2,2,4,1,1]{4,2,0,1,3:T(4,128)S(1)}, u32[]{:S(2)}, u32[]{:S(2)}) collective-permute-start(f32[2,2,4,1,1]{4,2,0,1,3:T(4,128)S(1)} %get-tuple-element.225), channel_id=1, source_target_pairs={{128,0},{129,1},{130,2},{131,3},{132,4},{133,5},{134,6},{135,7},{1... | collective-permute-start | bytes 200 | tf_op jit(solution)/shard_map/ppermute | solution.py:30
  121.8 9.2 %collective-permute-start.22 = (f32[2,2,4,1,128]{4,2,1,0,3:T(4,128)S(1)}, f32[2,2,4,1,128]{4,2,1,0,3:T(4,128)S(1)}, u32[]{:S(2)}, u32[]{:S(2)}) collective-permute-start(f32[2,2,4,1,128]{4,2,1,0,3:T(4,128)S(1)} %fusion.299), channel_id=1, source_target_pairs={{0,1},{1,2},{2,3},{3,4},{4,5},{5,6},{6,7},{7,8},{8,9},{9,10},{10,1... | collective-permute-start | bytes 24584 | tf_op jit(solution)/shard_map/ppermute | solution.py:28
  131.0 3.3 collective-permute-start.23
  139.1 7.0 %collective-permute-start.25 = (f32[2,2,4,1,1]{4,2,0,1,3:T(4,128)S(1)}, f32[2,2,4,1,1]{4,2,0,1,3:T(4,128)S(1)}, u32[]{:S(2)}, u32[]{:S(2)}) collective-permute-start(f32[2,2,4,1,1]{4,2,0,1,3:T(4,128)S(1)} %get-tuple-element.219), channel_id=1, source_target_pairs={{128,0},{129,1},{130,2},{131,3},{132,4},{133,5},{134,6},{135,7},{1... | collective-permute-start | bytes 200 | tf_op jit(solution)/shard_map/ppermute | solution.py:30
  146.3 9.2 %collective-permute-start.26 = (f32[2,2,4,1,128]{4,2,1,0,3:T(4,128)S(1)}, f32[2,2,4,1,128]{4,2,1,0,3:T(4,128)S(1)}, u32[]{:S(2)}, u32[]{:S(2)}) collective-permute-start(f32[2,2,4,1,128]{4,2,1,0,3:T(4,128)S(1)} %fusion.297), channel_id=1, source_target_pairs={{0,1},{1,2},{2,3},{3,4},{4,5},{5,6},{6,7},{7,8},{8,9},{9,10},{10,1... | collective-permute-start | bytes 24584 | tf_op jit(solution)/shard_map/ppermute | solution.py:28
  155.5 3.3 collective-permute-start.27
  163.6 7.0 %collective-permute-start.29 = (f32[2,2,4,1,1]{4,2,0,1,3:T(4,128)S(1)}, f32[2,2,4,1,1]{4,2,0,1,3:T(4,128)S(1)}, u32[]{:S(2)}, u32[]{:S(2)}) collective-permute-start(f32[2,2,4,1,1]{4,2,0,1,3:T(4,128)S(1)} %get-tuple-element.213), channel_id=1, source_target_pairs={{128,0},{129,1},{130,2},{131,3},{132,4},{133,5},{134,6},{135,7},{1... | collective-permute-start | bytes 200 | tf_op jit(solution)/shard_map/ppermute | solution.py:30
  170.8 9.2 %collective-permute-start.30 = (f32[2,2,4,1,128]{4,2,1,0,3:T(4,128)S(1)}, f32[2,2,4,1,128]{4,2,1,0,3:T(4,128)S(1)}, u32[]{:S(2)}, u32[]{:S(2)}) collective-permute-start(f32[2,2,4,1,128]{4,2,1,0,3:T(4,128)S(1)} %fusion.295), channel_id=1, source_target_pairs={{0,1},{1,2},{2,3},{3,4},{4,5},{5,6},{6,7},{7,8},{8,9},{9,10},{10,1... | collective-permute-start | bytes 24584 | tf_op jit(solution)/shard_map/ppermute | solution.py:28
  180.0 3.3 collective-permute-start.31
  189.9 3.4 collective-permute-start.32
  193.3 7.5 %collective-permute-start.33 = (f32[5,5,4,1,1]{4,2,0,1,3:T(4,128)S(1)}, f32[5,5,4,1,1]{4,2,0,1,3:T(4,128)S(1)}, u32[]{:S(2)}, u32[]{:S(2)}) collective-permute-start(f32[5,5,4,1,1]{4,2,0,1,3:T(4,128)S(1)} %get-tuple-element.135), channel_id=1, source_target_pairs={{128,0},{129,1},{130,2},{131,3},{132,4},{133,5},{134,6},{135,7},{1... | collective-permute-start | bytes 1208 | tf_op jit(solution)/shard_map/ppermute | solution.py:30
  201.1 9.8 %collective-permute-start.34 = (f32[5,5,4,1,128]{4,2,1,0,3:T(4,128)S(1)}, f32[5,5,4,1,128]{4,2,1,0,3:T(4,128)S(1)}, u32[]{:S(2)}, u32[]{:S(2)}) collective-permute-start(f32[5,5,4,1,128]{4,2,1,0,3:T(4,128)S(1)} %maximum_bitcast_fusion.24), channel_id=1, source_target_pairs={{0,1},{1,2},{2,3},{3,4},{4,5},{5,6},{6,7},{7,8},{8,9},{9,10},{10,1... | collective-permute-start | bytes 153608 | tf_op jit(solution)/shard_map/ppermute | solution.py:28
  210.9 3.7 collective-permute-start.35
  223.5 7.5 %collective-permute-start.37 = (f32[5,5,4,1,1]{4,2,0,1,3:T(4,128)S(1)}, f32[5,5,4,1,1]{4,2,0,1,3:T(4,128)S(1)}, u32[]{:S(2)}, u32[]{:S(2)}) collective-permute-start(f32[5,5,4,1,1]{4,2,0,1,3:T(4,128)S(1)} %get-tuple-element.129), channel_id=1, source_target_pairs={{128,0},{129,1},{130,2},{131,3},{132,4},{133,5},{134,6},{135,7},{1... | collective-permute-start | bytes 1208 | tf_op jit(solution)/shard_map/ppermute | solution.py:30
  231.3 9.7 %collective-permute-start.38 = (f32[5,5,4,1,128]{4,2,1,0,3:T(4,128)S(1)}, f32[5,5,4,1,128]{4,2,1,0,3:T(4,128)S(1)}, u32[]{:S(2)}, u32[]{:S(2)}) collective-permute-start(f32[5,5,4,1,128]{4,2,1,0,3:T(4,128)S(1)} %maximum_bitcast_fusion.20), channel_id=1, source_target_pairs={{0,1},{1,2},{2,3},{3,4},{4,5},{5,6},{6,7},{7,8},{8,9},{9,10},{10,1... | collective-permute-start | bytes 153608 | tf_op jit(solution)/shard_map/ppermute | solution.py:28
  240.9 3.7 collective-permute-start.39
  250.3 3.4 collective-permute-start.40
  253.7 7.5 %collective-permute-start.41 = (f32[5,5,4,1,1]{4,2,0,1,3:T(4,128)S(1)}, f32[5,5,4,1,1]{4,2,0,1,3:T(4,128)S(1)}, u32[]{:S(2)}, u32[]{:S(2)}) collective-permute-start(f32[5,5,4,1,1]{4,2,0,1,3:T(4,128)S(1)} %get-tuple-element.123), channel_id=1, source_target_pairs={{128,0},{129,1},{130,2},{131,3},{132,4},{133,5},{134,6},{135,7},{1... | collective-permute-start | bytes 1208 | tf_op jit(solution)/shard_map/ppermute | solution.py:30
  261.4 9.7 %collective-permute-start.42 = (f32[5,5,4,1,128]{4,2,1,0,3:T(4,128)S(1)}, f32[5,5,4,1,128]{4,2,1,0,3:T(4,128)S(1)}, u32[]{:S(2)}, u32[]{:S(2)}) collective-permute-start(f32[5,5,4,1,128]{4,2,1,0,3:T(4,128)S(1)} %maximum_bitcast_fusion.16), channel_id=1, source_target_pairs={{0,1},{1,2},{2,3},{3,4},{4,5},{5,6},{6,7},{7,8},{8,9},{9,10},{10,1... | collective-permute-start | bytes 153608 | tf_op jit(solution)/shard_map/ppermute | solution.py:28
  271.1 3.7 collective-permute-start.43
  280.5 3.3 collective-permute-start.44
  283.8 7.5 %collective-permute-start.45 = (f32[5,5,4,1,1]{4,2,0,1,3:T(4,128)S(1)}, f32[5,5,4,1,1]{4,2,0,1,3:T(4,128)S(1)}, u32[]{:S(2)}, u32[]{:S(2)}) collective-permute-start(f32[5,5,4,1,1]{4,2,0,1,3:T(4,128)S(1)} %get-tuple-element.117), channel_id=1, source_target_pairs={{128,0},{129,1},{130,2},{131,3},{132,4},{133,5},{134,6},{135,7},{1... | collective-permute-start | bytes 1208 | tf_op jit(solution)/shard_map/ppermute | solution.py:30
  291.6 9.7 %collective-permute-start.46 = (f32[5,5,4,1,128]{4,2,1,0,3:T(4,128)S(1)}, f32[5,5,4,1,128]{4,2,1,0,3:T(4,128)S(1)}, u32[]{:S(2)}, u32[]{:S(2)}) collective-permute-start(f32[5,5,4,1,128]{4,2,1,0,3:T(4,128)S(1)} %maximum_bitcast_fusion.12), channel_id=1, source_target_pairs={{0,1},{1,2},{2,3},{3,4},{4,5},{5,6},{6,7},{7,8},{8,9},{9,10},{10,1... | collective-permute-start | bytes 153608 | tf_op jit(solution)/shard_map/ppermute | solution.py:28
  301.3 3.7 collective-permute-start.47
  314.5 7.0 %collective-permute-start.49 = (f32[2,2,4,1,1]{4,2,0,1,3:T(4,128)S(1)}, f32[2,2,4,1,1]{4,2,0,1,3:T(4,128)S(1)}, u32[]{:S(2)}, u32[]{:S(2)}) collective-permute-start(f32[2,2,4,1,1]{4,2,0,1,3:T(4,128)S(1)} %get-tuple-element.207), channel_id=1, source_target_pairs={{128,0},{129,1},{130,2},{131,3},{132,4},{133,5},{134,6},{135,7},{1... | collective-permute-start | bytes 200 | tf_op jit(solution)/shard_map/ppermute | solution.py:30
  321.7 9.2 %collective-permute-start.50 = (f32[2,2,4,1,128]{4,2,1,0,3:T(4,128)S(1)}, f32[2,2,4,1,128]{4,2,1,0,3:T(4,128)S(1)}, u32[]{:S(2)}, u32[]{:S(2)}) collective-permute-start(f32[2,2,4,1,128]{4,2,1,0,3:T(4,128)S(1)} %fusion.293), channel_id=1, source_target_pairs={{0,1},{1,2},{2,3},{3,4},{4,5},{5,6},{6,7},{7,8},{8,9},{9,10},{10,1... | collective-permute-start | bytes 24584 | tf_op jit(solution)/shard_map/ppermute | solution.py:28
  330.9 3.3 collective-permute-start.51
  339.0 7.0 %collective-permute-start.53 = (f32[2,2,4,1,1]{4,2,0,1,3:T(4,128)S(1)}, f32[2,2,4,1,1]{4,2,0,1,3:T(4,128)S(1)}, u32[]{:S(2)}, u32[]{:S(2)}) collective-permute-start(f32[2,2,4,1,1]{4,2,0,1,3:T(4,128)S(1)} %get-tuple-element.201), channel_id=1, source_target_pairs={{128,0},{129,1},{130,2},{131,3},{132,4},{133,5},{134,6},{135,7},{1... | collective-permute-start | bytes 200 | tf_op jit(solution)/shard_map/ppermute | solution.py:30
  346.2 9.2 %collective-permute-start.54 = (f32[2,2,4,1,128]{4,2,1,0,3:T(4,128)S(1)}, f32[2,2,4,1,128]{4,2,1,0,3:T(4,128)S(1)}, u32[]{:S(2)}, u32[]{:S(2)}) collective-permute-start(f32[2,2,4,1,128]{4,2,1,0,3:T(4,128)S(1)} %fusion.291), channel_id=1, source_target_pairs={{0,1},{1,2},{2,3},{3,4},{4,5},{5,6},{6,7},{7,8},{8,9},{9,10},{10,1... | collective-permute-start | bytes 24584 | tf_op jit(solution)/shard_map/ppermute | solution.py:28
  363.5 7.0 %collective-permute-start.57 = (f32[2,2,4,1,1]{4,2,0,1,3:T(4,128)S(1)}, f32[2,2,4,1,1]{4,2,0,1,3:T(4,128)S(1)}, u32[]{:S(2)}, u32[]{:S(2)}) collective-permute-start(f32[2,2,4,1,1]{4,2,0,1,3:T(4,128)S(1)} %get-tuple-element.195), channel_id=1, source_target_pairs={{128,0},{129,1},{130,2},{131,3},{132,4},{133,5},{134,6},{135,7},{1... | collective-permute-start | bytes 200 | tf_op jit(solution)/shard_map/ppermute | solution.py:30
  370.7 9.2 %collective-permute-start.58 = (f32[2,2,4,1,128]{4,2,1,0,3:T(4,128)S(1)}, f32[2,2,4,1,128]{4,2,1,0,3:T(4,128)S(1)}, u32[]{:S(2)}, u32[]{:S(2)}) collective-permute-start(f32[2,2,4,1,128]{4,2,1,0,3:T(4,128)S(1)} %fusion.289), channel_id=1, source_target_pairs={{0,1},{1,2},{2,3},{3,4},{4,5},{5,6},{6,7},{7,8},{8,9},{9,10},{10,1... | collective-permute-start | bytes 24584 | tf_op jit(solution)/shard_map/ppermute | solution.py:28
  388.0 7.0 %collective-permute-start.61 = (f32[2,2,4,1,1]{4,2,0,1,3:T(4,128)S(1)}, f32[2,2,4,1,1]{4,2,0,1,3:T(4,128)S(1)}, u32[]{:S(2)}, u32[]{:S(2)}) collective-permute-start(f32[2,2,4,1,1]{4,2,0,1,3:T(4,128)S(1)} %get-tuple-element.189), channel_id=1, source_target_pairs={{128,0},{129,1},{130,2},{131,3},{132,4},{133,5},{134,6},{135,7},{1... | collective-permute-start | bytes 200 | tf_op jit(solution)/shard_map/ppermute | solution.py:30
  395.2 9.2 %collective-permute-start.62 = (f32[2,2,4,1,128]{4,2,0,1,3:T(4,128)S(1)}, f32[2,2,4,1,128]{4,2,0,1,3:T(4,128)S(1)}, u32[]{:S(2)}, u32[]{:S(2)}) collective-permute-start(f32[2,2,4,1,128]{4,2,0,1,3:T(4,128)S(1)} %fusion.287), channel_id=1, source_target_pairs={{0,1},{1,2},{2,3},{3,4},{4,5},{5,6},{6,7},{7,8},{8,9},{9,10},{10,1... | collective-permute-start | bytes 24584 | tf_op jit(solution)/shard_map/ppermute | solution.py:28
  414.3 3.4 collective-permute-start.64
  417.7 7.5 %collective-permute-start.65 = (f32[5,5,4,1,1]{4,2,0,1,3:T(4,128)S(1)}, f32[5,5,4,1,1]{4,2,0,1,3:T(4,128)S(1)}, u32[]{:S(2)}, u32[]{:S(2)}) collective-permute-start(f32[5,5,4,1,1]{4,2,0,1,3:T(4,128)S(1)} %get-tuple-element.111), channel_id=1, source_target_pairs={{128,0},{129,1},{130,2},{131,3},{132,4},{133,5},{134,6},{135,7},{1... | collective-permute-start | bytes 1208 | tf_op jit(solution)/shard_map/ppermute | solution.py:30
  425.5 9.7 %collective-permute-start.66 = (f32[5,5,4,1,128]{4,2,0,1,3:T(4,128)S(1)}, f32[5,5,4,1,128]{4,2,0,1,3:T(4,128)S(1)}, u32[]{:S(2)}, u32[]{:S(2)}) collective-permute-start(f32[5,5,4,1,128]{4,2,0,1,3:T(4,128)S(1)} %maximum_bitcast_fusion.8), channel_id=1, source_target_pairs={{0,1},{1,2},{2,3},{3,4},{4,5},{5,6},{6,7},{7,8},{8,9},{9,10},{10,1... | collective-permute-start | bytes 153608 | tf_op jit(solution)/shard_map/ppermute | solution.py:28
  435.2 3.7 collective-permute-start.67
  444.6 3.3 collective-permute-start.68
  448.0 7.5 %collective-permute-start.69 = (f32[5,5,4,1,1]{4,2,0,1,3:T(4,128)S(1)}, f32[5,5,4,1,1]{4,2,0,1,3:T(4,128)S(1)}, u32[]{:S(2)}, u32[]{:S(2)}) collective-permute-start(f32[5,5,4,1,1]{4,2,0,1,3:T(4,128)S(1)} %get-tuple-element.105), channel_id=1, source_target_pairs={{128,0},{129,1},{130,2},{131,3},{132,4},{133,5},{134,6},{135,7},{1... | collective-permute-start | bytes 1208 | tf_op jit(solution)/shard_map/ppermute | solution.py:30
  455.7 9.7 %collective-permute-start.70 = (f32[5,5,4,1,128]{4,2,1,0,3:T(4,128)S(1)}, f32[5,5,4,1,128]{4,2,1,0,3:T(4,128)S(1)}, u32[]{:S(2)}, u32[]{:S(2)}) collective-permute-start(f32[5,5,4,1,128]{4,2,1,0,3:T(4,128)S(1)} %maximum_bitcast_fusion.6), channel_id=1, source_target_pairs={{0,1},{1,2},{2,3},{3,4},{4,5},{5,6},{6,7},{7,8},{8,9},{9,10},{10,1... | collective-permute-start | bytes 153608 | tf_op jit(solution)/shard_map/ppermute | solution.py:28
  465.4 3.7 collective-permute-start.71
  474.8 3.3 collective-permute-start.72
  478.2 7.5 %collective-permute-start.73 = (f32[5,5,4,1,1]{4,2,0,1,3:T(4,128)S(1)}, f32[5,5,4,1,1]{4,2,0,1,3:T(4,128)S(1)}, u32[]{:S(2)}, u32[]{:S(2)}) collective-permute-start(f32[5,5,4,1,1]{4,2,0,1,3:T(4,128)S(1)} %get-tuple-element.99), channel_id=1, source_target_pairs={{128,0},{129,1},{130,2},{131,3},{132,4},{133,5},{134,6},{135,7},{1... | collective-permute-start | bytes 1208 | tf_op jit(solution)/shard_map/ppermute | solution.py:30
  486.0 9.7 %collective-permute-start.74 = (f32[5,5,4,1,128]{4,2,0,1,3:T(4,128)S(1)}, f32[5,5,4,1,128]{4,2,0,1,3:T(4,128)S(1)}, u32[]{:S(2)}, u32[]{:S(2)}) collective-permute-start(f32[5,5,4,1,128]{4,2,0,1,3:T(4,128)S(1)} %maximum_bitcast_fusion.2), channel_id=1, source_target_pairs={{0,1},{1,2},{2,3},{3,4},{4,5},{5,6},{6,7},{7,8},{8,9},{9,10},{10,1... | collective-permute-start | bytes 153608 | tf_op jit(solution)/shard_map/ppermute | solution.py:28
  495.6 3.7 collective-permute-start.75
  (40 other events, 190.7 us)
where the time goes:
time: 511 us; the launch traced here: 502 us
  waiting for transfers between devices  267 us (52%)
  starting transfers between devices  144 us (28%)
  matrix products  62 us (12%)
  other arithmetic  12.6 us (2%)
  local copies, waits for them, and re-layouts  12.5 us (2%)
    ppermute x38, waiting for transfers between devices, padded_2(): lax.ppermute(tail, axis, [(i, (i + 1) % count) for i in range(ends)])  139 us
    ppermute x38, waiting for transfers between devices, padded_2(): lax.ppermute(head, axis, [((i + 1) % count, i) for i in range(ends)])  127 us
    ppermute x38, starting transfers between devices, padded_2(): lax.ppermute(head, axis, [((i + 1) % count, i) for i in range(ends)])  74 us
    ppermute x38, starting transfers between devices, padded_2(): lax.ppermute(tail, axis, [(i, (i + 1) % count) for i in range(ends)])  69.9 us
    dot_general x52, matrix products, along(): jnp.einsum('pa,a...->p...', matrix, field, precision=lax.Precision.HIGHEST)  23.3 us
    dot_general x52, matrix products, along(): jnp.einsum('qb,ab...->aq...', matrix, field, precision=lax.Precision.HIGH...  23 us
    dot_general x36, matrix products, along(): jnp.einsum('rc,abc...->abr...', matrix, field, precision=lax.Precision.HI...  15.7 us
  transfers between devices with their start and end apart: 76, of which 66 were waited for; matrix products, arithmetic and copies ran while one was open for 3% of the time, Pallas kernels for 0%

commit v1 on v0

v1 whole, which is shorter than its diff:
```python
import math

import jax
import jax.numpy as jnp
import numpy as np
from jax import lax
from jax.experimental import pallas as pl
from jax.experimental.pallas import tpu as pltpu
from jax.sharding import PartitionSpec as P

AXES = ("ex", "ey", "lin")
N = 5
NC = 4
WIN = 14
FINE_RELAX = 0.25
COARSE_RELAX = 0.4
F32 = jnp.float32

points = np.array([-1.0, -math.sqrt(3.0 / 7.0), 0.0, math.sqrt(3.0 / 7.0), 1.0])
weights = np.array([0.1, 49.0 / 90.0, 32.0 / 45.0, 49.0 / 90.0, 0.1])


def stiffness():
    eye = np.eye(N)
    spread = points[:, None] - points[None, :] + eye
    factors = np.prod(spread, axis=1)
    deriv = factors[:, None] / (factors[None, :] * spread)
    deriv = np.where(eye > 0, (np.sum(1.0 / spread, axis=1) - 1.0)[:, None], deriv)
    return deriv.T @ (weights[:, None] * deriv)


STIFF = stiffness()
LINE = STIFF / weights[:, None]
EVEN = [[float(LINE[i, j] + LINE[i, 4 - j]) / 2 for j in range(2)] for i in range(3)]
ODD = [[float(LINE[i, j] - LINE[i, 4 - j]) / 2 for j in range(2)] for i in range(2)]
INTERP = np.stack([(1.0 - points) / 2.0, (1.0 + points) / 2.0], axis=1)
SYM = [0, 1, 2, 1, 0]


def weight(*nodes):
    return float(np.prod([weights[SYM[k]] for k in sorted(SYM[n] for n in nodes)]))


def inverse_factor(a, b, c):
    s, w = np.diag(STIFF), weights
    a, b, c = sorted(SYM[n] for n in (a, b, c))
    return FINE_RELAX / float(s[a] * w[b] * w[c] + w[a] * s[b] * w[c] + w[a] * w[b] * s[c])


def at(a, b, c):
    return a * 25 + b * 5 + c


def line(u):
    m2 = u[2] + u[2]
    e0, e1 = u[0] + u[4] - m2, u[1] + u[3] - m2
    o0, o1 = u[0] - u[4], u[1] - u[3]
    even = [EVEN[i][0] * e0 + EVEN[i][1] * e1 for i in range(3)]
    odd = [ODD[i][0] * o0 + ODD[i][1] * o1 for i in range(2)]
    return [even[0] + odd[0], even[1] + odd[1], even[2], even[1] - odd[1], even[0] - odd[0]]


class Moves:
    def __init__(self, info=None):
        sub = lax.broadcasted_iota(jnp.int32, (8, 128), 0)
        lane = lax.broadcasted_iota(jnp.int32, (8, 128), 1)
        self.low = sub < 4
        self.top = (sub & 3) == 3
        self.bottom = (sub & 3) == 0
        self.lane_first = lane == 0
        self.lane_last = lane == 127
        self.last = jnp.logical_and(lane == 127, sub >= 4)
        if info is not None:
            self.even = jnp.full((8, 128), info[0], jnp.int32) == 0
            self.copy0 = jnp.full((8, 128), info[1], jnp.int32) == 0
            self.strip = info[2]

    def above(self, x):
        return jnp.where(self.top, 0.0, pltpu.roll(x, 7, 0))

    def below(self, x):
        return jnp.where(self.bottom, 0.0, pltpu.roll(x, 1, 0))

    def before(self, x):
        r = pltpu.roll(x, 1, 1)
        return jnp.where(self.lane_first, jnp.where(self.low, 0.0, pltpu.roll(r, 4, 0)), r)

    def after(self, x, end):
        r = pltpu.roll(x, 127, 1)
        return jnp.where(self.lane_last, jnp.where(self.low, pltpu.roll(r, 4, 0), end), r)

    def pick(self, x, y):
        return jnp.where(self.even, x, y)


def apply_operator(mv, u_ref, coeff, y_ref, acc_ref, up_ref):
    for b in range(N):
        for c in range(N):
            u = [u_ref[at(a, b, c)] for a in range(4)]
            u.append(mv.above(u[0]))
            up_ref[b * 5 + c] = u[4]
            for a, value in enumerate(line(u)):
                acc_ref[at(a, b, c)] = value
    for a in (4, 0, 1, 2, 3):
        scale = {}
        for b in range(3):
            for c in range(b, 3):
                scale[b, c] = scale[c, b] = coeff * weight(a, b, c)
        u = [[up_ref[b * 5 + c] if a == 4 else u_ref[at(a, b, c)] for c in range(N)] for b in range(N)]
        across = [line([u[b][c] for b in range(N)]) for c in range(N)]
        for b in range(N):
            along = line(u[b])
            y = [(acc_ref[at(a, b, c)] + along[c] + across[c][b]) * scale[SYM[b], SYM[c]] for c in range(N)]
            if a == 4:
                for c in range(N):
                    up_ref[b * 5 + c] = y[c]
                continue
            if a == 0:
                y = [y[c] + mv.below(up_ref[b * 5 + c]) for c in range(N)]
            y[0] = y[0] + mv.before(y[4])
            for c in range(N):
                y_ref[at(a, b, c)] = y[c]


def put_faces(mv, y_ref, a_ref, b_ref, first=0):
    for a in range(4):
        for c in range(N):
            low, high = y_ref[at(a, 0, c)], y_ref[at(a, 4, c)]
            a_ref[first + a * 5 + c] = mv.pick(high, low)
            b_ref[first + a * 5 + c] = mv.pick(low, high)


def got_faces(mv, a_ref, b_ref, count, strips, a_first=0, b_first=0):
    has_left = jnp.where(mv.strip > 0, 1.0, 0.0).astype(F32)
    has_right = jnp.where(mv.strip < strips - 1, 1.0, 0.0).astype(F32)
    left, right = [], []
    for k in range(count):
        x, y = a_ref[a_first + k], b_ref[b_first + k]
        left.append(mv.pick(y, x) * has_left)
        right.append(mv.pick(x, y) * has_right)
    return left, right


def inverse_at(inv_ref, a, b, c):
    kind = (0 if a == 0 else 6) + (0 if b == 0 else 4 if b == 4 else 2) + (0 if c == 0 else 1)
    return inv_ref[kind] * inverse_factor(a, b, c)


def residual_row(mv, f_ref, y_ref, left, right, a, b):
    row = []
    for c in range(N):
        r = f_ref[at(a, b, c)] - y_ref[at(a, b, c)]
        if b == 0:
            r = r - left[a * 5 + c]
        if b == 4:
            r = r - right[a * 5 + c]
        row.append(r)
    return row


def smooth(mv, u_ref, f_ref, y_ref, left, right, inv_ref, out_ref):
    for a in range(4):
        for b in range(N):
            r = residual_row(mv, f_ref, y_ref, left, right, a, b)
            u = [u_ref[at(a, b, c)] + r[c] * inverse_at(inv_ref, a, b, c) for c in range(N)]
            u[4] = mv.after(u[0], u[4])
            for c in range(N):
                out_ref[at(a, b, c)] = u[c]


def half_rows(mv, ref, out_ref):
    for n in range(0, 100, 2):
        x, y = ref[n], ref[n + 1]
        x = jnp.where(mv.copy0, x, pltpu.roll(x, 4, 0))
        y = jnp.where(mv.copy0, pltpu.roll(y, 4, 0), y)
        out_ref[pl.ds(4 * n, 8)] = jnp.where(mv.low, x, y)


def pack_kernel(load_ref, kappa_ref, wet_ref, out_ref):
    row = lax.broadcasted_iota(jnp.int32, (100, 128), 0)
    out_ref[pl.ds(0, 100)] = load_ref[pl.ds(0, 100)] + jnp.where((row & 3) == 0, 0.0, load_ref[pl.ds(399, 100)])
    out_ref[pl.ds(100, 300)] = load_ref[pl.ds(100, 300)]
    coeff = kappa_ref[...] * jnp.where(wet_ref[...] == 1, 1.0, 0.05).astype(F32)
    out_ref[pl.ds(400, 4)] = coeff
    out_ref[pl.ds(404, 4)] = coeff


def unpack_kernel(info, same_ref, other_ref, f_ref, coeff_ref, a_ref, b_ref):
    mv = Moves(info)

    def pair(n):
        x, y = same_ref[pl.ds(4 * n, 8)], other_ref[pl.ds(4 * n, 8)]
        h0, h1 = jnp.where(mv.copy0, x, y), jnp.where(mv.copy0, y, x)
        return jnp.where(mv.low, h0, pltpu.roll(h1, 4, 0)), jnp.where(mv.low, pltpu.roll(h0, 4, 0), h1)

    for n in range(0, 100, 2):
        f_ref[n], f_ref[n + 1] = pair(n)
    coeff, _ = pair(100)
    coeff_ref[...] = coeff
    for a in range(4):
        for b in range(N):
            f_ref[at(a, b, 0)] = f_ref[at(a, b, 0)] + mv.before(f_ref[at(a, b, 4)])
    put_faces(mv, f_ref, a_ref, b_ref)
    a_ref[20] = coeff
    b_ref[20] = coeff


def first_kernel(strips, info, part_ref, coeff_ref, ga_ref, gb_ref, u_ref, y_ref, f_ref, inv_ref, a_ref, b_ref, acc_ref, up_ref):
    mv = Moves(info)
    left, right = got_faces(mv, ga_ref, gb_ref, 21, strips)
    coeff = coeff_ref[...]
    for kind_b, value in enumerate((coeff + left[20], coeff, coeff + right[20])):
        for kind_a, v in enumerate((value + mv.below(value), value)):
            inv_ref[kind_a * 6 + kind_b * 2] = 1.0 / (v + mv.before(v))
            inv_ref[kind_a * 6 + kind_b * 2 + 1] = 1.0 / v
    for a in range(4):
        for b in range(N):
            f = [part_ref[at(a, b, c)] for c in range(N)]
            if b == 0:
                f = [f[c] + left[a * 5 + c] for c in range(N)]
            if b == 4:
                f = [f[c] + right[a * 5 + c] for c in range(N)]
            u = [f[c] * inverse_at(inv_ref, a, b, c) for c in range(N)]
            u[4] = mv.after(u[0], u[4])
            for c in range(N):
                f_ref[at(a, b, c)] = f[c]
                u_ref[at(a, b, c)] = u[c]
    apply_operator(mv, u_ref, coeff, y_ref, acc_ref, up_ref)
    put_faces(mv, y_ref, a_ref, b_ref)


def sweep_kernel(strips, info, u_ref, y_ref, f_ref, inv_ref, coeff_ref, ga_ref, gb_ref, un_ref, yn_ref, a_ref, b_ref, acc_ref, up_ref):
    mv = Moves(info)
    left, right = got_faces(mv, ga_ref, gb_ref, 20, strips)
    smooth(mv, u_ref, f_ref, y_ref, left, right, inv_ref, un_ref)
    apply_operator(mv, un_ref, coeff_ref[...], yn_ref, acc_ref, up_ref)
    put_faces(mv, yn_ref, a_ref, b_ref)


def last_sweep_kernel(strips, info, u_ref, y_ref, f_ref, inv_ref, coeff_ref, ga_ref, gb_ref, yn_ref, a_ref, b_ref, half_ref, un_ref, acc_ref, up_ref):
    sweep_kernel(strips, info, u_ref, y_ref, f_ref, inv_ref, coeff_ref, ga_ref, gb_ref, un_ref, yn_ref, a_ref, b_ref, acc_ref, up_ref)
    half_rows(Moves(info), un_ref, half_ref)


def restrict_kernel(strips, info, u_ref, y_ref, f_ref, inv_ref, coeff_ref, ga_ref, gb_ref, part_ref, un_ref, own_ref, a_ref, b_ref, yn_ref, acc_ref, up_ref):
    mv = Moves(info)
    left, right = got_faces(mv, ga_ref, gb_ref, 20, strips)
    smooth(mv, u_ref, f_ref, y_ref, left, right, inv_ref, un_ref)
    apply_operator(mv, un_ref, coeff_ref[...], yn_ref, acc_ref, up_ref)
    put_faces(mv, yn_ref, a_ref, b_ref, 5)
    z = [[], []]
    for c in range(N):
        rows = [[], []]
        for a in range(4):
            r = [part_ref[at(a, b, c)] - yn_ref[at(a, b, c)] for b in range(N)]
            inner = [sum(float(INTERP[b, side]) * r[b] for b in (1, 2, 3)) for side in range(2)]
            rows[0].append(r[0] + inner[0])
            rows[1].append(r[4] + inner[1])
        for side in range(2):
            x = rows[side]
            low = x[0] + sum(float(INTERP[a, 0]) * x[a] for a in (1, 2, 3))
            z[side].append(low + mv.below(sum(float(INTERP[a, 1]) * x[a] for a in (1, 2, 3))))
    for side in range(2):
        x = z[side]
        inner = [sum(float(INTERP[c, k]) * x[c] for c in (1, 2, 3)) for k in range(2)]
        own_ref[side * 2] = x[0] + inner[0] + mv.before(inner[1])
        own_ref[side * 2 + 1] = jnp.where(mv.last, x[4] + inner[1], 0.0)
    own_ref[4] = coeff_ref[...]
    for k in range(5):
        a_ref[k] = own_ref[k]


def chip_kernel(info, own_ref, ga_ref, b_ref, chip_ref, near_ref):
    mv = Moves(info)
    for k in range(5):
        x, y = own_ref[k], ga_ref[k]
        low, high = mv.pick(x, y), mv.pick(y, x)
        chip_ref[k] = low
        chip_ref[5 + k] = high
        near_ref[k] = low
        near_ref[5 + k] = high
    for k in range(20):
        near_ref[10 + k] = b_ref[5 + k]


def side_kernel(near_ref, second_ref, third_ref, out_ref):
    for k in range(10):
        out_ref[k] = near_ref[k]
        out_ref[10 + k] = second_ref[k]
        out_ref[20 + k] = third_ref[k]


def coarse_solve(mv, strips, chip_ref, mine_ref, other_ref):
    base = mv.strip - (mv.strip & 1) - 6
    window = []
    for w in range(WIN):
        rows = []
        ok = jnp.where(jnp.logical_and(base + w >= 0, base + w < strips), 1.0, 0.0).astype(F32)
        for k in range(5):
            if w in (6, 7):
                rows.append(chip_ref[(w - 6) * 5 + k])
                continue
            if w < 6:
                slot = (2 - w // 2) * 10 + (w % 2) * 5 + k
                x = mv.pick(mine_ref[slot], other_ref[slot])
            else:
                slot = (w // 2 - 4) * 10 + (w % 2) * 5 + k
                x = mv.pick(other_ref[slot], mine_ref[slot])
            rows.append(x * ok)
        window.append(rows)
    coeffs = [rows[4] for rows in window]
    load, inverse, value = {}, {}, {}
    factor = COARSE_RELAX / (2.0 / 3.0)
    for j in range(2, 13):
        load[j] = [window[j - 1][2 + g] + window[j][g] for g in range(2)]
        k = coeffs[j - 1] + coeffs[j]
        k = k + mv.below(k)
        inverse[j] = [jnp.where(v > 0.0, factor / v, 0.0) for v in (k + mv.before(k), k)]
        value[j] = [inverse[j][g] * load[j][g] for g in range(2)]
    for step in range(NC - 1):
        first, final = 2 + step, 12 - step
        nodes = {}
        for j in range(first, final + 1):
            value[j][1] = mv.after(value[j][0], value[j][1])
            nodes[j] = [value[j], [mv.above(v) for v in value[j]]]
        sums = {j: [[None, None], [None, None]] for j in range(first, final + 1)}
        for j in range(first, final):
            v = {(a, b, c): nodes[j + b][a][c] for a in range(2) for b in range(2) for c in range(2)}
            for axis in range(3):
                v = butterfly(v, axis)
            cf = [coeffs[j] * 0.125, coeffs[j] * (0.125 * 2.0 / 3.0), coeffs[j] * (0.125 / 3.0)]
            v = {key: None if sum(key) == 0 else x * cf[sum(key) - 1] for key, x in v.items()}
            for axis in range(3):
                v = butterfly(v, axis)
            for (a, b, c), x in v.items():
                old = sums[j + b][a][c]
                sums[j + b][a][c] = x if old is None else old + x
        new = {}
        for j in range(first + 1, final):
            s = sums[j]
            row = [s[0][c] + mv.below(s[1][c]) for c in range(2)]
            row[0] = row[0] + mv.before(row[1])
            new[j] = [value[j][g] + inverse[j][g] * (load[j][g] - row[g]) for g in range(2)]
        value = new
    for j in value:
        value[j][1] = mv.after(value[j][0], value[j][1])
    lines = [[mv.pick(value[5 + m][g], value[6 + m][g]) for g in range(2)] for m in range(4)]
    return lines, mv.pick(coeffs[5], coeffs[6]), mv.pick(coeffs[7], coeffs[8])


def butterfly(v, axis):
    out = {}
    for key in v:
        if key[axis]:
            continue
        up = tuple(1 if k == axis else key[k] for k in range(3))
        x, y = v[key], v[up]
        out[key] = y if x is None else x + y
        out[up] = -y if x is None else x - y
    return out


def nodal(mv, pair, count):
    rows = []
    up = [mv.above(v) for v in pair]
    for a in range(count):
        lo, hi = float(INTERP[a, 0]), float(INTERP[a, 1])
        if a == 0:
            ends = pair
        elif a == 4:
            ends = up
        else:
            ends = [lo * pair[g] + hi * up[g] for g in range(2)]
        rows.append([ends[0] if c == 0 else ends[1] if c == 4 else float(INTERP[c, 0]) * ends[0] + float(INTERP[c, 1]) * ends[1] for c in range(N)])
    return rows


def neighbour_face(mv, near, far, coeff):
    w = [float(x) for x in weights]
    x = nodal(mv, near, N)
    z = nodal(mv, far, N)
    y = []
    for a in range(N):
        row = []
        for c in range(N):
            v = (x[a][c] - z[a][c]) * (0.5 * weight(a, c))
            if a in (0, 4):
                v = v + (x[a][c] - x[4 - a][c]) * (0.5 * w[0] * w[SYM[c]])
            if c in (0, 4):
                v = v + (x[a][c] - x[a][4 - c]) * (0.5 * w[0] * w[SYM[a]])
            row.append(v * coeff)
        y.append(row)
    out = []
    for a in range(4):
        row = [y[0][c] + mv.below(y[4][c]) for c in range(N)] if a == 0 else y[a]
        row[0] = row[0] + mv.before(row[4])
        out.extend(row)
    return out


def correct_kernel(strips, info, u_ref, f_ref, inv_ref, coeff_ref, ga_ref, near_ref, chip_ref, mine_ref, other_ref, un_ref, yn_ref, a_ref, b_ref, ua_ref, ya_ref, face_ref, acc_ref, up_ref):
    mv = Moves(info)
    coeff = coeff_ref[...]
    lines, coeff_left, coeff_right = coarse_solve(mv, strips, chip_ref, mine_ref, other_ref)
    for k, v in enumerate(neighbour_face(mv, lines[1], lines[0], coeff_left)):
        face_ref[k] = v
    for k, v in enumerate(neighbour_face(mv, lines[2], lines[3], coeff_right)):
        face_ref[20 + k] = v
    low, high = nodal(mv, lines[1], 4), nodal(mv, lines[2], 4)
    for a in range(4):
        for b in range(N):
            for c in range(N):
                if b == 0:
                    v = low[a][c]
                elif b == 4:
                    v = high[a][c]
                else:
                    v = float(INTERP[b, 0]) * low[a][c] + float(INTERP[b, 1]) * high[a][c]
                ua_ref[at(a, b, c)] = u_ref[at(a, b, c)] + v
    apply_operator(mv, ua_ref, coeff, ya_ref, acc_ref, up_ref)
    left, right = got_faces(mv, ga_ref, near_ref, 20, strips, 5, 10)
    left = [left[k] + face_ref[k] for k in range(20)]
    right = [right[k] + face_ref[20 + k] for k in range(20)]
    smooth(mv, ua_ref, f_ref, ya_ref, left, right, inv_ref, un_ref)
    apply_operator(mv, un_ref, coeff, yn_ref, acc_ref, up_ref)
    put_faces(mv, yn_ref, a_ref, b_ref)


def residual_kernel(strips, info, y_ref, f_ref, ga_ref, gb_ref, half_ref, r_ref):
    mv = Moves(info)
    left, right = got_faces(mv, ga_ref, gb_ref, 20, strips)
    for a in range(4):
        for b in range(N):
            r = residual_row(mv, f_ref, y_ref, left, right, a, b)
            r[4] = mv.after(r[0], r[4])
            for c in range(N):
                r_ref[at(a, b, c)] = r[c]
    half_rows(mv, r_ref, half_ref)


def spread_kernel(half_ref, out_ref):
    out_ref[pl.ds(0, 400)] = half_ref[...]
    row = lax.broadcasted_iota(jnp.int32, (100, 128), 0)
    out_ref[pl.ds(400, 100)] = jnp.where((row & 3) == 3, 0.0, half_ref[pl.ds(1, 100)])


VM = pl.BlockSpec(memory_space=pltpu.VMEM)
SM = pl.BlockSpec(memory_space=pltpu.SMEM)
FIELD = (100, 8, 128)
WORK = [(125, 8, 128), (25, 8, 128)]


def call(name, kernel, outs, scratch, info, *args):
    specs = [VM] * len(args)
    operands = args
    if info is not None:
        specs, operands = [SM] + specs, (info, *args)
    return pl.pallas_call(
        kernel,
        out_shape=[jax.ShapeDtypeStruct(s, F32) for s in outs],
        in_specs=specs,
        out_specs=[VM] * len(outs),
        scratch_shapes=[pltpu.VMEM(s, F32) for s in scratch],
        compiler_params=pltpu.CompilerParams(vmem_limit_bytes=12 * 1024 * 1024),
        name=name,
    )(*operands)


def placement(sizes):
    _, ey, lin = sizes
    if (ey, lin) != (2, 64):
        return list(range(ey * lin))
    order = []
    for q in range(64):
        side, p, y = q // 32, (q % 32) // 4, q % 4
        z = p if side == 0 else 7 - p
        order.append(side * 64 + z * 8 + (y if p % 2 == 0 else 3 - y) * 2)
    return [order[s // 2] + s % 2 for s in range(128)]


def per_device(sizes):
    strips = sizes[1] * sizes[2]
    chips = strips // 2
    place = placement(sizes)
    device = [[copy * strips + place[s] for s in range(strips)] for copy in range(2)]
    to_same = [(e * strips + s, device[e][s]) for e in range(2) for s in range(strips)]
    to_other = [(e * strips + s, device[1 - e][s]) for e in range(2) for s in range(strips)]
    back = [(b, a) for a, b in to_same]
    within = [(device[e][s], device[e][s ^ 1]) for e in range(2) for s in range(strips)]

    def chip_pairs(d):
        pairs = []
        for e in range(2):
            for s in range(strips):
                k = (s // 2 - d) % chips if s % 2 == 0 else (s // 2 + d) % chips
                pairs.append((device[e][s], device[e][2 * k + 1 - s % 2]))
        return pairs

    beyond = {d: chip_pairs(d) for d in (1, 2, 3)}
    table = np.zeros((2 * strips, 4), np.int32)
    for copy in range(2):
        for s in range(strips):
            table[device[copy][s], :3] = (s % 2, copy, s)

    def swap(x, pairs):
        return lax.ppermute(x, AXES, pairs)

    def run(load, kappa, wet):
        info = lax.dynamic_index_in_dim(jnp.asarray(table), lax.axis_index(AXES), 0, keepdims=False)
        (packed,) = call("pack", pack_kernel, [(408, 128)], [], None, load.reshape(500, 128), kappa.reshape(4, 128), wet.reshape(4, 128))
        same, other = swap(packed, to_same), swap(packed, to_other)
        part, coeff, a, b = call("unpack", unpack_kernel, [FIELD, (8, 128), (21, 8, 128), (21, 8, 128)], [], info, same, other)
        faces = [(20, 8, 128), (20, 8, 128)]

        def bound(kernel):
            def body(*refs):
                kernel(strips, *refs)
            return body

        def trade(a, b):
            return swap(a, within), swap(b, beyond[1])

        a, b = trade(a, b)
        u, y, f, inv, a, b = call("first", bound(first_kernel), [FIELD, FIELD, FIELD, (12, 8, 128), *faces], WORK, info, part, coeff, a, b)

        def sweep(u, y, a, b):
            a, b = trade(a, b)
            return call("sweep", bound(sweep_kernel), [FIELD, FIELD, *faces], WORK, info, u, y, f, inv, coeff, a, b)

        def sweep_and_correct(u, y, a, b):
            a, b = trade(a, b)
            u, own, a, b = call("restrict", bound(restrict_kernel), [FIELD, (5, 8, 128), (25, 8, 128), (25, 8, 128)], [FIELD, *WORK], info, u, y, f, inv, coeff, a, b, part)
            a = swap(a, within)
            chip, near = call("chip", chip_kernel, [(10, 8, 128), (30, 8, 128)], [], info, own, a, b)
            near, second, third = swap(near, beyond[1]), swap(chip, beyond[2]), swap(chip, beyond[3])
            (mine,) = call("side", side_kernel, [(30, 8, 128)], [], None, near, second, third)
            theirs = swap(mine, within)
            return call("correct", bound(correct_kernel), [FIELD, FIELD, *faces], [FIELD, FIELD, (40, 8, 128), *WORK], info, u, f, inv, coeff, a, near, chip, mine, theirs)

        u, y, a, b = sweep_and_correct(u, y, a, b)
        u, y, a, b = sweep(u, y, a, b)
        u, y, a, b = sweep(u, y, a, b)
        u, y, a, b = sweep_and_correct(u, y, a, b)
        a, b = trade(a, b)
        y, a, b, half = call("last", bound(last_sweep_kernel), [FIELD, *faces, (400, 128)], [FIELD, *WORK], info, u, y, f, inv, coeff, a, b)
        a, b = trade(a, b)
        half = swap(half, back)
        (left_half,) = call("residual", bound(residual_kernel), [(400, 128)], [FIELD], info, y, f, a, b)
        (solved,) = call("spread", spread_kernel, [(500, 128)], [], None, half)
        (rest,) = call("spread", spread_kernel, [(500, 128)], [], None, swap(left_half, back))
        return solved.reshape(load.shape), rest.reshape(load.shape)

    return run


def solution(mesh):
    sizes = tuple(mesh.shape[name] for name in AXES)
    whole = P(None, None, None, None, ("ey", "lin"), "ex")
    flat = P(None, ("ey", "lin"), "ex")
    return jax.shard_map(per_device(sizes), mesh=mesh, in_specs=(whole, flat, flat), out_specs=(whole, whole), check_vma=False)
```

time: 511 us -> 122 us (0.24)
  the two profiles are of different devices: /device:TPU:2 before, /device:TPU:98 now
where the time goes in v1:
time: 122 us
  waiting for transfers between devices  65.7 us (54%)
  starting transfers between devices  38 us (31%)
  Pallas kernels  13.2 us (11%)
  local copies, waits for them, and re-layouts  4.07 us (3%)
    ppermute x28, waiting for transfers between devices, swap(): return lax.ppermute(x, AXES, pairs)  65.7 us
    ppermute x28, starting transfers between devices, swap(): return lax.ppermute(x, AXES, pairs)  38 us
    pallas_call x17, Pallas kernels, call(): pl.pallas_call(kernel, out_shape=[jax.ShapeDtypeStruct(s, F32) for s in o...  13.2 us
  transfers between devices with their start and end apart: 28, of which 20 were waited for; matrix products, arithmetic and copies ran while one was open for 1% of the time, Pallas kernels for 1%

profile of v1, /device:TPU:98, one launch (start us, length us, event | category | flops | bytes accessed | tf_op | source)
XLA Modules:
  0.0 121.8 jit_solution(3171761366485780016)
XLA Ops:
  0.6 1.1 pad
  1.8 0.7 copy-done.1
  2.5 7.2 %collective-permute-start.1 = (f32[408,128]{1,0:T(8,128)S(1)}, f32[408,128]{1,0:T(8,128)S(1)}, u32[]{:S(2)}, u32[]{:S(2)}) collective-permute-start(f32[408,128]{1,0:T(8,128)S(1)} %pack.1), channel_id=1, source_target_pairs={{0,128},{1,129},{2,130},{3,131},{4,132},{5,133},{6,134},{7,135},{8... | collective-permute-start | bytes 626696 | tf_op jit(solution)/shard_map/ppermute | solution.py:506
  9.7 2.0 %collective-permute-start = (f32[408,128]{1,0:T(8,128)S(1)}, f32[408,128]{1,0:T(8,128)S(1)}, u32[]{:S(2)}, u32[]{:S(2)}) collective-permute-start(f32[408,128]{1,0:T(8,128)S(1)} %pack.1), channel_id=1, source_target_pairs={{0,0},{1,1},{2,2},{3,3},{4,4},{5,5},{6,6},{7,7},{8,14},{9,15},{10,... | collective-permute-start | bytes 626696 | tf_op jit(solution)/shard_map/ppermute | solution.py:506
  11.7 0.7 dynamic-slice_bitcast_fusion.info.refs_0_
  12.4 10.8 %collective-permute-done.1.other_ref = f32[408,128]{1,0:T(8,128)S(1)} collective-permute-done((f32[408,128]{1,0:T(8,128)S(1)}, f32[408,128]{1,0:T(8,128)S(1)}, u32[]{:S(2)}, u32[]{:S(2)}) %collective-permute-start.1) | collective-permute-done | bytes 208928 | tf_op jit(solution)/shard_map/ppermute | solution.py:506
  23.2 4.1 %collective-permute-done.same_ref = f32[408,128]{1,0:T(8,128)S(1)} collective-permute-done((f32[408,128]{1,0:T(8,128)S(1)}, f32[408,128]{1,0:T(8,128)S(1)}, u32[]{:S(2)}, u32[]{:S(2)}) %collective-permute-start) | collective-permute-done | bytes 208928 | tf_op jit(solution)/shard_map/ppermute | solution.py:506
  27.3 0.6 unpack.1
  27.9 0.1 collective-permute-start.2
  28.0 4.6 %collective-permute-start.3 = (f32[21,8,128]{2,1,0:T(8,128)S(1)}, f32[21,8,128]{2,1,0:T(8,128)S(1)}, u32[]{:S(2)}, u32[]{:S(2)}) collective-permute-start(f32[21,8,128]{2,1,0:T(8,128)S(1)} %get-tuple-element.47), channel_id=1, source_target_pairs={{0,65},{1,2},{2,1},{3,4},{4,3},{5,6},{6,5},{7,14},{14,7},{15,12},{... | collective-permute-start | bytes 258056 | tf_op jit(solution)/shard_map/ppermute | solution.py:506
  32.6 2.2 %collective-permute-done.3.refs_4_ = f32[21,8,128]{2,1,0:T(8,128)S(1)} collective-permute-done((f32[21,8,128]{2,1,0:T(8,128)S(1)}, f32[21,8,128]{2,1,0:T(8,128)S(1)}, u32[]{:S(2)}, u32[]{:S(2)}) %collective-permute-start.3) | collective-permute-done | bytes 86048 | tf_op jit(solution)/shard_map/ppermute | solution.py:506
  34.8 1.1 first.1
  35.9 0.1 collective-permute-start.4
  36.0 3.0 %collective-permute-start.5 = (f32[20,8,128]{2,1,0:T(8,128)S(1)}, f32[20,8,128]{2,1,0:T(8,128)S(1)}, u32[]{:S(2)}, u32[]{:S(2)}) collective-permute-start(f32[20,8,128]{2,1,0:T(8,128)S(1)} %get-tuple-element.53), channel_id=1, source_target_pairs={{0,65},{1,2},{2,1},{3,4},{4,3},{5,6},{6,5},{7,14},{14,7},{15,12},{... | collective-permute-start | bytes 245768 | tf_op jit(solution)/shard_map/ppermute | solution.py:506
  39.0 2.1 %collective-permute-done.5.refs_7_ = f32[20,8,128]{2,1,0:T(8,128)S(1)} collective-permute-done((f32[20,8,128]{2,1,0:T(8,128)S(1)}, f32[20,8,128]{2,1,0:T(8,128)S(1)}, u32[]{:S(2)}, u32[]{:S(2)}) %collective-permute-start.5) | collective-permute-done | bytes 81952 | tf_op jit(solution)/shard_map/ppermute | solution.py:506
  41.1 1.1 restrict.2
  42.2 0.1 collective-permute-start.6
  42.3 1.3 %collective-permute-done.6.ga_ref.refs_5_ = f32[25,8,128]{2,1,0:T(8,128)S(1)} collective-permute-done((f32[25,8,128]{2,1,0:T(8,128)S(1)}, f32[25,8,128]{2,1,0:T(8,128)S(1)}, u32[]{:S(2)}, u32[]{:S(2)}) %collective-permute-start.6) | collective-permute-done | bytes 102432 | tf_op jit(solution)/shard_map/ppermute | solution.py:506
  43.6 0.6 chip.2
  44.2 3.0 %collective-permute-start.7 = (f32[30,8,128]{2,1,0:T(8,128)S(1)}, f32[30,8,128]{2,1,0:T(8,128)S(1)}, u32[]{:S(2)}, u32[]{:S(2)}) collective-permute-start(f32[30,8,128]{2,1,0:T(8,128)S(1)} %get-tuple-element.58), channel_id=1, source_target_pairs={{0,65},{1,2},{2,1},{3,4},{4,3},{5,6},{6,5},{7,14},{14,7},{15,12},{... | collective-permute-start | bytes 368648 | tf_op jit(solution)/shard_map/ppermute | solution.py:506
  47.2 0.3 collective-permute-start.9
  47.6 0.9 collective-permute-start.8
  48.4 5.8 %collective-permute-done.9.third_ref = f32[10,8,128]{2,1,0:T(8,128)S(1)} collective-permute-done((f32[10,8,128]{2,1,0:T(8,128)S(1)}, f32[10,8,128]{2,1,0:T(8,128)S(1)}, u32[]{:S(2)}, u32[]{:S(2)}) %collective-permute-start.9) | collective-permute-done | bytes 40992 | tf_op jit(solution)/shard_map/ppermute | solution.py:506
  54.3 0.1 collective-permute-start.10
  54.4 1.3 %collective-permute-done.10.refs_9_ = f32[30,8,128]{2,1,0:T(8,128)S(1)} collective-permute-done((f32[30,8,128]{2,1,0:T(8,128)S(1)}, f32[30,8,128]{2,1,0:T(8,128)S(1)}, u32[]{:S(2)}, u32[]{:S(2)}) %collective-permute-start.10) | collective-permute-done | bytes 122912 | tf_op jit(solution)/shard_map/ppermute | solution.py:506
  55.7 2.2 %correct.2 = (f32[100,8,128]{2,1,0:T(8,128)S(1)}, f32[100,8,128]{2,1,0:T(8,128)S(1)}, f32[20,8,128]{2,1,0:T(8,128)S(1)}, f32[20,8,128]{2,1,0:T(8,128)S(1)}) custom-call(s32[4]{0:T(128)S(1)} %dynamic-slice_bitcast_fusion.info.refs_0_, f32[100,8,128]{2,1,0:T(8,128)S(1)} %get-tuple-element.54.refs_1_, f32[100,8,128]{2,1,0:T(8,128)S(1)} %get-tuple-element.50.refs_3_.refs_2_, ...), custom_call_target="tpu_custom_call" | custom-call | tf_op jit(solution)/shard_map/correct/pallas_call | solution.py:458
  57.9 0.2 collective-permute-start.11
  58.1 1.0 collective-permute-start.12
  59.1 0.2 collective-permute-done.11.refs_6_
  59.3 3.9 %collective-permute-done.12.refs_7_ = f32[20,8,128]{2,1,0:T(8,128)S(1)} collective-permute-done((f32[20,8,128]{2,1,0:T(8,128)S(1)}, f32[20,8,128]{2,1,0:T(8,128)S(1)}, u32[]{:S(2)}, u32[]{:S(2)}) %collective-permute-start.12) | collective-permute-done | bytes 81952 | tf_op jit(solution)/shard_map/ppermute | solution.py:506
  63.2 1.0 sweep.2
  64.2 0.1 collective-permute-start.13
  64.3 1.1 collective-permute-start.14
  65.4 0.2 collective-permute-done.13.refs_6_
  65.6 3.9 %collective-permute-done.14.refs_7_ = f32[20,8,128]{2,1,0:T(8,128)S(1)} collective-permute-done((f32[20,8,128]{2,1,0:T(8,128)S(1)}, f32[20,8,128]{2,1,0:T(8,128)S(1)}, u32[]{:S(2)}, u32[]{:S(2)}) %collective-permute-start.14) | collective-permute-done | bytes 81952 | tf_op jit(solution)/shard_map/ppermute | solution.py:506
  69.5 1.0 sweep.3
  70.5 0.3 collective-permute-start.15
  70.8 1.1 collective-permute-start.16
  71.9 0.2 collective-permute-done.15.refs_6_
  72.1 3.9 %collective-permute-done.16.refs_7_ = f32[20,8,128]{2,1,0:T(8,128)S(1)} collective-permute-done((f32[20,8,128]{2,1,0:T(8,128)S(1)}, f32[20,8,128]{2,1,0:T(8,128)S(1)}, u32[]{:S(2)}, u32[]{:S(2)}) %collective-permute-start.16) | collective-permute-done | bytes 81952 | tf_op jit(solution)/shard_map/ppermute | solution.py:506
  76.0 1.1 restrict.3
  77.1 0.1 collective-permute-start.17
  77.2 1.3 %collective-permute-done.17.ga_ref.refs_5_ = f32[25,8,128]{2,1,0:T(8,128)S(1)} collective-permute-done((f32[25,8,128]{2,1,0:T(8,128)S(1)}, f32[25,8,128]{2,1,0:T(8,128)S(1)}, u32[]{:S(2)}, u32[]{:S(2)}) %collective-permute-start.17) | collective-permute-done | bytes 102432 | tf_op jit(solution)/shard_map/ppermute | solution.py:506
  78.5 0.6 chip.3
  79.0 1.1 collective-permute-start.18
  80.1 0.3 collective-permute-start.20
  80.4 2.9 %collective-permute-start.19 = (f32[10,8,128]{2,1,0:T(8,128)S(1)}, f32[10,8,128]{2,1,0:T(8,128)S(1)}, u32[]{:S(2)}, u32[]{:S(2)}) collective-permute-start(f32[10,8,128]{2,1,0:T(8,128)S(1)} %get-tuple-element.77.refs_7_), channel_id=1, source_target_pairs={{0,67},{1,4},{2,65},{3,6},{4,1},{5,14},{6,3},{7,12},{14,5},{15,10}... | collective-permute-start | bytes 122888 | tf_op jit(solution)/shard_map/ppermute | solution.py:506
  83.3 3.9 %collective-permute-done.20.third_ref = f32[10,8,128]{2,1,0:T(8,128)S(1)} collective-permute-done((f32[10,8,128]{2,1,0:T(8,128)S(1)}, f32[10,8,128]{2,1,0:T(8,128)S(1)}, u32[]{:S(2)}, u32[]{:S(2)}) %collective-permute-start.20) | collective-permute-done | bytes 40992 | tf_op jit(solution)/shard_map/ppermute | solution.py:506
  87.3 0.1 collective-permute-start.21
  87.4 1.3 %collective-permute-done.21.refs_9_ = f32[30,8,128]{2,1,0:T(8,128)S(1)} collective-permute-done((f32[30,8,128]{2,1,0:T(8,128)S(1)}, f32[30,8,128]{2,1,0:T(8,128)S(1)}, u32[]{:S(2)}, u32[]{:S(2)}) %collective-permute-start.21) | collective-permute-done | bytes 122912 | tf_op jit(solution)/shard_map/ppermute | solution.py:506
  88.7 2.2 %correct.3 = (f32[100,8,128]{2,1,0:T(8,128)S(1)}, f32[100,8,128]{2,1,0:T(8,128)S(1)}, f32[20,8,128]{2,1,0:T(8,128)S(1)}, f32[20,8,128]{2,1,0:T(8,128)S(1)}) custom-call(s32[4]{0:T(128)S(1)} %dynamic-slice_bitcast_fusion.info.refs_0_, f32[100,8,128]{2,1,0:T(8,128)S(1)} %get-tuple-element.72.refs_1_, f32[100,8,128]{2,1,0:T(8,128)S(1)} %get-tuple-element.50.refs_3_.refs_2_, ...), custom_call_target="tpu_custom_call" | custom-call | tf_op jit(solution)/shard_map/correct/pallas_call | solution.py:458
  90.9 0.2 collective-permute-start.22
  91.1 1.9 %collective-permute-start.23 = (f32[20,8,128]{2,1,0:T(8,128)S(1)}, f32[20,8,128]{2,1,0:T(8,128)S(1)}, u32[]{:S(2)}, u32[]{:S(2)}) collective-permute-start(f32[20,8,128]{2,1,0:T(8,128)S(1)} %get-tuple-element.81), channel_id=1, source_target_pairs={{0,65},{1,2},{2,1},{3,4},{4,3},{5,6},{6,5},{7,14},{14,7},{15,12},{... | collective-permute-start | bytes 245768 | tf_op jit(solution)/shard_map/ppermute | solution.py:506
  93.0 3.2 %collective-permute-done.23.refs_7_ = f32[20,8,128]{2,1,0:T(8,128)S(1)} collective-permute-done((f32[20,8,128]{2,1,0:T(8,128)S(1)}, f32[20,8,128]{2,1,0:T(8,128)S(1)}, u32[]{:S(2)}, u32[]{:S(2)}) %collective-permute-start.23) | collective-permute-done | bytes 81952 | tf_op jit(solution)/shard_map/ppermute | solution.py:506
  96.2 1.0 last.1
  97.3 2.0 %collective-permute-start.26 = (f32[20,8,128]{2,1,0:T(8,128)S(1)}, f32[20,8,128]{2,1,0:T(8,128)S(1)}, u32[]{:S(2)}, u32[]{:S(2)}) collective-permute-start(f32[20,8,128]{2,1,0:T(8,128)S(1)} %get-tuple-element.85), channel_id=1, source_target_pairs={{0,65},{1,2},{2,1},{3,4},{4,3},{5,6},{6,5},{7,14},{14,7},{15,12},{... | collective-permute-start | bytes 245768 | tf_op jit(solution)/shard_map/ppermute | solution.py:506
  99.3 2.2 %collective-permute-start.24 = (f32[400,128]{1,0:T(8,128)S(1)}, f32[400,128]{1,0:T(8,128)S(1)}, u32[]{:S(2)}, u32[]{:S(2)}) collective-permute-start(f32[400,128]{1,0:T(8,128)S(1)} %get-tuple-element.82), channel_id=1, source_target_pairs={{0,0},{1,1},{2,2},{3,3},{4,4},{5,5},{6,6},{7,7},{14,8},{15,9},{12,... | collective-permute-start | bytes 614408 | tf_op jit(solution)/shard_map/ppermute | solution.py:506
  101.5 4.7 %collective-permute-done.26.refs_4_ = f32[20,8,128]{2,1,0:T(8,128)S(1)} collective-permute-done((f32[20,8,128]{2,1,0:T(8,128)S(1)}, f32[20,8,128]{2,1,0:T(8,128)S(1)}, u32[]{:S(2)}, u32[]{:S(2)}) %collective-permute-start.26) | collective-permute-done | bytes 81952 | tf_op jit(solution)/shard_map/ppermute | solution.py:506
  106.2 0.7 residual.1
  106.8 1.9 %collective-permute-start.27 = (f32[400,128]{1,0:T(8,128)S(1)}, f32[400,128]{1,0:T(8,128)S(1)}, u32[]{:S(2)}, u32[]{:S(2)}) collective-permute-start(f32[400,128]{1,0:T(8,128)S(1)} %residual.1), channel_id=1, source_target_pairs={{0,0},{1,1},{2,2},{3,3},{4,4},{5,5},{6,6},{7,7},{14,8},{15,9},{12,... | collective-permute-start | bytes 614408 | tf_op jit(solution)/shard_map/ppermute | solution.py:506
  108.8 8.6 %collective-permute-done.24.half_ref = f32[400,128]{1,0:T(8,128)S(1)} collective-permute-done((f32[400,128]{1,0:T(8,128)S(1)}, f32[400,128]{1,0:T(8,128)S(1)}, u32[]{:S(2)}, u32[]{:S(2)}) %collective-permute-start.24) | collective-permute-done | bytes 204832 | tf_op jit(solution)/shard_map/ppermute | solution.py:506
  117.4 0.8 reshape.22
  118.1 2.9 %collective-permute-done.27.half_ref = f32[400,128]{1,0:T(8,128)S(1)} collective-permute-done((f32[400,128]{1,0:T(8,128)S(1)}, f32[400,128]{1,0:T(8,128)S(1)}, u32[]{:S(2)}, u32[]{:S(2)}) %collective-permute-start.27) | collective-permute-done | bytes 204832 | tf_op jit(solution)/shard_map/ppermute | solution.py:506
  121.0 0.8 reshape.23
  (18 shorter events, 0.2 us)
Async XLA Ops:
  1.8 0.7 copy-start.1
  1.8 0.7 copy-start
  2.5 20.7 %collective-permute-start.1 = (f32[408,128]{1,0:T(8,128)S(1)}, f32[408,128]{1,0:T(8,128)S(1)}, u32[]{:S(2)}, u32[]{:S(2)}) collective-permute-start(f32[408,128]{1,0:T(8,128)S(1)} %pack.1), channel_id=1, source_target_pairs={{0,128},{1,129},{2,130},{3,131},{4,132},{5,133},{6,134},{7,135},{8... | collective-permute-start | bytes 626696 | tf_op jit(solution)/shard_map/ppermute | solution.py:506
  9.7 17.5 %collective-permute-start = (f32[408,128]{1,0:T(8,128)S(1)}, f32[408,128]{1,0:T(8,128)S(1)}, u32[]{:S(2)}, u32[]{:S(2)}) collective-permute-start(f32[408,128]{1,0:T(8,128)S(1)} %pack.1), channel_id=1, source_target_pairs={{0,0},{1,1},{2,2},{3,3},{4,4},{5,5},{6,6},{7,7},{8,14},{9,15},{10,... | collective-permute-start | bytes 626696 | tf_op jit(solution)/shard_map/ppermute | solution.py:506
  27.9 4.7 %collective-permute-start.2 = (f32[21,8,128]{2,1,0:T(8,128)S(1)}, f32[21,8,128]{2,1,0:T(8,128)S(1)}, u32[]{:S(2)}, u32[]{:S(2)}) collective-permute-start(f32[21,8,128]{2,1,0:T(8,128)S(1)} %get-tuple-element.46), channel_id=1, source_target_pairs={{0,1},{1,0},{2,3},{3,2},{4,5},{5,4},{6,7},{7,6},{14,15},{15,14},{1... | collective-permute-start | bytes 258056 | tf_op jit(solution)/shard_map/ppermute | solution.py:506
  28.0 6.8 %collective-permute-start.3 = (f32[21,8,128]{2,1,0:T(8,128)S(1)}, f32[21,8,128]{2,1,0:T(8,128)S(1)}, u32[]{:S(2)}, u32[]{:S(2)}) collective-permute-start(f32[21,8,128]{2,1,0:T(8,128)S(1)} %get-tuple-element.47), channel_id=1, source_target_pairs={{0,65},{1,2},{2,1},{3,4},{4,3},{5,6},{6,5},{7,14},{14,7},{15,12},{... | collective-permute-start | bytes 258056 | tf_op jit(solution)/shard_map/ppermute | solution.py:506
  35.9 3.1 %collective-permute-start.4 = (f32[20,8,128]{2,1,0:T(8,128)S(1)}, f32[20,8,128]{2,1,0:T(8,128)S(1)}, u32[]{:S(2)}, u32[]{:S(2)}) collective-permute-start(f32[20,8,128]{2,1,0:T(8,128)S(1)} %get-tuple-element.52), channel_id=1, source_target_pairs={{0,1},{1,0},{2,3},{3,2},{4,5},{5,4},{6,7},{7,6},{14,15},{15,14},{1... | collective-permute-start | bytes 245768 | tf_op jit(solution)/shard_map/ppermute | solution.py:506
  36.0 5.2 %collective-permute-start.5 = (f32[20,8,128]{2,1,0:T(8,128)S(1)}, f32[20,8,128]{2,1,0:T(8,128)S(1)}, u32[]{:S(2)}, u32[]{:S(2)}) collective-permute-start(f32[20,8,128]{2,1,0:T(8,128)S(1)} %get-tuple-element.53), channel_id=1, source_target_pairs={{0,65},{1,2},{2,1},{3,4},{4,3},{5,6},{6,5},{7,14},{14,7},{15,12},{... | collective-permute-start | bytes 245768 | tf_op jit(solution)/shard_map/ppermute | solution.py:506
  42.2 1.4 %collective-permute-start.6 = (f32[25,8,128]{2,1,0:T(8,128)S(1)}, f32[25,8,128]{2,1,0:T(8,128)S(1)}, u32[]{:S(2)}, u32[]{:S(2)}) collective-permute-start(f32[25,8,128]{2,1,0:T(8,128)S(1)} %get-tuple-element.55), channel_id=1, source_target_pairs={{0,1},{1,0},{2,3},{3,2},{4,5},{5,4},{6,7},{7,6},{14,15},{15,14},{1... | collective-permute-start | bytes 307208 | tf_op jit(solution)/shard_map/ppermute | solution.py:506
  44.2 10.1 %collective-permute-start.7 = (f32[30,8,128]{2,1,0:T(8,128)S(1)}, f32[30,8,128]{2,1,0:T(8,128)S(1)}, u32[]{:S(2)}, u32[]{:S(2)}) collective-permute-start(f32[30,8,128]{2,1,0:T(8,128)S(1)} %get-tuple-element.58), channel_id=1, source_target_pairs={{0,65},{1,2},{2,1},{3,4},{4,3},{5,6},{6,5},{7,14},{14,7},{15,12},{... | collective-permute-start | bytes 368648 | tf_op jit(solution)/shard_map/ppermute | solution.py:506
  47.2 7.0 %collective-permute-start.9 = (f32[10,8,128]{2,1,0:T(8,128)S(1)}, f32[10,8,128]{2,1,0:T(8,128)S(1)}, u32[]{:S(2)}, u32[]{:S(2)}) collective-permute-start(f32[10,8,128]{2,1,0:T(8,128)S(1)} %get-tuple-element.59.refs_7_), channel_id=1, source_target_pairs={{0,69},{1,6},{2,67},{3,14},{4,65},{5,12},{6,1},{7,10},{14,3},{15,8... | collective-permute-start | bytes 122888 | tf_op jit(solution)/shard_map/ppermute | solution.py:506
  47.6 6.7 %collective-permute-start.8 = (f32[10,8,128]{2,1,0:T(8,128)S(1)}, f32[10,8,128]{2,1,0:T(8,128)S(1)}, u32[]{:S(2)}, u32[]{:S(2)}) collective-permute-start(f32[10,8,128]{2,1,0:T(8,128)S(1)} %get-tuple-element.59.refs_7_), channel_id=1, source_target_pairs={{0,67},{1,4},{2,65},{3,6},{4,1},{5,14},{6,3},{7,12},{14,5},{15,10}... | collective-permute-start | bytes 122888 | tf_op jit(solution)/shard_map/ppermute | solution.py:506
  54.3 1.4 %collective-permute-start.10 = (f32[30,8,128]{2,1,0:T(8,128)S(1)}, f32[30,8,128]{2,1,0:T(8,128)S(1)}, u32[]{:S(2)}, u32[]{:S(2)}) collective-permute-start(f32[30,8,128]{2,1,0:T(8,128)S(1)} %side.2.refs_8_), channel_id=1, source_target_pairs={{0,1},{1,0},{2,3},{3,2},{4,5},{5,4},{6,7},{7,6},{14,15},{15,14},{1... | collective-permute-start | bytes 368648 | tf_op jit(solution)/shard_map/ppermute | solution.py:506
  57.9 1.4 %collective-permute-start.11 = (f32[20,8,128]{2,1,0:T(8,128)S(1)}, f32[20,8,128]{2,1,0:T(8,128)S(1)}, u32[]{:S(2)}, u32[]{:S(2)}) collective-permute-start(f32[20,8,128]{2,1,0:T(8,128)S(1)} %get-tuple-element.62), channel_id=1, source_target_pairs={{0,1},{1,0},{2,3},{3,2},{4,5},{5,4},{6,7},{7,6},{14,15},{15,14},{1... | collective-permute-start | bytes 245768 | tf_op jit(solution)/shard_map/ppermute | solution.py:506
  58.1 5.1 %collective-permute-start.12 = (f32[20,8,128]{2,1,0:T(8,128)S(1)}, f32[20,8,128]{2,1,0:T(8,128)S(1)}, u32[]{:S(2)}, u32[]{:S(2)}) collective-permute-start(f32[20,8,128]{2,1,0:T(8,128)S(1)} %get-tuple-element.63), channel_id=1, source_target_pairs={{0,65},{1,2},{2,1},{3,4},{4,3},{5,6},{6,5},{7,14},{14,7},{15,12},{... | collective-permute-start | bytes 245768 | tf_op jit(solution)/shard_map/ppermute | solution.py:506
  64.2 1.4 %collective-permute-start.13 = (f32[20,8,128]{2,1,0:T(8,128)S(1)}, f32[20,8,128]{2,1,0:T(8,128)S(1)}, u32[]{:S(2)}, u32[]{:S(2)}) collective-permute-start(f32[20,8,128]{2,1,0:T(8,128)S(1)} %get-tuple-element.66), channel_id=1, source_target_pairs={{0,1},{1,0},{2,3},{3,2},{4,5},{5,4},{6,7},{7,6},{14,15},{15,14},{1... | collective-permute-start | bytes 245768 | tf_op jit(solution)/shard_map/ppermute | solution.py:506
  64.3 5.2 %collective-permute-start.14 = (f32[20,8,128]{2,1,0:T(8,128)S(1)}, f32[20,8,128]{2,1,0:T(8,128)S(1)}, u32[]{:S(2)}, u32[]{:S(2)}) collective-permute-start(f32[20,8,128]{2,1,0:T(8,128)S(1)} %get-tuple-element.67), channel_id=1, source_target_pairs={{0,65},{1,2},{2,1},{3,4},{4,3},{5,6},{6,5},{7,14},{14,7},{15,12},{... | collective-permute-start | bytes 245768 | tf_op jit(solution)/shard_map/ppermute | solution.py:506
  70.5 1.5 %collective-permute-start.15 = (f32[20,8,128]{2,1,0:T(8,128)S(1)}, f32[20,8,128]{2,1,0:T(8,128)S(1)}, u32[]{:S(2)}, u32[]{:S(2)}) collective-permute-start(f32[20,8,128]{2,1,0:T(8,128)S(1)} %get-tuple-element.70), channel_id=1, source_target_pairs={{0,1},{1,0},{2,3},{3,2},{4,5},{5,4},{6,7},{7,6},{14,15},{15,14},{1... | collective-permute-start | bytes 245768 | tf_op jit(solution)/shard_map/ppermute | solution.py:506
  70.8 5.2 %collective-permute-start.16 = (f32[20,8,128]{2,1,0:T(8,128)S(1)}, f32[20,8,128]{2,1,0:T(8,128)S(1)}, u32[]{:S(2)}, u32[]{:S(2)}) collective-permute-start(f32[20,8,128]{2,1,0:T(8,128)S(1)} %get-tuple-element.71), channel_id=1, source_target_pairs={{0,65},{1,2},{2,1},{3,4},{4,3},{5,6},{6,5},{7,14},{14,7},{15,12},{... | collective-permute-start | bytes 245768 | tf_op jit(solution)/shard_map/ppermute | solution.py:506
  77.1 1.4 %collective-permute-start.17 = (f32[25,8,128]{2,1,0:T(8,128)S(1)}, f32[25,8,128]{2,1,0:T(8,128)S(1)}, u32[]{:S(2)}, u32[]{:S(2)}) collective-permute-start(f32[25,8,128]{2,1,0:T(8,128)S(1)} %get-tuple-element.73), channel_id=1, source_target_pairs={{0,1},{1,0},{2,3},{3,2},{4,5},{5,4},{6,7},{7,6},{14,15},{15,14},{1... | collective-permute-start | bytes 307208 | tf_op jit(solution)/shard_map/ppermute | solution.py:506
  79.0 8.2 %collective-permute-start.18 = (f32[30,8,128]{2,1,0:T(8,128)S(1)}, f32[30,8,128]{2,1,0:T(8,128)S(1)}, u32[]{:S(2)}, u32[]{:S(2)}) collective-permute-start(f32[30,8,128]{2,1,0:T(8,128)S(1)} %get-tuple-element.76), channel_id=1, source_target_pairs={{0,65},{1,2},{2,1},{3,4},{4,3},{5,6},{6,5},{7,14},{14,7},{15,12},{... | collective-permute-start | bytes 368648 | tf_op jit(solution)/shard_map/ppermute | solution.py:506
  80.1 7.1 %collective-permute-start.20 = (f32[10,8,128]{2,1,0:T(8,128)S(1)}, f32[10,8,128]{2,1,0:T(8,128)S(1)}, u32[]{:S(2)}, u32[]{:S(2)}) collective-permute-start(f32[10,8,128]{2,1,0:T(8,128)S(1)} %get-tuple-element.77.refs_7_), channel_id=1, source_target_pairs={{0,69},{1,6},{2,67},{3,14},{4,65},{5,12},{6,1},{7,10},{14,3},{15,8... | collective-permute-start | bytes 122888 | tf_op jit(solution)/shard_map/ppermute | solution.py:506
  80.4 6.8 %collective-permute-start.19 = (f32[10,8,128]{2,1,0:T(8,128)S(1)}, f32[10,8,128]{2,1,0:T(8,128)S(1)}, u32[]{:S(2)}, u32[]{:S(2)}) collective-permute-start(f32[10,8,128]{2,1,0:T(8,128)S(1)} %get-tuple-element.77.refs_7_), channel_id=1, source_target_pairs={{0,67},{1,4},{2,65},{3,6},{4,1},{5,14},{6,3},{7,12},{14,5},{15,10}... | collective-permute-start | bytes 122888 | tf_op jit(solution)/shard_map/ppermute | solution.py:506
  87.3 1.4 %collective-permute-start.21 = (f32[30,8,128]{2,1,0:T(8,128)S(1)}, f32[30,8,128]{2,1,0:T(8,128)S(1)}, u32[]{:S(2)}, u32[]{:S(2)}) collective-permute-start(f32[30,8,128]{2,1,0:T(8,128)S(1)} %side.3.refs_8_), channel_id=1, source_target_pairs={{0,1},{1,0},{2,3},{3,2},{4,5},{5,4},{6,7},{7,6},{14,15},{15,14},{1... | collective-permute-start | bytes 368648 | tf_op jit(solution)/shard_map/ppermute | solution.py:506
  90.9 2.1 %collective-permute-start.22 = (f32[20,8,128]{2,1,0:T(8,128)S(1)}, f32[20,8,128]{2,1,0:T(8,128)S(1)}, u32[]{:S(2)}, u32[]{:S(2)}) collective-permute-start(f32[20,8,128]{2,1,0:T(8,128)S(1)} %get-tuple-element.80), channel_id=1, source_target_pairs={{0,1},{1,0},{2,3},{3,2},{4,5},{5,4},{6,7},{7,6},{14,15},{15,14},{1... | collective-permute-start | bytes 245768 | tf_op jit(solution)/shard_map/ppermute | solution.py:506
  91.1 5.1 %collective-permute-start.23 = (f32[20,8,128]{2,1,0:T(8,128)S(1)}, f32[20,8,128]{2,1,0:T(8,128)S(1)}, u32[]{:S(2)}, u32[]{:S(2)}) collective-permute-start(f32[20,8,128]{2,1,0:T(8,128)S(1)} %get-tuple-element.81), channel_id=1, source_target_pairs={{0,65},{1,2},{2,1},{3,4},{4,3},{5,6},{6,5},{7,14},{14,7},{15,12},{... | collective-permute-start | bytes 245768 | tf_op jit(solution)/shard_map/ppermute | solution.py:506
  97.2 4.3 %collective-permute-start.25 = (f32[20,8,128]{2,1,0:T(8,128)S(1)}, f32[20,8,128]{2,1,0:T(8,128)S(1)}, u32[]{:S(2)}, u32[]{:S(2)}) collective-permute-start(f32[20,8,128]{2,1,0:T(8,128)S(1)} %get-tuple-element.84), channel_id=1, source_target_pairs={{0,1},{1,0},{2,3},{3,2},{4,5},{5,4},{6,7},{7,6},{14,15},{15,14},{1... | collective-permute-start | bytes 245768 | tf_op jit(solution)/shard_map/ppermute | solution.py:506
  97.3 8.8 %collective-permute-start.26 = (f32[20,8,128]{2,1,0:T(8,128)S(1)}, f32[20,8,128]{2,1,0:T(8,128)S(1)}, u32[]{:S(2)}, u32[]{:S(2)}) collective-permute-start(f32[20,8,128]{2,1,0:T(8,128)S(1)} %get-tuple-element.85), channel_id=1, source_target_pairs={{0,65},{1,2},{2,1},{3,4},{4,3},{5,6},{6,5},{7,14},{14,7},{15,12},{... | collective-permute-start | bytes 245768 | tf_op jit(solution)/shard_map/ppermute | solution.py:506
  99.3 18.0 %collective-permute-start.24 = (f32[400,128]{1,0:T(8,128)S(1)}, f32[400,128]{1,0:T(8,128)S(1)}, u32[]{:S(2)}, u32[]{:S(2)}) collective-permute-start(f32[400,128]{1,0:T(8,128)S(1)} %get-tuple-element.82), channel_id=1, source_target_pairs={{0,0},{1,1},{2,2},{3,3},{4,4},{5,5},{6,6},{7,7},{14,8},{15,9},{12,... | collective-permute-start | bytes 614408 | tf_op jit(solution)/shard_map/ppermute | solution.py:506
  106.8 14.1 %collective-permute-start.27 = (f32[400,128]{1,0:T(8,128)S(1)}, f32[400,128]{1,0:T(8,128)S(1)}, u32[]{:S(2)}, u32[]{:S(2)}) collective-permute-start(f32[400,128]{1,0:T(8,128)S(1)} %residual.1), channel_id=1, source_target_pairs={{0,0},{1,1},{2,2},{3,3},{4,4},{5,5},{6,6},{7,7},{14,8},{15,9},{12,... | collective-permute-start | bytes 614408 | tf_op jit(solution)/shard_map/ppermute | solution.py:506

commit v2 on v1

--- a/solution.py
+++ b/solution.py
@@ -61,7 +61,7 @@
 
 
 class Moves:
-    def __init__(self, info=None):
+    def __init__(self, marks=None):
         sub = lax.broadcasted_iota(jnp.int32, (8, 128), 0)
         lane = lax.broadcasted_iota(jnp.int32, (8, 128), 1)
         self.low = sub < 4
@@ -70,10 +70,10 @@
         self.lane_first = lane == 0
         self.lane_last = lane == 127
         self.last = jnp.logical_and(lane == 127, sub >= 4)
-        if info is not None:
-            self.even = jnp.full((8, 128), info[0], jnp.int32) == 0
-            self.copy0 = jnp.full((8, 128), info[1], jnp.int32) == 0
-            self.strip = info[2]
+        self.marks = marks
+        if marks is not None:
+            self.even = marks[0] > 0.5
+            self.copy0 = marks[1] > 0.5
 
     def above(self, x):
         return jnp.where(self.top, 0.0, pltpu.roll(x, 7, 0))
@@ -130,9 +130,8 @@
             b_ref[first + a * 5 + c] = mv.pick(low, high)
 
 
-def got_faces(mv, a_ref, b_ref, count, strips, a_first=0, b_first=0):
-    has_left = jnp.where(mv.strip > 0, 1.0, 0.0).astype(F32)
-    has_right = jnp.where(mv.strip < strips - 1, 1.0, 0.0).astype(F32)
+def got_faces(mv, a_ref, b_ref, count, a_first=0, b_first=0):
+    has_left, has_right = mv.marks[2], mv.marks[3]
     left, right = [], []
     for k in range(count):
         x, y = a_ref[a_first + k], b_ref[b_first + k]
@@ -176,17 +175,17 @@
         out_ref[pl.ds(4 * n, 8)] = jnp.where(mv.low, x, y)
 
 
-def pack_kernel(load_ref, kappa_ref, wet_ref, out_ref):
+def pack_kernel(load_ref, out_ref):
     row = lax.broadcasted_iota(jnp.int32, (100, 128), 0)
     out_ref[pl.ds(0, 100)] = load_ref[pl.ds(0, 100)] + jnp.where((row & 3) == 0, 0.0, load_ref[pl.ds(399, 100)])
     out_ref[pl.ds(100, 300)] = load_ref[pl.ds(100, 300)]
-    coeff = kappa_ref[...] * jnp.where(wet_ref[...] == 1, 1.0, 0.05).astype(F32)
+    coeff = load_ref[pl.ds(500, 4)]
     out_ref[pl.ds(400, 4)] = coeff
     out_ref[pl.ds(404, 4)] = coeff
 
 
-def unpack_kernel(info, same_ref, other_ref, f_ref, coeff_ref, a_ref, b_ref):
-    mv = Moves(info)
+def unpack_kernel(marks, same_ref, other_ref, f_ref, coeff_ref, a_ref, b_ref):
+    mv = Moves(marks)
 
     def pair(n):
         x, y = same_ref[pl.ds(4 * n, 8)], other_ref[pl.ds(4 * n, 8)]
@@ -205,9 +204,9 @@
     b_ref[20] = coeff
 
 
-def first_kernel(strips, info, part_ref, coeff_ref, ga_ref, gb_ref, u_ref, y_ref, f_ref, inv_ref, a_ref, b_ref, acc_ref, up_ref):
-    mv = Moves(info)
-    left, right = got_faces(mv, ga_ref, gb_ref, 21, strips)
+def first_kernel(marks, part_ref, coeff_ref, ga_ref, gb_ref, u_ref, y_ref, f_ref, inv_ref, a_ref, b_ref, acc_ref, up_ref):
+    mv = Moves(marks)
+    left, right = got_faces(mv, ga_ref, gb_ref, 21)
     coeff = coeff_ref[...]
     for kind_b, value in enumerate((coeff + left[20], coeff, coeff + right[20])):
         for kind_a, v in enumerate((value + mv.below(value), value)):
@@ -229,22 +228,22 @@
     put_faces(mv, y_ref, a_ref, b_ref)
 
 
-def sweep_kernel(strips, info, u_ref, y_ref, f_ref, inv_ref, coeff_ref, ga_ref, gb_ref, un_ref, yn_ref, a_ref, b_ref, acc_ref, up_ref):
-    mv = Moves(info)
-    left, right = got_faces(mv, ga_ref, gb_ref, 20, strips)
+def sweep_kernel(marks, u_ref, y_ref, f_ref, inv_ref, coeff_ref, ga_ref, gb_ref, un_ref, yn_ref, a_ref, b_ref, acc_ref, up_ref):
+    mv = Moves(marks)
+    left, right = got_faces(mv, ga_ref, gb_ref, 20)
     smooth(mv, u_ref, f_ref, y_ref, left, right, inv_ref, un_ref)
     apply_operator(mv, un_ref, coeff_ref[...], yn_ref, acc_ref, up_ref)
     put_faces(mv, yn_ref, a_ref, b_ref)
 
 
-def last_sweep_kernel(strips, info, u_ref, y_ref, f_ref, inv_ref, coeff_ref, ga_ref, gb_ref, yn_ref, a_ref, b_ref, half_ref, un_ref, acc_ref, up_ref):
-    sweep_kernel(strips, info, u_ref, y_ref, f_ref, inv_ref, coeff_ref, ga_ref, gb_ref, un_ref, yn_ref, a_ref, b_ref, acc_ref, up_ref)
-    half_rows(Moves(info), un_ref, half_ref)
-
-
-def restrict_kernel(strips, info, u_ref, y_ref, f_ref, inv_ref, coeff_ref, ga_ref, gb_ref, part_ref, un_ref, own_ref, a_ref, b_ref, yn_ref, acc_ref, up_ref):
-    mv = Moves(info)
-    left, right = got_faces(mv, ga_ref, gb_ref, 20, strips)
+def last_sweep_kernel(marks, u_ref, y_ref, f_ref, inv_ref, coeff_ref, ga_ref, gb_ref, yn_ref, a_ref, b_ref, half_ref, un_ref, acc_ref, up_ref):
+    sweep_kernel(marks, u_ref, y_ref, f_ref, inv_ref, coeff_ref, ga_ref, gb_ref, un_ref, yn_ref, a_ref, b_ref, acc_ref, up_ref)
+    half_rows(Moves(marks), un_ref, half_ref)
+
+
+def restrict_kernel(marks, u_ref, y_ref, f_ref, inv_ref, coeff_ref, ga_ref, gb_ref, part_ref, un_ref, own_ref, a_ref, b_ref, yn_ref, acc_ref, up_ref):
+    mv = Moves(marks)
+    left, right = got_faces(mv, ga_ref, gb_ref, 20)
     smooth(mv, u_ref, f_ref, y_ref, left, right, inv_ref, un_ref)
     apply_operator(mv, un_ref, coeff_ref[...], yn_ref, acc_ref, up_ref)
     put_faces(mv, yn_ref, a_ref, b_ref, 5)
@@ -270,8 +269,8 @@
         a_ref[k] = own_ref[k]
 
 
-def chip_kernel(info, own_ref, ga_ref, b_ref, chip_ref, near_ref):
-    mv = Moves(info)
+def chip_kernel(marks, own_ref, ga_ref, b_ref, chip_ref, near_ref):
+    mv = Moves(marks)
     for k in range(5):
         x, y = own_ref[k], ga_ref[k]
         low, high = mv.pick(x, y), mv.pick(y, x)
@@ -290,12 +289,11 @@
         out_ref[20 + k] = third_ref[k]
 
 
-def coarse_solve(mv, strips, chip_ref, mine_ref, other_ref):
-    base = mv.strip - (mv.strip & 1) - 6
+def coarse_solve(mv, chip_ref, mine_ref, other_ref):
     window = []
     for w in range(WIN):
         rows = []
-        ok = jnp.where(jnp.logical_and(base + w >= 0, base + w < strips), 1.0, 0.0).astype(F32)
+        ok = mv.marks[4 + w]
         for k in range(5):
             if w in (6, 7):
                 rows.append(chip_ref[(w - 6) * 5 + k])
@@ -398,10 +396,10 @@
     return out
 
 
-def correct_kernel(strips, info, u_ref, f_ref, inv_ref, coeff_ref, ga_ref, near_ref, chip_ref, mine_ref, other_ref, un_ref, yn_ref, a_ref, b_ref, ua_ref, ya_ref, face_ref, acc_ref, up_ref):
-    mv = Moves(info)
+def correct_kernel(marks, u_ref, f_ref, inv_ref, coeff_ref, ga_ref, near_ref, chip_ref, mine_ref, other_ref, un_ref, yn_ref, a_ref, b_ref, ua_ref, ya_ref, face_ref, acc_ref, up_ref):
+    mv = Moves(marks)
     coeff = coeff_ref[...]
-    lines, coeff_left, coeff_right = coarse_solve(mv, strips, chip_ref, mine_ref, other_ref)
+    lines, coeff_left, coeff_right = coarse_solve(mv, chip_ref, mine_ref, other_ref)
     for k, v in enumerate(neighbour_face(mv, lines[1], lines[0], coeff_left)):
         face_ref[k] = v
     for k, v in enumerate(neighbour_face(mv, lines[2], lines[3], coeff_right)):
@@ -418,7 +416,7 @@
                     v = float(INTERP[b, 0]) * low[a][c] + float(INTERP[b, 1]) * high[a][c]
                 ua_ref[at(a, b, c)] = u_ref[at(a, b, c)] + v
     apply_operator(mv, ua_ref, coeff, ya_ref, acc_ref, up_ref)
-    left, right = got_faces(mv, ga_ref, near_ref, 20, strips, 5, 10)
+    left, right = got_faces(mv, ga_ref, near_ref, 20, 5, 10)
     left = [left[k] + face_ref[k] for k in range(20)]
     right = [right[k] + face_ref[20 + k] for k in range(20)]
     smooth(mv, ua_ref, f_ref, ya_ref, left, right, inv_ref, un_ref)
@@ -426,9 +424,9 @@
     put_faces(mv, yn_ref, a_ref, b_ref)
 
 
-def residual_kernel(strips, info, y_ref, f_ref, ga_ref, gb_ref, half_ref, r_ref):
-    mv = Moves(info)
-    left, right = got_faces(mv, ga_ref, gb_ref, 20, strips)
+def residual_kernel(marks, y_ref, f_ref, ga_ref, gb_ref, half_ref, r_ref):
+    mv = Moves(marks)
+    left, right = got_faces(mv, ga_ref, gb_ref, 20)
     for a in range(4):
         for b in range(N):
             r = residual_row(mv, f_ref, y_ref, left, right, a, b)
@@ -445,37 +443,34 @@
 
 
 VM = pl.BlockSpec(memory_space=pltpu.VMEM)
-SM = pl.BlockSpec(memory_space=pltpu.SMEM)
 FIELD = (100, 8, 128)
 WORK = [(125, 8, 128), (25, 8, 128)]
 
 
-def call(name, kernel, outs, scratch, info, *args):
-    specs = [VM] * len(args)
-    operands = args
-    if info is not None:
-        specs, operands = [SM] + specs, (info, *args)
+def call(name, kernel, outs, scratch, *args):
     return pl.pallas_call(
         kernel,
         out_shape=[jax.ShapeDtypeStruct(s, F32) for s in outs],
-        in_specs=specs,
+        in_specs=[VM] * len(args),
         out_specs=[VM] * len(outs),
         scratch_shapes=[pltpu.VMEM(s, F32) for s in scratch],
         compiler_params=pltpu.CompilerParams(vmem_limit_bytes=12 * 1024 * 1024),
         name=name,
-    )(*operands)
+    )(*args)
+
+
+MODE = "flip"
 
 
 def placement(sizes):
     _, ey, lin = sizes
-    if (ey, lin) != (2, 64):
-        return list(range(ey * lin))
-    order = []
-    for q in range(64):
-        side, p, y = q // 32, (q % 32) // 4, q % 4
-        z = p if side == 0 else 7 - p
-        order.append(side * 64 + z * 8 + (y if p % 2 == 0 else 3 - y) * 2)
-    return [order[s // 2] + s % 2 for s in range(128)]
+    place = list(range(ey * lin))
+    if lin == 64 and MODE == "flip":
+        for s in range(ey * lin):
+            z, y, core = s // 8 % 8, s // 2 % 4, s % 2
+            if z % 2:
+                place[s] = s - y * 2 + (3 - y) * 2
+    return place
 
 
 def per_device(sizes):
@@ -492,62 +487,67 @@
         pairs = []
         for e in range(2):
             for s in range(strips):
-                k = (s // 2 - d) % chips if s % 2 == 0 else (s // 2 + d) % chips
-                pairs.append((device[e][s], device[e][2 * k + 1 - s % 2]))
+                k = s // 2 - d if s % 2 == 0 else s // 2 + d
+                if 0 <= k < chips:
+                    pairs.append((device[e][s], device[e][2 * k + 1 - s % 2]))
+                else:
+                    pairs.append((device[e][s], device[1 - e][s]))
         return pairs
 
     beyond = {d: chip_pairs(d) for d in (1, 2, 3)}
-    table = np.zeros((2 * strips, 4), np.int32)
+    table = np.zeros((2 * strips, 4 + WIN), np.float32)
     for copy in range(2):
         for s in range(strips):
-            table[device[copy][s], :3] = (s % 2, copy, s)
+            window = [0 <= s - s % 2 - 6 + w < strips for w in range(WIN)]
+            table[device[copy][s]] = [s % 2 == 0, copy == 0, s > 0, s < strips - 1, *window]
 
     def swap(x, pairs):
         return lax.ppermute(x, AXES, pairs)
 
+    def restore(x):
+        return x if place == sorted(place) else swap(x, back)
+
     def run(load, kappa, wet):
-        info = lax.dynamic_index_in_dim(jnp.asarray(table), lax.axis_index(AXES), 0, keepdims=False)
-        (packed,) = call("pack", pack_kernel, [(408, 128)], [], None, load.reshape(500, 128), kappa.reshape(4, 128), wet.reshape(4, 128))
-        same, other = swap(packed, to_same), swap(packed, to_other)
-        part, coeff, a, b = call("unpack", unpack_kernel, [FIELD, (8, 128), (21, 8, 128), (21, 8, 128)], [], info, same, other)
+        marks = lax.dynamic_index_in_dim(jnp.asarray(table), lax.axis_index(AXES), 0, keepdims=False)
+        marks = jnp.broadcast_to(marks[:, None, None], (4 + WIN, 8, 128))
+        coeff = kappa * jnp.where(wet == 1, 1.0, 0.05).astype(F32)
+        packed = jnp.concatenate([load.reshape(500, 1, 128), coeff.reshape(4, 1, 128)]).reshape(504, 128)
+        (packed,) = call("pack", pack_kernel, [(408, 128)], [], packed)
+        same, other = packed if place == sorted(place) else swap(packed, to_same), swap(packed, to_other)
+        part, coeff, a, b = call("unpack", unpack_kernel, [FIELD, (8, 128), (21, 8, 128), (21, 8, 128)], [], marks, same, other)
         faces = [(20, 8, 128), (20, 8, 128)]
-
-        def bound(kernel):
-            def body(*refs):
-                kernel(strips, *refs)
-            return body
 
         def trade(a, b):
             return swap(a, within), swap(b, beyond[1])
 
         a, b = trade(a, b)
-        u, y, f, inv, a, b = call("first", bound(first_kernel), [FIELD, FIELD, FIELD, (12, 8, 128), *faces], WORK, info, part, coeff, a, b)
+        u, y, f, inv, a, b = call("first", first_kernel, [FIELD, FIELD, FIELD, (12, 8, 128), *faces], WORK, marks, part, coeff, a, b)
 
         def sweep(u, y, a, b):
             a, b = trade(a, b)
-            return call("sweep", bound(sweep_kernel), [FIELD, FIELD, *faces], WORK, info, u, y, f, inv, coeff, a, b)
+            return call("sweep", sweep_kernel, [FIELD, FIELD, *faces], WORK, marks, u, y, f, inv, coeff, a, b)
 
         def sweep_and_correct(u, y, a, b):
             a, b = trade(a, b)
-            u, own, a, b = call("restrict", bound(restrict_kernel), [FIELD, (5, 8, 128), (25, 8, 128), (25, 8, 128)], [FIELD, *WORK], info, u, y, f, inv, coeff, a, b, part)
+            u, own, a, b = call("restrict", restrict_kernel, [FIELD, (5, 8, 128), (25, 8, 128), (25, 8, 128)], [FIELD, *WORK], marks, u, y, f, inv, coeff, a, b, part)
             a = swap(a, within)
-            chip, near = call("chip", chip_kernel, [(10, 8, 128), (30, 8, 128)], [], info, own, a, b)
+            chip, near = call("chip", chip_kernel, [(10, 8, 128), (30, 8, 128)], [], marks, own, a, b)
             near, second, third = swap(near, beyond[1]), swap(chip, beyond[2]), swap(chip, beyond[3])
-            (mine,) = call("side", side_kernel, [(30, 8, 128)], [], None, near, second, third)
+            (mine,) = call("side", side_kernel, [(30, 8, 128)], [], near, second, third)
             theirs = swap(mine, within)
-            return call("correct", bound(correct_kernel), [FIELD, FIELD, *faces], [FIELD, FIELD, (40, 8, 128), *WORK], info, u, f, inv, coeff, a, near, chip, mine, theirs)
+            return call("correct", correct_kernel, [FIELD, FIELD, *faces], [FIELD, FIELD, (40, 8, 128), *WORK], marks, u, f, inv, coeff, a, near, chip, mine, theirs)
 
         u, y, a, b = sweep_and_correct(u, y, a, b)
         u, y, a, b = sweep(u, y, a, b)
         u, y, a, b = sweep(u, y, a, b)
         u, y, a, b = sweep_and_correct(u, y, a, b)
         a, b = trade(a, b)
-        y, a, b, half = call("last", bound(last_sweep_kernel), [FIELD, *faces, (400, 128)], [FIELD, *WORK], info, u, y, f, inv, coeff, a, b)
+        y, a, b, half = call("last", last_sweep_kernel, [FIELD, *faces, (400, 128)], [FIELD, *WORK], marks, u, y, f, inv, coeff, a, b)
         a, b = trade(a, b)
-        half = swap(half, back)
-        (left_half,) = call("residual", bound(residual_kernel), [(400, 128)], [FIELD], info, y, f, a, b)
-        (solved,) = call("spread", spread_kernel, [(500, 128)], [], None, half)
-        (rest,) = call("spread", spread_kernel, [(500, 128)], [], None, swap(left_half, back))
+        half = restore(half)
+        (left_half,) = call("residual", residual_kernel, [(400, 128)], [FIELD], marks, y, f, a, b)
+        (solved,) = call("spread", spread_kernel, [(500, 128)], [], half)
+        (rest,) = call("spread", spread_kernel, [(500, 128)], [], restore(left_half))
         return solved.reshape(load.shape), rest.reshape(load.shape)
 
     return run

time: 122 us -> 104 us (0.85)
  the two profiles are of different devices: /device:TPU:98 before, /device:TPU:225 now
where the time goes in v2:
time: 104 us
  waiting for transfers between devices  55.7 us (54%)
  starting transfers between devices  36.6 us (35%)
  Pallas kernels  6.74 us (6%)
  local copies, waits for them, and re-layouts  3.95 us (4%)
    ppermute x28, waiting for transfers between devices, swap(): return lax.ppermute(x, AXES, pairs)  55.7 us
    ppermute x28, starting transfers between devices, swap(): return lax.ppermute(x, AXES, pairs)  36.6 us
    pallas_call x17, Pallas kernels, call(): pl.pallas_call(kernel, out_shape=[jax.ShapeDtypeStruct(s, F32) for s in o...  6.74 us
  transfers between devices with their start and end apart: 28, of which 19 were waited for; matrix products, arithmetic and copies ran while one was open for 1% of the time, Pallas kernels for 0%

profile of v2, /device:TPU:225, one launch (start us, length us, event | category | flops | bytes accessed | tf_op | source)
XLA Modules:
  0.0 103.9 jit_solution(1421669263485763894)
XLA Ops:
  0.6 1.0 copy.12
  1.6 0.0 copy-start
  1.6 0.7 copy-done
  2.4 5.3 %collective-permute-start.1 = (f32[408,128]{1,0:T(8,128)S(1)}, f32[408,128]{1,0:T(8,128)S(1)}, u32[]{:S(2)}, u32[]{:S(2)}) collective-permute-start(f32[408,128]{1,0:T(8,128)S(1)} %pack.1), channel_id=1, source_target_pairs={{0,128},{1,129},{2,130},{3,131},{4,132},{5,133},{6,134},{7,135},{8... | collective-permute-start | bytes 626696 | tf_op jit(solution)/shard_map/ppermute | solution.py:505
  7.6 1.9 %collective-permute-start = (f32[408,128]{1,0:T(8,128)S(1)}, f32[408,128]{1,0:T(8,128)S(1)}, u32[]{:S(2)}, u32[]{:S(2)}) collective-permute-start(f32[408,128]{1,0:T(8,128)S(1)} %pack.1), channel_id=1, source_target_pairs={{0,0},{1,1},{2,2},{3,3},{4,4},{5,5},{6,6},{7,7},{8,14},{9,15},{10,... | collective-permute-start | bytes 626696 | tf_op jit(solution)/shard_map/ppermute | solution.py:505
  9.6 0.7 dynamic-slice_bitcast_fusion
  10.3 2.1 %collective-permute-done.1.other_ref = f32[408,128]{1,0:T(8,128)S(1)} collective-permute-done((f32[408,128]{1,0:T(8,128)S(1)}, f32[408,128]{1,0:T(8,128)S(1)}, u32[]{:S(2)}, u32[]{:S(2)}) %collective-permute-start.1) | collective-permute-done | bytes 208928 | tf_op jit(solution)/shard_map/ppermute | solution.py:505
  12.3 4.6 %collective-permute-done.same_ref = f32[408,128]{1,0:T(8,128)S(1)} collective-permute-done((f32[408,128]{1,0:T(8,128)S(1)}, f32[408,128]{1,0:T(8,128)S(1)}, u32[]{:S(2)}, u32[]{:S(2)}) %collective-permute-start) | collective-permute-done | bytes 208928 | tf_op jit(solution)/shard_map/ppermute | solution.py:505
  16.9 0.1 broadcast_in_dim.17.marks
  17.0 0.1 unpack.1
  17.1 1.5 %collective-permute-start.2 = (f32[21,8,128]{2,1,0:T(8,128)S(1)}, f32[21,8,128]{2,1,0:T(8,128)S(1)}, u32[]{:S(2)}, u32[]{:S(2)}) collective-permute-start(f32[21,8,128]{2,1,0:T(8,128)S(1)} %get-tuple-element.46), channel_id=1, source_target_pairs={{0,1},{1,0},{2,3},{3,2},{4,5},{5,4},{6,7},{7,6},{14,15},{15,14},{1... | collective-permute-start | bytes 258056 | tf_op jit(solution)/shard_map/ppermute | solution.py:505
  18.6 0.0 collective-permute-start.3
  18.6 0.9 collective-permute-done.2.ga_ref
  19.5 5.1 %collective-permute-done.3.gb_ref = f32[21,8,128]{2,1,0:T(8,128)S(1)} collective-permute-done((f32[21,8,128]{2,1,0:T(8,128)S(1)}, f32[21,8,128]{2,1,0:T(8,128)S(1)}, u32[]{:S(2)}, u32[]{:S(2)}) %collective-permute-start.3) | collective-permute-done | bytes 86048 | tf_op jit(solution)/shard_map/ppermute | solution.py:505
  24.6 0.5 first.1
  25.1 0.1 collective-permute-start.4
  25.2 0.1 collective-permute-start.5
  25.3 1.2 %collective-permute-done.4.ga_ref = f32[20,8,128]{2,1,0:T(8,128)S(1)} collective-permute-done((f32[20,8,128]{2,1,0:T(8,128)S(1)}, f32[20,8,128]{2,1,0:T(8,128)S(1)}, u32[]{:S(2)}, u32[]{:S(2)}) %collective-permute-start.4) | collective-permute-done | bytes 81952 | tf_op jit(solution)/shard_map/ppermute | solution.py:505
  26.5 4.8 %collective-permute-done.5.gb_ref = f32[20,8,128]{2,1,0:T(8,128)S(1)} collective-permute-done((f32[20,8,128]{2,1,0:T(8,128)S(1)}, f32[20,8,128]{2,1,0:T(8,128)S(1)}, u32[]{:S(2)}, u32[]{:S(2)}) %collective-permute-start.5) | collective-permute-done | bytes 81952 | tf_op jit(solution)/shard_map/ppermute | solution.py:505
  31.3 0.5 restrict.2
  31.8 0.1 collective-permute-start.6
  31.9 1.3 %collective-permute-done.6.ga_ref = f32[25,8,128]{2,1,0:T(8,128)S(1)} collective-permute-done((f32[25,8,128]{2,1,0:T(8,128)S(1)}, f32[25,8,128]{2,1,0:T(8,128)S(1)}, u32[]{:S(2)}, u32[]{:S(2)}) %collective-permute-start.6) | collective-permute-done | bytes 102432 | tf_op jit(solution)/shard_map/ppermute | solution.py:505
  33.3 0.2 collective-permute-start.7
  33.4 0.0 collective-permute-start.9
  33.5 5.0 %collective-permute-start.8 = (f32[10,8,128]{2,1,0:T(8,128)S(1)}, f32[10,8,128]{2,1,0:T(8,128)S(1)}, u32[]{:S(2)}, u32[]{:S(2)}) collective-permute-start(f32[10,8,128]{2,1,0:T(8,128)S(1)} %get-tuple-element.59.chip_ref), channel_id=1, source_target_pairs={{0,128},{1,4},{2,130},{3,6},{4,1},{5,14},{6,3},{7,12},{14,5},{15,1... | collective-permute-start | bytes 122888 | tf_op jit(solution)/shard_map/ppermute | solution.py:505
  38.4 3.1 %collective-permute-done.9.third_ref = f32[10,8,128]{2,1,0:T(8,128)S(1)} collective-permute-done((f32[10,8,128]{2,1,0:T(8,128)S(1)}, f32[10,8,128]{2,1,0:T(8,128)S(1)}, u32[]{:S(2)}, u32[]{:S(2)}) %collective-permute-start.9) | collective-permute-done | bytes 40992 | tf_op jit(solution)/shard_map/ppermute | solution.py:505
  41.5 0.0 collective-permute-done.8.second_ref
  41.5 1.0 collective-permute-start.10
  42.5 1.0 collective-permute-done.10.other_ref
  43.5 1.6 %correct.2 = (f32[100,8,128]{2,1,0:T(8,128)S(1)}, f32[100,8,128]{2,1,0:T(8,128)S(1)}, f32[20,8,128]{2,1,0:T(8,128)S(1)}, f32[20,8,128]{2,1,0:T(8,128)S(1)}) custom-call(f32[18,8,128]{2,1,0:T(8,128)S(1)} %broadcast_in_dim.17.marks, f32[100,8,128]{2,1,0:T(8,128)S(1)} %get-tuple-element.54.u_ref, f32[100,8,128]{2,1,0:T(8,128)S(1)} %get-tuple-element.50.f_ref, ...), custom_call_target="tpu_custom_call" | custom-call | tf_op jit(solution)/shard_map/correct/pallas_call | solution.py:451
  45.1 0.4 collective-permute-start.11
  45.6 2.9 %collective-permute-start.12 = (f32[20,8,128]{2,1,0:T(8,128)S(1)}, f32[20,8,128]{2,1,0:T(8,128)S(1)}, u32[]{:S(2)}, u32[]{:S(2)}) collective-permute-start(f32[20,8,128]{2,1,0:T(8,128)S(1)} %get-tuple-element.63), channel_id=1, source_target_pairs={{0,128},{1,2},{2,1},{3,4},{4,3},{5,6},{6,5},{7,14},{14,7},{15,12},... | collective-permute-start | bytes 245768 | tf_op jit(solution)/shard_map/ppermute | solution.py:505
  48.5 3.1 %collective-permute-done.12.gb_ref = f32[20,8,128]{2,1,0:T(8,128)S(1)} collective-permute-done((f32[20,8,128]{2,1,0:T(8,128)S(1)}, f32[20,8,128]{2,1,0:T(8,128)S(1)}, u32[]{:S(2)}, u32[]{:S(2)}) %collective-permute-start.12) | collective-permute-done | bytes 81952 | tf_op jit(solution)/shard_map/ppermute | solution.py:505
  51.6 0.5 sweep.2
  52.1 0.1 collective-permute-start.13
  52.2 2.9 %collective-permute-start.14 = (f32[20,8,128]{2,1,0:T(8,128)S(1)}, f32[20,8,128]{2,1,0:T(8,128)S(1)}, u32[]{:S(2)}, u32[]{:S(2)}) collective-permute-start(f32[20,8,128]{2,1,0:T(8,128)S(1)} %get-tuple-element.67), channel_id=1, source_target_pairs={{0,128},{1,2},{2,1},{3,4},{4,3},{5,6},{6,5},{7,14},{14,7},{15,12},... | collective-permute-start | bytes 245768 | tf_op jit(solution)/shard_map/ppermute | solution.py:505
  55.1 3.2 %collective-permute-done.14.gb_ref = f32[20,8,128]{2,1,0:T(8,128)S(1)} collective-permute-done((f32[20,8,128]{2,1,0:T(8,128)S(1)}, f32[20,8,128]{2,1,0:T(8,128)S(1)}, u32[]{:S(2)}, u32[]{:S(2)}) %collective-permute-start.14) | collective-permute-done | bytes 81952 | tf_op jit(solution)/shard_map/ppermute | solution.py:505
  58.4 0.5 sweep.3
  58.8 0.1 collective-permute-start.15
  58.9 3.0 %collective-permute-start.16 = (f32[20,8,128]{2,1,0:T(8,128)S(1)}, f32[20,8,128]{2,1,0:T(8,128)S(1)}, u32[]{:S(2)}, u32[]{:S(2)}) collective-permute-start(f32[20,8,128]{2,1,0:T(8,128)S(1)} %get-tuple-element.71), channel_id=1, source_target_pairs={{0,128},{1,2},{2,1},{3,4},{4,3},{5,6},{6,5},{7,14},{14,7},{15,12},... | collective-permute-start | bytes 245768 | tf_op jit(solution)/shard_map/ppermute | solution.py:505
  61.9 3.3 %collective-permute-done.16.gb_ref = f32[20,8,128]{2,1,0:T(8,128)S(1)} collective-permute-done((f32[20,8,128]{2,1,0:T(8,128)S(1)}, f32[20,8,128]{2,1,0:T(8,128)S(1)}, u32[]{:S(2)}, u32[]{:S(2)}) %collective-permute-start.16) | collective-permute-done | bytes 81952 | tf_op jit(solution)/shard_map/ppermute | solution.py:505
  65.2 0.6 restrict.3
  65.8 0.1 collective-permute-start.17
  65.9 1.3 %collective-permute-done.17.ga_ref = f32[25,8,128]{2,1,0:T(8,128)S(1)} collective-permute-done((f32[25,8,128]{2,1,0:T(8,128)S(1)}, f32[25,8,128]{2,1,0:T(8,128)S(1)}, u32[]{:S(2)}, u32[]{:S(2)}) %collective-permute-start.17) | collective-permute-done | bytes 102432 | tf_op jit(solution)/shard_map/ppermute | solution.py:505
  67.2 2.8 %collective-permute-start.18 = (f32[30,8,128]{2,1,0:T(8,128)S(1)}, f32[30,8,128]{2,1,0:T(8,128)S(1)}, u32[]{:S(2)}, u32[]{:S(2)}) collective-permute-start(f32[30,8,128]{2,1,0:T(8,128)S(1)} %get-tuple-element.76), channel_id=1, source_target_pairs={{0,128},{1,2},{2,1},{3,4},{4,3},{5,6},{6,5},{7,14},{14,7},{15,12},... | collective-permute-start | bytes 368648 | tf_op jit(solution)/shard_map/ppermute | solution.py:505
  70.0 2.4 %collective-permute-start.19 = (f32[10,8,128]{2,1,0:T(8,128)S(1)}, f32[10,8,128]{2,1,0:T(8,128)S(1)}, u32[]{:S(2)}, u32[]{:S(2)}) collective-permute-start(f32[10,8,128]{2,1,0:T(8,128)S(1)} %get-tuple-element.77.chip_ref), channel_id=1, source_target_pairs={{0,128},{1,4},{2,130},{3,6},{4,1},{5,14},{6,3},{7,12},{14,5},{15,1... | collective-permute-start | bytes 122888 | tf_op jit(solution)/shard_map/ppermute | solution.py:505
  72.4 5.6 %collective-permute-done.20.third_ref = f32[10,8,128]{2,1,0:T(8,128)S(1)} collective-permute-done((f32[10,8,128]{2,1,0:T(8,128)S(1)}, f32[10,8,128]{2,1,0:T(8,128)S(1)}, u32[]{:S(2)}, u32[]{:S(2)}) %collective-permute-start.20) | collective-permute-done | bytes 40992 | tf_op jit(solution)/shard_map/ppermute | solution.py:505
  77.9 0.1 collective-permute-start.21
  78.0 1.3 %collective-permute-done.21.other_ref = f32[30,8,128]{2,1,0:T(8,128)S(1)} collective-permute-done((f32[30,8,128]{2,1,0:T(8,128)S(1)}, f32[30,8,128]{2,1,0:T(8,128)S(1)}, u32[]{:S(2)}, u32[]{:S(2)}) %collective-permute-start.21) | collective-permute-done | bytes 122912 | tf_op jit(solution)/shard_map/ppermute | solution.py:505
  79.4 1.7 %correct.3 = (f32[100,8,128]{2,1,0:T(8,128)S(1)}, f32[100,8,128]{2,1,0:T(8,128)S(1)}, f32[20,8,128]{2,1,0:T(8,128)S(1)}, f32[20,8,128]{2,1,0:T(8,128)S(1)}) custom-call(f32[18,8,128]{2,1,0:T(8,128)S(1)} %broadcast_in_dim.17.marks, f32[100,8,128]{2,1,0:T(8,128)S(1)} %get-tuple-element.72.u_ref, f32[100,8,128]{2,1,0:T(8,128)S(1)} %get-tuple-element.50.f_ref, ...), custom_call_target="tpu_custom_call" | custom-call | tf_op jit(solution)/shard_map/correct/pallas_call | solution.py:451
  81.0 0.2 collective-permute-start.22
  81.3 1.3 %collective-permute-start.23 = (f32[20,8,128]{2,1,0:T(8,128)S(1)}, f32[20,8,128]{2,1,0:T(8,128)S(1)}, u32[]{:S(2)}, u32[]{:S(2)}) collective-permute-start(f32[20,8,128]{2,1,0:T(8,128)S(1)} %get-tuple-element.81), channel_id=1, source_target_pairs={{0,128},{1,2},{2,1},{3,4},{4,3},{5,6},{6,5},{7,14},{14,7},{15,12},... | collective-permute-start | bytes 245768 | tf_op jit(solution)/shard_map/ppermute | solution.py:505
  82.5 4.7 %collective-permute-done.23.gb_ref = f32[20,8,128]{2,1,0:T(8,128)S(1)} collective-permute-done((f32[20,8,128]{2,1,0:T(8,128)S(1)}, f32[20,8,128]{2,1,0:T(8,128)S(1)}, u32[]{:S(2)}, u32[]{:S(2)}) %collective-permute-start.23) | collective-permute-done | bytes 81952 | tf_op jit(solution)/shard_map/ppermute | solution.py:505
  87.2 0.5 last.1
  87.8 0.1 collective-permute-start.25
  87.9 1.3 %collective-permute-start.26 = (f32[20,8,128]{2,1,0:T(8,128)S(1)}, f32[20,8,128]{2,1,0:T(8,128)S(1)}, u32[]{:S(2)}, u32[]{:S(2)}) collective-permute-start(f32[20,8,128]{2,1,0:T(8,128)S(1)} %get-tuple-element.85), channel_id=1, source_target_pairs={{0,128},{1,2},{2,1},{3,4},{4,3},{5,6},{6,5},{7,14},{14,7},{15,12},... | collective-permute-start | bytes 245768 | tf_op jit(solution)/shard_map/ppermute | solution.py:505
  89.2 1.9 %collective-permute-start.24 = (f32[400,128]{1,0:T(8,128)S(1)}, f32[400,128]{1,0:T(8,128)S(1)}, u32[]{:S(2)}, u32[]{:S(2)}) collective-permute-start(f32[400,128]{1,0:T(8,128)S(1)} %get-tuple-element.82), channel_id=1, source_target_pairs={{0,0},{1,1},{2,2},{3,3},{4,4},{5,5},{6,6},{7,7},{14,8},{15,9},{12,... | collective-permute-start | bytes 614408 | tf_op jit(solution)/shard_map/ppermute | solution.py:505
  91.1 2.8 %collective-permute-done.26.gb_ref = f32[20,8,128]{2,1,0:T(8,128)S(1)} collective-permute-done((f32[20,8,128]{2,1,0:T(8,128)S(1)}, f32[20,8,128]{2,1,0:T(8,128)S(1)}, u32[]{:S(2)}, u32[]{:S(2)}) %collective-permute-start.26) | collective-permute-done | bytes 81952 | tf_op jit(solution)/shard_map/ppermute | solution.py:505
  93.9 0.1 residual.1
  94.0 1.9 %collective-permute-start.27 = (f32[400,128]{1,0:T(8,128)S(1)}, f32[400,128]{1,0:T(8,128)S(1)}, u32[]{:S(2)}, u32[]{:S(2)}) collective-permute-start(f32[400,128]{1,0:T(8,128)S(1)} %residual.1), channel_id=1, source_target_pairs={{0,0},{1,1},{2,2},{3,3},{4,4},{5,5},{6,6},{7,7},{14,8},{15,9},{12,... | collective-permute-start | bytes 614408 | tf_op jit(solution)/shard_map/ppermute | solution.py:505
  96.0 3.3 %collective-permute-done.24.half_ref = f32[400,128]{1,0:T(8,128)S(1)} collective-permute-done((f32[400,128]{1,0:T(8,128)S(1)}, f32[400,128]{1,0:T(8,128)S(1)}, u32[]{:S(2)}, u32[]{:S(2)}) %collective-permute-start.24) | collective-permute-done | bytes 204832 | tf_op jit(solution)/shard_map/ppermute | solution.py:505
  99.3 0.8 reshape.20
  100.1 3.0 %collective-permute-done.27.half_ref = f32[400,128]{1,0:T(8,128)S(1)} collective-permute-done((f32[400,128]{1,0:T(8,128)S(1)}, f32[400,128]{1,0:T(8,128)S(1)}, u32[]{:S(2)}, u32[]{:S(2)}) %collective-permute-start.27) | collective-permute-done | bytes 204832 | tf_op jit(solution)/shard_map/ppermute | solution.py:505
  103.1 0.8 reshape.21
  (20 shorter events, 0.2 us)
Async XLA Ops:
  0.6 1.0 copy-start.1
  1.6 0.7 copy-start
  2.4 10.0 %collective-permute-start.1 = (f32[408,128]{1,0:T(8,128)S(1)}, f32[408,128]{1,0:T(8,128)S(1)}, u32[]{:S(2)}, u32[]{:S(2)}) collective-permute-start(f32[408,128]{1,0:T(8,128)S(1)} %pack.1), channel_id=1, source_target_pairs={{0,128},{1,129},{2,130},{3,131},{4,132},{5,133},{6,134},{7,135},{8... | collective-permute-start | bytes 626696 | tf_op jit(solution)/shard_map/ppermute | solution.py:505
  7.6 9.3 %collective-permute-start = (f32[408,128]{1,0:T(8,128)S(1)}, f32[408,128]{1,0:T(8,128)S(1)}, u32[]{:S(2)}, u32[]{:S(2)}) collective-permute-start(f32[408,128]{1,0:T(8,128)S(1)} %pack.1), channel_id=1, source_target_pairs={{0,0},{1,1},{2,2},{3,3},{4,4},{5,5},{6,6},{7,7},{8,14},{9,15},{10,... | collective-permute-start | bytes 626696 | tf_op jit(solution)/shard_map/ppermute | solution.py:505
  17.1 2.4 %collective-permute-start.2 = (f32[21,8,128]{2,1,0:T(8,128)S(1)}, f32[21,8,128]{2,1,0:T(8,128)S(1)}, u32[]{:S(2)}, u32[]{:S(2)}) collective-permute-start(f32[21,8,128]{2,1,0:T(8,128)S(1)} %get-tuple-element.46), channel_id=1, source_target_pairs={{0,1},{1,0},{2,3},{3,2},{4,5},{5,4},{6,7},{7,6},{14,15},{15,14},{1... | collective-permute-start | bytes 258056 | tf_op jit(solution)/shard_map/ppermute | solution.py:505
  18.6 6.0 %collective-permute-start.3 = (f32[21,8,128]{2,1,0:T(8,128)S(1)}, f32[21,8,128]{2,1,0:T(8,128)S(1)}, u32[]{:S(2)}, u32[]{:S(2)}) collective-permute-start(f32[21,8,128]{2,1,0:T(8,128)S(1)} %get-tuple-element.47), channel_id=1, source_target_pairs={{0,128},{1,2},{2,1},{3,4},{4,3},{5,6},{6,5},{7,14},{14,7},{15,12},... | collective-permute-start | bytes 258056 | tf_op jit(solution)/shard_map/ppermute | solution.py:505
  25.1 1.4 %collective-permute-start.4 = (f32[20,8,128]{2,1,0:T(8,128)S(1)}, f32[20,8,128]{2,1,0:T(8,128)S(1)}, u32[]{:S(2)}, u32[]{:S(2)}) collective-permute-start(f32[20,8,128]{2,1,0:T(8,128)S(1)} %get-tuple-element.52), channel_id=1, source_target_pairs={{0,1},{1,0},{2,3},{3,2},{4,5},{5,4},{6,7},{7,6},{14,15},{15,14},{1... | collective-permute-start | bytes 245768 | tf_op jit(solution)/shard_map/ppermute | solution.py:505
  25.2 6.1 %collective-permute-start.5 = (f32[20,8,128]{2,1,0:T(8,128)S(1)}, f32[20,8,128]{2,1,0:T(8,128)S(1)}, u32[]{:S(2)}, u32[]{:S(2)}) collective-permute-start(f32[20,8,128]{2,1,0:T(8,128)S(1)} %get-tuple-element.53), channel_id=1, source_target_pairs={{0,128},{1,2},{2,1},{3,4},{4,3},{5,6},{6,5},{7,14},{14,7},{15,12},... | collective-permute-start | bytes 245768 | tf_op jit(solution)/shard_map/ppermute | solution.py:505
  31.8 1.4 %collective-permute-start.6 = (f32[25,8,128]{2,1,0:T(8,128)S(1)}, f32[25,8,128]{2,1,0:T(8,128)S(1)}, u32[]{:S(2)}, u32[]{:S(2)}) collective-permute-start(f32[25,8,128]{2,1,0:T(8,128)S(1)} %get-tuple-element.55), channel_id=1, source_target_pairs={{0,1},{1,0},{2,3},{3,2},{4,5},{5,4},{6,7},{7,6},{14,15},{15,14},{1... | collective-permute-start | bytes 307208 | tf_op jit(solution)/shard_map/ppermute | solution.py:505
  33.3 8.2 %collective-permute-start.7 = (f32[30,8,128]{2,1,0:T(8,128)S(1)}, f32[30,8,128]{2,1,0:T(8,128)S(1)}, u32[]{:S(2)}, u32[]{:S(2)}) collective-permute-start(f32[30,8,128]{2,1,0:T(8,128)S(1)} %get-tuple-element.58), channel_id=1, source_target_pairs={{0,128},{1,2},{2,1},{3,4},{4,3},{5,6},{6,5},{7,14},{14,7},{15,12},... | collective-permute-start | bytes 368648 | tf_op jit(solution)/shard_map/ppermute | solution.py:505
  33.4 8.0 %collective-permute-start.9 = (f32[10,8,128]{2,1,0:T(8,128)S(1)}, f32[10,8,128]{2,1,0:T(8,128)S(1)}, u32[]{:S(2)}, u32[]{:S(2)}) collective-permute-start(f32[10,8,128]{2,1,0:T(8,128)S(1)} %get-tuple-element.59.chip_ref), channel_id=1, source_target_pairs={{0,128},{1,6},{2,130},{3,14},{4,132},{5,12},{6,1},{7,10},{14,3},{1... | collective-permute-start | bytes 122888 | tf_op jit(solution)/shard_map/ppermute | solution.py:505
  33.5 8.0 %collective-permute-start.8 = (f32[10,8,128]{2,1,0:T(8,128)S(1)}, f32[10,8,128]{2,1,0:T(8,128)S(1)}, u32[]{:S(2)}, u32[]{:S(2)}) collective-permute-start(f32[10,8,128]{2,1,0:T(8,128)S(1)} %get-tuple-element.59.chip_ref), channel_id=1, source_target_pairs={{0,128},{1,4},{2,130},{3,6},{4,1},{5,14},{6,3},{7,12},{14,5},{15,1... | collective-permute-start | bytes 122888 | tf_op jit(solution)/shard_map/ppermute | solution.py:505
  41.5 2.0 %collective-permute-start.10 = (f32[30,8,128]{2,1,0:T(8,128)S(1)}, f32[30,8,128]{2,1,0:T(8,128)S(1)}, u32[]{:S(2)}, u32[]{:S(2)}) collective-permute-start(f32[30,8,128]{2,1,0:T(8,128)S(1)} %side.2.mine_ref), channel_id=1, source_target_pairs={{0,1},{1,0},{2,3},{3,2},{4,5},{5,4},{6,7},{7,6},{14,15},{15,14},{1... | collective-permute-start | bytes 368648 | tf_op jit(solution)/shard_map/ppermute | solution.py:505
  45.1 3.3 %collective-permute-start.11 = (f32[20,8,128]{2,1,0:T(8,128)S(1)}, f32[20,8,128]{2,1,0:T(8,128)S(1)}, u32[]{:S(2)}, u32[]{:S(2)}) collective-permute-start(f32[20,8,128]{2,1,0:T(8,128)S(1)} %get-tuple-element.62), channel_id=1, source_target_pairs={{0,1},{1,0},{2,3},{3,2},{4,5},{5,4},{6,7},{7,6},{14,15},{15,14},{1... | collective-permute-start | bytes 245768 | tf_op jit(solution)/shard_map/ppermute | solution.py:505
  45.6 6.0 %collective-permute-start.12 = (f32[20,8,128]{2,1,0:T(8,128)S(1)}, f32[20,8,128]{2,1,0:T(8,128)S(1)}, u32[]{:S(2)}, u32[]{:S(2)}) collective-permute-start(f32[20,8,128]{2,1,0:T(8,128)S(1)} %get-tuple-element.63), channel_id=1, source_target_pairs={{0,128},{1,2},{2,1},{3,4},{4,3},{5,6},{6,5},{7,14},{14,7},{15,12},... | collective-permute-start | bytes 245768 | tf_op jit(solution)/shard_map/ppermute | solution.py:505
  52.1 3.0 %collective-permute-start.13 = (f32[20,8,128]{2,1,0:T(8,128)S(1)}, f32[20,8,128]{2,1,0:T(8,128)S(1)}, u32[]{:S(2)}, u32[]{:S(2)}) collective-permute-start(f32[20,8,128]{2,1,0:T(8,128)S(1)} %get-tuple-element.66), channel_id=1, source_target_pairs={{0,1},{1,0},{2,3},{3,2},{4,5},{5,4},{6,7},{7,6},{14,15},{15,14},{1... | collective-permute-start | bytes 245768 | tf_op jit(solution)/shard_map/ppermute | solution.py:505
  52.2 6.2 %collective-permute-start.14 = (f32[20,8,128]{2,1,0:T(8,128)S(1)}, f32[20,8,128]{2,1,0:T(8,128)S(1)}, u32[]{:S(2)}, u32[]{:S(2)}) collective-permute-start(f32[20,8,128]{2,1,0:T(8,128)S(1)} %get-tuple-element.67), channel_id=1, source_target_pairs={{0,128},{1,2},{2,1},{3,4},{4,3},{5,6},{6,5},{7,14},{14,7},{15,12},... | collective-permute-start | bytes 245768 | tf_op jit(solution)/shard_map/ppermute | solution.py:505
  58.8 3.1 %collective-permute-start.15 = (f32[20,8,128]{2,1,0:T(8,128)S(1)}, f32[20,8,128]{2,1,0:T(8,128)S(1)}, u32[]{:S(2)}, u32[]{:S(2)}) collective-permute-start(f32[20,8,128]{2,1,0:T(8,128)S(1)} %get-tuple-element.70), channel_id=1, source_target_pairs={{0,1},{1,0},{2,3},{3,2},{4,5},{5,4},{6,7},{7,6},{14,15},{15,14},{1... | collective-permute-start | bytes 245768 | tf_op jit(solution)/shard_map/ppermute | solution.py:505
  58.9 6.3 %collective-permute-start.16 = (f32[20,8,128]{2,1,0:T(8,128)S(1)}, f32[20,8,128]{2,1,0:T(8,128)S(1)}, u32[]{:S(2)}, u32[]{:S(2)}) collective-permute-start(f32[20,8,128]{2,1,0:T(8,128)S(1)} %get-tuple-element.71), channel_id=1, source_target_pairs={{0,128},{1,2},{2,1},{3,4},{4,3},{5,6},{6,5},{7,14},{14,7},{15,12},... | collective-permute-start | bytes 245768 | tf_op jit(solution)/shard_map/ppermute | solution.py:505
  65.8 1.4 %collective-permute-start.17 = (f32[25,8,128]{2,1,0:T(8,128)S(1)}, f32[25,8,128]{2,1,0:T(8,128)S(1)}, u32[]{:S(2)}, u32[]{:S(2)}) collective-permute-start(f32[25,8,128]{2,1,0:T(8,128)S(1)} %get-tuple-element.73), channel_id=1, source_target_pairs={{0,1},{1,0},{2,3},{3,2},{4,5},{5,4},{6,7},{7,6},{14,15},{15,14},{1... | collective-permute-start | bytes 307208 | tf_op jit(solution)/shard_map/ppermute | solution.py:505
  67.2 10.7 %collective-permute-start.18 = (f32[30,8,128]{2,1,0:T(8,128)S(1)}, f32[30,8,128]{2,1,0:T(8,128)S(1)}, u32[]{:S(2)}, u32[]{:S(2)}) collective-permute-start(f32[30,8,128]{2,1,0:T(8,128)S(1)} %get-tuple-element.76), channel_id=1, source_target_pairs={{0,128},{1,2},{2,1},{3,4},{4,3},{5,6},{6,5},{7,14},{14,7},{15,12},... | collective-permute-start | bytes 368648 | tf_op jit(solution)/shard_map/ppermute | solution.py:505
  70.0 7.9 %collective-permute-start.20 = (f32[10,8,128]{2,1,0:T(8,128)S(1)}, f32[10,8,128]{2,1,0:T(8,128)S(1)}, u32[]{:S(2)}, u32[]{:S(2)}) collective-permute-start(f32[10,8,128]{2,1,0:T(8,128)S(1)} %get-tuple-element.77.chip_ref), channel_id=1, source_target_pairs={{0,128},{1,6},{2,130},{3,14},{4,132},{5,12},{6,1},{7,10},{14,3},{1... | collective-permute-start | bytes 122888 | tf_op jit(solution)/shard_map/ppermute | solution.py:505
  70.0 7.9 %collective-permute-start.19 = (f32[10,8,128]{2,1,0:T(8,128)S(1)}, f32[10,8,128]{2,1,0:T(8,128)S(1)}, u32[]{:S(2)}, u32[]{:S(2)}) collective-permute-start(f32[10,8,128]{2,1,0:T(8,128)S(1)} %get-tuple-element.77.chip_ref), channel_id=1, source_target_pairs={{0,128},{1,4},{2,130},{3,6},{4,1},{5,14},{6,3},{7,12},{14,5},{15,1... | collective-permute-start | bytes 122888 | tf_op jit(solution)/shard_map/ppermute | solution.py:505
  77.9 1.4 %collective-permute-start.21 = (f32[30,8,128]{2,1,0:T(8,128)S(1)}, f32[30,8,128]{2,1,0:T(8,128)S(1)}, u32[]{:S(2)}, u32[]{:S(2)}) collective-permute-start(f32[30,8,128]{2,1,0:T(8,128)S(1)} %side.3.mine_ref), channel_id=1, source_target_pairs={{0,1},{1,0},{2,3},{3,2},{4,5},{5,4},{6,7},{7,6},{14,15},{15,14},{1... | collective-permute-start | bytes 368648 | tf_op jit(solution)/shard_map/ppermute | solution.py:505
  81.0 1.5 %collective-permute-start.22 = (f32[20,8,128]{2,1,0:T(8,128)S(1)}, f32[20,8,128]{2,1,0:T(8,128)S(1)}, u32[]{:S(2)}, u32[]{:S(2)}) collective-permute-start(f32[20,8,128]{2,1,0:T(8,128)S(1)} %get-tuple-element.80), channel_id=1, source_target_pairs={{0,1},{1,0},{2,3},{3,2},{4,5},{5,4},{6,7},{7,6},{14,15},{15,14},{1... | collective-permute-start | bytes 245768 | tf_op jit(solution)/shard_map/ppermute | solution.py:505
  81.3 6.0 %collective-permute-start.23 = (f32[20,8,128]{2,1,0:T(8,128)S(1)}, f32[20,8,128]{2,1,0:T(8,128)S(1)}, u32[]{:S(2)}, u32[]{:S(2)}) collective-permute-start(f32[20,8,128]{2,1,0:T(8,128)S(1)} %get-tuple-element.81), channel_id=1, source_target_pairs={{0,128},{1,2},{2,1},{3,4},{4,3},{5,6},{6,5},{7,14},{14,7},{15,12},... | collective-permute-start | bytes 245768 | tf_op jit(solution)/shard_map/ppermute | solution.py:505
  87.8 3.4 %collective-permute-start.25 = (f32[20,8,128]{2,1,0:T(8,128)S(1)}, f32[20,8,128]{2,1,0:T(8,128)S(1)}, u32[]{:S(2)}, u32[]{:S(2)}) collective-permute-start(f32[20,8,128]{2,1,0:T(8,128)S(1)} %get-tuple-element.84), channel_id=1, source_target_pairs={{0,1},{1,0},{2,3},{3,2},{4,5},{5,4},{6,7},{7,6},{14,15},{15,14},{1... | collective-permute-start | bytes 245768 | tf_op jit(solution)/shard_map/ppermute | solution.py:505
  87.9 6.1 %collective-permute-start.26 = (f32[20,8,128]{2,1,0:T(8,128)S(1)}, f32[20,8,128]{2,1,0:T(8,128)S(1)}, u32[]{:S(2)}, u32[]{:S(2)}) collective-permute-start(f32[20,8,128]{2,1,0:T(8,128)S(1)} %get-tuple-element.85), channel_id=1, source_target_pairs={{0,128},{1,2},{2,1},{3,4},{4,3},{5,6},{6,5},{7,14},{14,7},{15,12},... | collective-permute-start | bytes 245768 | tf_op jit(solution)/shard_map/ppermute | solution.py:505
  89.2 10.1 %collective-permute-start.24 = (f32[400,128]{1,0:T(8,128)S(1)}, f32[400,128]{1,0:T(8,128)S(1)}, u32[]{:S(2)}, u32[]{:S(2)}) collective-permute-start(f32[400,128]{1,0:T(8,128)S(1)} %get-tuple-element.82), channel_id=1, source_target_pairs={{0,0},{1,1},{2,2},{3,3},{4,4},{5,5},{6,6},{7,7},{14,8},{15,9},{12,... | collective-permute-start | bytes 614408 | tf_op jit(solution)/shard_map/ppermute | solution.py:505
  94.0 9.1 %collective-permute-start.27 = (f32[400,128]{1,0:T(8,128)S(1)}, f32[400,128]{1,0:T(8,128)S(1)}, u32[]{:S(2)}, u32[]{:S(2)}) collective-permute-start(f32[400,128]{1,0:T(8,128)S(1)} %residual.1), channel_id=1, source_target_pairs={{0,0},{1,1},{2,2},{3,3},{4,4},{5,5},{6,6},{7,7},{14,8},{15,9},{12,... | collective-permute-start | bytes 614408 | tf_op jit(solution)/shard_map/ppermute | solution.py:505

commit v3 on v2

--- a/solution.py
+++ b/solution.py
@@ -64,6 +64,7 @@
     def __init__(self, marks=None):
         sub = lax.broadcasted_iota(jnp.int32, (8, 128), 0)
         lane = lax.broadcasted_iota(jnp.int32, (8, 128), 1)
+        self.lane = lane
         self.low = sub < 4
         self.top = (sub & 3) == 3
         self.bottom = (sub & 3) == 0
@@ -123,11 +124,16 @@
 
 
 def put_faces(mv, y_ref, a_ref, b_ref, first=0):
+    ends = [jnp.zeros((8, 128), F32)] * 2
     for a in range(4):
-        for c in range(N):
+        for c in range(4):
             low, high = y_ref[at(a, 0, c)], y_ref[at(a, 4, c)]
-            a_ref[first + a * 5 + c] = mv.pick(high, low)
-            b_ref[first + a * 5 + c] = mv.pick(low, high)
+            a_ref[first + a * 4 + c] = mv.pick(high, low)
+            b_ref[first + a * 4 + c] = mv.pick(low, high)
+        for side in range(2):
+            ends[side] = jnp.where(mv.lane == a, pltpu.roll(y_ref[at(a, 4 * side, 4)], a + 1, 1), ends[side])
+    a_ref[first + 16] = mv.pick(ends[1], ends[0])
+    b_ref[first + 16] = mv.pick(ends[0], ends[1])
 
 
 def got_faces(mv, a_ref, b_ref, count, a_first=0, b_first=0):
@@ -137,7 +143,14 @@
         x, y = a_ref[a_first + k], b_ref[b_first + k]
         left.append(mv.pick(y, x) * has_left)
         right.append(mv.pick(x, y) * has_right)
-    return left, right
+    out = []
+    for v in (left, right):
+        rows = []
+        for a in range(4):
+            rows.extend(v[a * 4 : a * 4 + 4])
+            rows.append(pltpu.roll(v[16], 127 - a, 1))
+        out.append(rows + v[17:])
+    return out
 
 
 def inverse_at(inv_ref, a, b, c):
@@ -168,20 +181,32 @@
 
 
 def half_rows(mv, ref, out_ref):
-    for n in range(0, 100, 2):
-        x, y = ref[n], ref[n + 1]
-        x = jnp.where(mv.copy0, x, pltpu.roll(x, 4, 0))
-        y = jnp.where(mv.copy0, pltpu.roll(y, 4, 0), y)
-        out_ref[pl.ds(4 * n, 8)] = jnp.where(mv.low, x, y)
-
-
-def pack_kernel(load_ref, out_ref):
+    def turned(x):
+        return jnp.where(mv.copy0, x, pltpu.roll(x, 4, 0))
+
+    ends = jnp.zeros((8, 128), F32)
+    for k in range(20):
+        for c in (0, 2):
+            x, y = turned(ref[5 * k + c]), turned(ref[5 * k + c + 1])
+            out_ref[pl.ds(16 * k + 4 * c, 8)] = jnp.where(mv.low, x, pltpu.roll(y, 4, 0))
+        ends = jnp.where(mv.lane == k, pltpu.roll(turned(ref[5 * k + 4]), k + 1, 1), ends)
+    out_ref[pl.ds(320, 8)] = ends
+
+
+def pack_kernel(load_ref, out_ref, sum_ref):
     row = lax.broadcasted_iota(jnp.int32, (100, 128), 0)
-    out_ref[pl.ds(0, 100)] = load_ref[pl.ds(0, 100)] + jnp.where((row & 3) == 0, 0.0, load_ref[pl.ds(399, 100)])
-    out_ref[pl.ds(100, 300)] = load_ref[pl.ds(100, 300)]
-    coeff = load_ref[pl.ds(500, 4)]
-    out_ref[pl.ds(400, 4)] = coeff
-    out_ref[pl.ds(404, 4)] = coeff
+    sum_ref[pl.ds(0, 100)] = load_ref[pl.ds(0, 100)] + jnp.where((row & 3) == 0, 0.0, load_ref[pl.ds(399, 100)])
+    sum_ref[pl.ds(100, 404)] = load_ref[pl.ds(100, 404)]
+    row = lax.broadcasted_iota(jnp.int32, (16, 128), 0)
+    lane = lax.broadcasted_iota(jnp.int32, (16, 128), 1)
+    moved = jnp.logical_and(row < 4, lane > 0)
+    ends = jnp.zeros((16, 128), F32)
+    for k in range(20):
+        x = sum_ref[pl.ds(20 * k + 16, 16)]
+        out_ref[pl.ds(16 * k, 16)] = sum_ref[pl.ds(20 * k, 16)] + jnp.where(moved, pltpu.roll(x, 1, 1), 0.0)
+        ends = jnp.where(lane == k, pltpu.roll(x, k + 1, 1), ends)
+    out_ref[pl.ds(320, 4)] = ends[:4]
+    out_ref[pl.ds(324, 4)] = load_ref[pl.ds(500, 4)]
 
 
 def unpack_kernel(marks, same_ref, other_ref, f_ref, coeff_ref, a_ref, b_ref):
@@ -192,21 +217,23 @@
         h0, h1 = jnp.where(mv.copy0, x, y), jnp.where(mv.copy0, y, x)
         return jnp.where(mv.low, h0, pltpu.roll(h1, 4, 0)), jnp.where(mv.low, pltpu.roll(h0, 4, 0), h1)
 
-    for n in range(0, 100, 2):
-        f_ref[n], f_ref[n + 1] = pair(n)
-    coeff, _ = pair(100)
+    ends, coeff = pair(80)
     coeff_ref[...] = coeff
-    for a in range(4):
-        for b in range(N):
-            f_ref[at(a, b, 0)] = f_ref[at(a, b, 0)] + mv.before(f_ref[at(a, b, 4)])
+    joint = jnp.logical_and(mv.lane_first, jnp.logical_not(mv.low))
+    for k in range(20):
+        for c in (0, 2):
+            f_ref[5 * k + c], f_ref[5 * k + c + 1] = pair(4 * k + c)
+        over = pltpu.roll(pltpu.roll(ends, (128 - k) % 128, 1), 4, 0)
+        f_ref[5 * k] = f_ref[5 * k] + jnp.where(joint, over, 0.0)
+        f_ref[5 * k + 4] = pltpu.roll(ends, 127 - k, 1)
     put_faces(mv, f_ref, a_ref, b_ref)
-    a_ref[20] = coeff
-    b_ref[20] = coeff
+    a_ref[17] = coeff
+    b_ref[17] = coeff
 
 
 def first_kernel(marks, part_ref, coeff_ref, ga_ref, gb_ref, u_ref, y_ref, f_ref, inv_ref, a_ref, b_ref, acc_ref, up_ref):
     mv = Moves(marks)
-    left, right = got_faces(mv, ga_ref, gb_ref, 21)
+    left, right = got_faces(mv, ga_ref, gb_ref, 18)
     coeff = coeff_ref[...]
     for kind_b, value in enumerate((coeff + left[20], coeff, coeff + right[20])):
         for kind_a, v in enumerate((value + mv.below(value), value)):
@@ -230,7 +257,7 @@
 
 def sweep_kernel(marks, u_ref, y_ref, f_ref, inv_ref, coeff_ref, ga_ref, gb_ref, un_ref, yn_ref, a_ref, b_ref, acc_ref, up_ref):
     mv = Moves(marks)
-    left, right = got_faces(mv, ga_ref, gb_ref, 20)
+    left, right = got_faces(mv, ga_ref, gb_ref, 17)
     smooth(mv, u_ref, f_ref, y_ref, left, right, inv_ref, un_ref)
     apply_operator(mv, un_ref, coeff_ref[...], yn_ref, acc_ref, up_ref)
     put_faces(mv, yn_ref, a_ref, b_ref)
@@ -243,7 +270,7 @@
 
 def restrict_kernel(marks, u_ref, y_ref, f_ref, inv_ref, coeff_ref, ga_ref, gb_ref, part_ref, un_ref, own_ref, a_ref, b_ref, yn_ref, acc_ref, up_ref):
     mv = Moves(marks)
-    left, right = got_faces(mv, ga_ref, gb_ref, 20)
+    left, right = got_faces(mv, ga_ref, gb_ref, 17)
     smooth(mv, u_ref, f_ref, y_ref, left, right, inv_ref, un_ref)
     apply_operator(mv, un_ref, coeff_ref[...], yn_ref, acc_ref, up_ref)
     put_faces(mv, yn_ref, a_ref, b_ref, 5)
@@ -278,7 +305,7 @@
         chip_ref[5 + k] = high
         near_ref[k] = low
         near_ref[5 + k] = high
-    for k in range(20):
+    for k in range(17):
         near_ref[10 + k] = b_ref[5 + k]
 
 
@@ -416,7 +443,7 @@
                     v = float(INTERP[b, 0]) * low[a][c] + float(INTERP[b, 1]) * high[a][c]
                 ua_ref[at(a, b, c)] = u_ref[at(a, b, c)] + v
     apply_operator(mv, ua_ref, coeff, ya_ref, acc_ref, up_ref)
-    left, right = got_faces(mv, ga_ref, near_ref, 20, 5, 10)
+    left, right = got_faces(mv, ga_ref, near_ref, 17, 5, 10)
     left = [left[k] + face_ref[k] for k in range(20)]
     right = [right[k] + face_ref[20 + k] for k in range(20)]
     smooth(mv, ua_ref, f_ref, ya_ref, left, right, inv_ref, un_ref)
@@ -426,7 +453,7 @@
 
 def residual_kernel(marks, y_ref, f_ref, ga_ref, gb_ref, half_ref, r_ref):
     mv = Moves(marks)
-    left, right = got_faces(mv, ga_ref, gb_ref, 20)
+    left, right = got_faces(mv, ga_ref, gb_ref, 17)
     for a in range(4):
         for b in range(N):
             r = residual_row(mv, f_ref, y_ref, left, right, a, b)
@@ -437,9 +464,14 @@
 
 
 def spread_kernel(half_ref, out_ref):
-    out_ref[pl.ds(0, 400)] = half_ref[...]
+    lane = lax.broadcasted_iota(jnp.int32, (8, 128), 1)
+    ends = half_ref[pl.ds(320, 8)]
+    for k in range(20):
+        out_ref[pl.ds(20 * k, 16)] = half_ref[pl.ds(16 * k, 16)]
+        last = jnp.where(lane == 127, pltpu.roll(ends, 127 - k, 1), pltpu.roll(half_ref[pl.ds(16 * k, 8)], 127, 1))
+        out_ref[pl.ds(20 * k + 16, 4)] = last[:4]
     row = lax.broadcasted_iota(jnp.int32, (100, 128), 0)
-    out_ref[pl.ds(400, 100)] = jnp.where((row & 3) == 3, 0.0, half_ref[pl.ds(1, 100)])
+    out_ref[pl.ds(400, 100)] = jnp.where((row & 3) == 3, 0.0, out_ref[pl.ds(1, 100)])
 
 
 VM = pl.BlockSpec(memory_space=pltpu.VMEM)
@@ -459,17 +491,14 @@
     )(*args)
 
 
-MODE = "flip"
-
-
 def placement(sizes):
     _, ey, lin = sizes
     place = list(range(ey * lin))
-    if lin == 64 and MODE == "flip":
-        for s in range(ey * lin):
-            z, y, core = s // 8 % 8, s // 2 % 4, s % 2
-            if z % 2:
-                place[s] = s - y * 2 + (3 - y) * 2
+    if lin == 64:
+        for s in place[:]:
+            side, p, y, core = s // 64, s // 8 % 8, s // 2 % 4, s % 2
+            z = (p - side) % 8
+            place[s] = side * 64 + z * 8 + (3 - y if p % 2 else y) * 2 + core
     return place
 
 
@@ -512,10 +541,10 @@
         marks = jnp.broadcast_to(marks[:, None, None], (4 + WIN, 8, 128))
         coeff = kappa * jnp.where(wet == 1, 1.0, 0.05).astype(F32)
         packed = jnp.concatenate([load.reshape(500, 1, 128), coeff.reshape(4, 1, 128)]).reshape(504, 128)
-        (packed,) = call("pack", pack_kernel, [(408, 128)], [], packed)
+        (packed,) = call("pack", pack_kernel, [(328, 128)], [(504, 128)], packed)
         same, other = packed if place == sorted(place) else swap(packed, to_same), swap(packed, to_other)
-        part, coeff, a, b = call("unpack", unpack_kernel, [FIELD, (8, 128), (21, 8, 128), (21, 8, 128)], [], marks, same, other)
-        faces = [(20, 8, 128), (20, 8, 128)]
+        part, coeff, a, b = call("unpack", unpack_kernel, [FIELD, (8, 128), (18, 8, 128), (18, 8, 128)], [], marks, same, other)
+        faces = [(17, 8, 128), (17, 8, 128)]
 
         def trade(a, b):
             return swap(a, within), swap(b, beyond[1])
@@ -529,9 +558,9 @@
 
         def sweep_and_correct(u, y, a, b):
             a, b = trade(a, b)
-            u, own, a, b = call("restrict", restrict_kernel, [FIELD, (5, 8, 128), (25, 8, 128), (25, 8, 128)], [FIELD, *WORK], marks, u, y, f, inv, coeff, a, b, part)
+            u, own, a, b = call("restrict", restrict_kernel, [FIELD, (5, 8, 128), (22, 8, 128), (22, 8, 128)], [FIELD, *WORK], marks, u, y, f, inv, coeff, a, b, part)
             a = swap(a, within)
-            chip, near = call("chip", chip_kernel, [(10, 8, 128), (30, 8, 128)], [], marks, own, a, b)
+            chip, near = call("chip", chip_kernel, [(10, 8, 128), (27, 8, 128)], [], marks, own, a, b)
             near, second, third = swap(near, beyond[1]), swap(chip, beyond[2]), swap(chip, beyond[3])
             (mine,) = call("side", side_kernel, [(30, 8, 128)], [], near, second, third)
             theirs = swap(mine, within)
@@ -542,10 +571,10 @@
         u, y, a, b = sweep(u, y, a, b)
         u, y, a, b = sweep_and_correct(u, y, a, b)
         a, b = trade(a, b)
-        y, a, b, half = call("last", last_sweep_kernel, [FIELD, *faces, (400, 128)], [FIELD, *WORK], marks, u, y, f, inv, coeff, a, b)
+        y, a, b, half = call("last", last_sweep_kernel, [FIELD, *faces, (328, 128)], [FIELD, *WORK], marks, u, y, f, inv, coeff, a, b)
         a, b = trade(a, b)
         half = restore(half)
-        (left_half,) = call("residual", residual_kernel, [(400, 128)], [FIELD], marks, y, f, a, b)
+        (left_half,) = call("residual", residual_kernel, [(328, 128)], [FIELD], marks, y, f, a, b)
         (solved,) = call("spread", spread_kernel, [(500, 128)], [], half)
         (rest,) = call("spread", spread_kernel, [(500, 128)], [], restore(left_half))
         return solved.reshape(load.shape), rest.reshape(load.shape)

time: 104 us -> 95.9 us (0.922)
  the two profiles are of different devices: /device:TPU:225 before, /device:TPU:2 now
where the time goes in v3:
time: 95.9 us; the launch traced here: 94.7 us
  starting transfers between devices  42.2 us (44%)
  waiting for transfers between devices  40.6 us (42%)
  Pallas kernels  7.1 us (7%)
  local copies, waits for them, and re-layouts  3.95 us (4%)
    ppermute x28, starting transfers between devices, swap(): return lax.ppermute(x, AXES, pairs)  42.2 us
    ppermute x28, waiting for transfers between devices, swap(): return lax.ppermute(x, AXES, pairs)  40.6 us
    pallas_call x17, Pallas kernels, call(): pl.pallas_call(kernel, out_shape=[jax.ShapeDtypeStruct(s, F32) for s in o...  7.1 us
  transfers between devices with their start and end apart: 28, of which 20 were waited for; matrix products, arithmetic and copies ran while one was open for 2% of the time, Pallas kernels for 0%

profile of v3, /device:TPU:2, one launch (start us, length us, event | category | flops | bytes accessed | tf_op | source)
XLA Modules:
  0.0 94.7 jit_solution(348978338055325101)
XLA Ops:
  0.6 1.0 %copy.12 = f32[500,1,128]{2,0,1:T(8,128)S(1)} copy(f32[500,1,128]{2,1,0:T(1,128)} %bitcast.9) | data formatting | bytes 512000 | tf_op jit(solution)/shard_map/reshape | solution.py:543
  1.6 0.7 copy-done
  2.3 0.1 pack.1
  2.5 7.5 %collective-permute-start.1 = (f32[328,128]{1,0:T(8,128)S(1)}, f32[328,128]{1,0:T(8,128)S(1)}, u32[]{:S(2)}, u32[]{:S(2)}) collective-permute-start(f32[328,128]{1,0:T(8,128)S(1)} %pack.1), channel_id=1, source_target_pairs={{0,128},{1,129},{2,130},{3,131},{4,132},{5,133},{6,134},{7,135},{8... | collective-permute-start | bytes 503816 | tf_op jit(solution)/shard_map/ppermute | solution.py:534
  9.9 5.4 %collective-permute-start = (f32[328,128]{1,0:T(8,128)S(1)}, f32[328,128]{1,0:T(8,128)S(1)}, u32[]{:S(2)}, u32[]{:S(2)}) collective-permute-start(f32[328,128]{1,0:T(8,128)S(1)} %pack.1), channel_id=1, source_target_pairs={{0,0},{1,1},{2,2},{3,3},{4,4},{5,5},{6,6},{7,7},{8,14},{9,15},{10,... | collective-permute-start | bytes 503816 | tf_op jit(solution)/shard_map/ppermute | solution.py:534
  15.3 0.7 dynamic-slice_bitcast_fusion
  16.0 3.7 %collective-permute-done.same_ref = f32[328,128]{1,0:T(8,128)S(1)} collective-permute-done((f32[328,128]{1,0:T(8,128)S(1)}, f32[328,128]{1,0:T(8,128)S(1)}, u32[]{:S(2)}, u32[]{:S(2)}) %collective-permute-start) | collective-permute-done | bytes 167968 | tf_op jit(solution)/shard_map/ppermute | solution.py:534
  19.7 0.1 broadcast_in_dim.17.marks
  19.8 0.2 unpack.1
  20.0 0.5 collective-permute-start.3
  20.4 0.8 collective-permute-done.2.ga_ref
  21.2 2.6 %collective-permute-done.3.gb_ref = f32[18,8,128]{2,1,0:T(8,128)S(1)} collective-permute-done((f32[18,8,128]{2,1,0:T(8,128)S(1)}, f32[18,8,128]{2,1,0:T(8,128)S(1)}, u32[]{:S(2)}, u32[]{:S(2)}) %collective-permute-start.3) | collective-permute-done | bytes 73760 | tf_op jit(solution)/shard_map/ppermute | solution.py:534
  23.8 0.5 first.1
  24.4 0.5 collective-permute-start.4
  24.8 0.1 collective-permute-start.5
  24.9 0.8 collective-permute-done.4.ga_ref
  25.8 2.8 %collective-permute-done.5.gb_ref = f32[17,8,128]{2,1,0:T(8,128)S(1)} collective-permute-done((f32[17,8,128]{2,1,0:T(8,128)S(1)}, f32[17,8,128]{2,1,0:T(8,128)S(1)}, u32[]{:S(2)}, u32[]{:S(2)}) %collective-permute-start.5) | collective-permute-done | bytes 69664 | tf_op jit(solution)/shard_map/ppermute | solution.py:534
  28.6 0.6 restrict.2
  29.1 0.2 collective-permute-start.6
  29.3 1.2 %collective-permute-done.6.ga_ref = f32[22,8,128]{2,1,0:T(8,128)S(1)} collective-permute-done((f32[22,8,128]{2,1,0:T(8,128)S(1)}, f32[22,8,128]{2,1,0:T(8,128)S(1)}, u32[]{:S(2)}, u32[]{:S(2)}) %collective-permute-start.6) | collective-permute-done | bytes 90144 | tf_op jit(solution)/shard_map/ppermute | solution.py:534
  30.5 0.5 collective-permute-start.7
  31.0 4.6 %collective-permute-start.9 = (f32[10,8,128]{2,1,0:T(8,128)S(1)}, f32[10,8,128]{2,1,0:T(8,128)S(1)}, u32[]{:S(2)}, u32[]{:S(2)}) collective-permute-start(f32[10,8,128]{2,1,0:T(8,128)S(1)} %get-tuple-element.59.chip_ref), channel_id=1, source_target_pairs={{0,128},{1,6},{2,130},{3,14},{4,132},{5,12},{6,1},{7,10},{14,3},{1... | collective-permute-start | bytes 122888 | tf_op jit(solution)/shard_map/ppermute | solution.py:534
  35.6 1.7 %collective-permute-done.9.third_ref = f32[10,8,128]{2,1,0:T(8,128)S(1)} collective-permute-done((f32[10,8,128]{2,1,0:T(8,128)S(1)}, f32[10,8,128]{2,1,0:T(8,128)S(1)}, u32[]{:S(2)}, u32[]{:S(2)}) %collective-permute-start.9) | collective-permute-done | bytes 40992 | tf_op jit(solution)/shard_map/ppermute | solution.py:534
  37.3 3.2 %collective-permute-done.8.second_ref = f32[10,8,128]{2,1,0:T(8,128)S(1)} collective-permute-done((f32[10,8,128]{2,1,0:T(8,128)S(1)}, f32[10,8,128]{2,1,0:T(8,128)S(1)}, u32[]{:S(2)}, u32[]{:S(2)}) %collective-permute-start.8) | collective-permute-done | bytes 40992 | tf_op jit(solution)/shard_map/ppermute | solution.py:534
  40.6 0.1 collective-permute-start.10
  40.7 1.3 %collective-permute-done.10.other_ref = f32[30,8,128]{2,1,0:T(8,128)S(1)} collective-permute-done((f32[30,8,128]{2,1,0:T(8,128)S(1)}, f32[30,8,128]{2,1,0:T(8,128)S(1)}, u32[]{:S(2)}, u32[]{:S(2)}) %collective-permute-start.10) | collective-permute-done | bytes 122912 | tf_op jit(solution)/shard_map/ppermute | solution.py:534
  42.0 1.6 %correct.2 = (f32[100,8,128]{2,1,0:T(8,128)S(1)}, f32[100,8,128]{2,1,0:T(8,128)S(1)}, f32[17,8,128]{2,1,0:T(8,128)S(1)}, f32[17,8,128]{2,1,0:T(8,128)S(1)}) custom-call(f32[18,8,128]{2,1,0:T(8,128)S(1)} %broadcast_in_dim.17.marks, f32[100,8,128]{2,1,0:T(8,128)S(1)} %get-tuple-element.54.u_ref, f32[100,8,128]{2,1,0:T(8,128)S(1)} %get-tuple-element.50.f_ref, ...), custom_call_target="tpu_custom_call" | custom-call | tf_op jit(solution)/shard_map/correct/pallas_call | solution.py:483
  43.6 0.2 collective-permute-start.11
  43.8 3.4 %collective-permute-start.12 = (f32[17,8,128]{2,1,0:T(8,128)S(1)}, f32[17,8,128]{2,1,0:T(8,128)S(1)}, u32[]{:S(2)}, u32[]{:S(2)}) collective-permute-start(f32[17,8,128]{2,1,0:T(8,128)S(1)} %get-tuple-element.63), channel_id=1, source_target_pairs={{0,128},{1,2},{2,1},{3,4},{4,3},{5,6},{6,5},{7,14},{14,7},{15,12},... | collective-permute-start | bytes 208904 | tf_op jit(solution)/shard_map/ppermute | solution.py:534
  47.2 2.0 %collective-permute-done.12.gb_ref = f32[17,8,128]{2,1,0:T(8,128)S(1)} collective-permute-done((f32[17,8,128]{2,1,0:T(8,128)S(1)}, f32[17,8,128]{2,1,0:T(8,128)S(1)}, u32[]{:S(2)}, u32[]{:S(2)}) %collective-permute-start.12) | collective-permute-done | bytes 69664 | tf_op jit(solution)/shard_map/ppermute | solution.py:534
  49.2 0.5 sweep.2
  49.7 0.1 collective-permute-start.13
  49.8 1.9 %collective-permute-start.14 = (f32[17,8,128]{2,1,0:T(8,128)S(1)}, f32[17,8,128]{2,1,0:T(8,128)S(1)}, u32[]{:S(2)}, u32[]{:S(2)}) collective-permute-start(f32[17,8,128]{2,1,0:T(8,128)S(1)} %get-tuple-element.67), channel_id=1, source_target_pairs={{0,128},{1,2},{2,1},{3,4},{4,3},{5,6},{6,5},{7,14},{14,7},{15,12},... | collective-permute-start | bytes 208904 | tf_op jit(solution)/shard_map/ppermute | solution.py:534
  51.7 2.0 %collective-permute-done.14.gb_ref = f32[17,8,128]{2,1,0:T(8,128)S(1)} collective-permute-done((f32[17,8,128]{2,1,0:T(8,128)S(1)}, f32[17,8,128]{2,1,0:T(8,128)S(1)}, u32[]{:S(2)}, u32[]{:S(2)}) %collective-permute-start.14) | collective-permute-done | bytes 69664 | tf_op jit(solution)/shard_map/ppermute | solution.py:534
  53.6 0.5 sweep.3
  54.1 0.6 collective-permute-start.15
  54.8 1.7 %collective-permute-start.16 = (f32[17,8,128]{2,1,0:T(8,128)S(1)}, f32[17,8,128]{2,1,0:T(8,128)S(1)}, u32[]{:S(2)}, u32[]{:S(2)}) collective-permute-start(f32[17,8,128]{2,1,0:T(8,128)S(1)} %get-tuple-element.71), channel_id=1, source_target_pairs={{0,128},{1,2},{2,1},{3,4},{4,3},{5,6},{6,5},{7,14},{14,7},{15,12},... | collective-permute-start | bytes 208904 | tf_op jit(solution)/shard_map/ppermute | solution.py:534
  56.5 2.0 %collective-permute-done.16.gb_ref = f32[17,8,128]{2,1,0:T(8,128)S(1)} collective-permute-done((f32[17,8,128]{2,1,0:T(8,128)S(1)}, f32[17,8,128]{2,1,0:T(8,128)S(1)}, u32[]{:S(2)}, u32[]{:S(2)}) %collective-permute-start.16) | collective-permute-done | bytes 69664 | tf_op jit(solution)/shard_map/ppermute | solution.py:534
  58.5 0.6 restrict.3
  59.0 0.2 collective-permute-start.17
  59.3 1.1 %collective-permute-done.17.ga_ref = f32[22,8,128]{2,1,0:T(8,128)S(1)} collective-permute-done((f32[22,8,128]{2,1,0:T(8,128)S(1)}, f32[22,8,128]{2,1,0:T(8,128)S(1)}, u32[]{:S(2)}, u32[]{:S(2)}) %collective-permute-start.17) | collective-permute-done | bytes 90144 | tf_op jit(solution)/shard_map/ppermute | solution.py:534
  60.4 1.8 %collective-permute-start.18 = (f32[27,8,128]{2,1,0:T(8,128)S(1)}, f32[27,8,128]{2,1,0:T(8,128)S(1)}, u32[]{:S(2)}, u32[]{:S(2)}) collective-permute-start(f32[27,8,128]{2,1,0:T(8,128)S(1)} %get-tuple-element.76), channel_id=1, source_target_pairs={{0,128},{1,2},{2,1},{3,4},{4,3},{5,6},{6,5},{7,14},{14,7},{15,12},... | collective-permute-start | bytes 331784 | tf_op jit(solution)/shard_map/ppermute | solution.py:534
  62.3 3.3 %collective-permute-start.20 = (f32[10,8,128]{2,1,0:T(8,128)S(1)}, f32[10,8,128]{2,1,0:T(8,128)S(1)}, u32[]{:S(2)}, u32[]{:S(2)}) collective-permute-start(f32[10,8,128]{2,1,0:T(8,128)S(1)} %get-tuple-element.77.chip_ref), channel_id=1, source_target_pairs={{0,128},{1,6},{2,130},{3,14},{4,132},{5,12},{6,1},{7,10},{14,3},{1... | collective-permute-start | bytes 122888 | tf_op jit(solution)/shard_map/ppermute | solution.py:534
  65.6 1.7 %collective-permute-done.20.third_ref = f32[10,8,128]{2,1,0:T(8,128)S(1)} collective-permute-done((f32[10,8,128]{2,1,0:T(8,128)S(1)}, f32[10,8,128]{2,1,0:T(8,128)S(1)}, u32[]{:S(2)}, u32[]{:S(2)}) %collective-permute-start.20) | collective-permute-done | bytes 40992 | tf_op jit(solution)/shard_map/ppermute | solution.py:534
  67.3 3.2 %collective-permute-done.19.second_ref = f32[10,8,128]{2,1,0:T(8,128)S(1)} collective-permute-done((f32[10,8,128]{2,1,0:T(8,128)S(1)}, f32[10,8,128]{2,1,0:T(8,128)S(1)}, u32[]{:S(2)}, u32[]{:S(2)}) %collective-permute-start.19) | collective-permute-done | bytes 40992 | tf_op jit(solution)/shard_map/ppermute | solution.py:534
  70.5 0.1 collective-permute-start.21
  70.6 1.3 %collective-permute-done.21.other_ref = f32[30,8,128]{2,1,0:T(8,128)S(1)} collective-permute-done((f32[30,8,128]{2,1,0:T(8,128)S(1)}, f32[30,8,128]{2,1,0:T(8,128)S(1)}, u32[]{:S(2)}, u32[]{:S(2)}) %collective-permute-start.21) | collective-permute-done | bytes 122912 | tf_op jit(solution)/shard_map/ppermute | solution.py:534
  71.9 1.6 %correct.3 = (f32[100,8,128]{2,1,0:T(8,128)S(1)}, f32[100,8,128]{2,1,0:T(8,128)S(1)}, f32[17,8,128]{2,1,0:T(8,128)S(1)}, f32[17,8,128]{2,1,0:T(8,128)S(1)}) custom-call(f32[18,8,128]{2,1,0:T(8,128)S(1)} %broadcast_in_dim.17.marks, f32[100,8,128]{2,1,0:T(8,128)S(1)} %get-tuple-element.72.u_ref, f32[100,8,128]{2,1,0:T(8,128)S(1)} %get-tuple-element.50.f_ref, ...), custom_call_target="tpu_custom_call" | custom-call | tf_op jit(solution)/shard_map/correct/pallas_call | solution.py:483
  73.6 0.2 collective-permute-start.22
  73.8 3.5 %collective-permute-start.23 = (f32[17,8,128]{2,1,0:T(8,128)S(1)}, f32[17,8,128]{2,1,0:T(8,128)S(1)}, u32[]{:S(2)}, u32[]{:S(2)}) collective-permute-start(f32[17,8,128]{2,1,0:T(8,128)S(1)} %get-tuple-element.81), channel_id=1, source_target_pairs={{0,128},{1,2},{2,1},{3,4},{4,3},{5,6},{6,5},{7,14},{14,7},{15,12},... | collective-permute-start | bytes 208904 | tf_op jit(solution)/shard_map/ppermute | solution.py:534
  77.3 2.0 %collective-permute-done.23.gb_ref = f32[17,8,128]{2,1,0:T(8,128)S(1)} collective-permute-done((f32[17,8,128]{2,1,0:T(8,128)S(1)}, f32[17,8,128]{2,1,0:T(8,128)S(1)}, u32[]{:S(2)}, u32[]{:S(2)}) %collective-permute-start.23) | collective-permute-done | bytes 69664 | tf_op jit(solution)/shard_map/ppermute | solution.py:534
  79.3 0.5 last.1
  79.8 0.1 collective-permute-start.25
  79.9 1.9 %collective-permute-start.26 = (f32[17,8,128]{2,1,0:T(8,128)S(1)}, f32[17,8,128]{2,1,0:T(8,128)S(1)}, u32[]{:S(2)}, u32[]{:S(2)}) collective-permute-start(f32[17,8,128]{2,1,0:T(8,128)S(1)} %get-tuple-element.85), channel_id=1, source_target_pairs={{0,128},{1,2},{2,1},{3,4},{4,3},{5,6},{6,5},{7,14},{14,7},{15,12},... | collective-permute-start | bytes 208904 | tf_op jit(solution)/shard_map/ppermute | solution.py:534
  81.8 1.9 %collective-permute-start.24 = (f32[328,128]{1,0:T(8,128)S(1)}, f32[328,128]{1,0:T(8,128)S(1)}, u32[]{:S(2)}, u32[]{:S(2)}) collective-permute-start(f32[328,128]{1,0:T(8,128)S(1)} %get-tuple-element.82), channel_id=1, source_target_pairs={{0,0},{1,1},{2,2},{3,3},{4,4},{5,5},{6,6},{7,7},{14,8},{15,9},{12,... | collective-permute-start | bytes 503816 | tf_op jit(solution)/shard_map/ppermute | solution.py:534
  83.7 0.1 collective-permute-done.26.gb_ref
  83.8 0.2 residual.1
  84.0 1.9 %collective-permute-start.27 = (f32[328,128]{1,0:T(8,128)S(1)}, f32[328,128]{1,0:T(8,128)S(1)}, u32[]{:S(2)}, u32[]{:S(2)}) collective-permute-start(f32[328,128]{1,0:T(8,128)S(1)} %residual.1), channel_id=1, source_target_pairs={{0,0},{1,1},{2,2},{3,3},{4,4},{5,5},{6,6},{7,7},{14,8},{15,9},{12,... | collective-permute-start | bytes 503816 | tf_op jit(solution)/shard_map/ppermute | solution.py:534
  85.9 4.4 %collective-permute-done.24.half_ref = f32[328,128]{1,0:T(8,128)S(1)} collective-permute-done((f32[328,128]{1,0:T(8,128)S(1)}, f32[328,128]{1,0:T(8,128)S(1)}, u32[]{:S(2)}, u32[]{:S(2)}) %collective-permute-start.24) | collective-permute-done | bytes 167968 | tf_op jit(solution)/shard_map/ppermute | solution.py:534
  90.4 0.1 spread.2
  90.5 0.8 reshape.20
  91.3 2.6 %collective-permute-done.27.half_ref = f32[328,128]{1,0:T(8,128)S(1)} collective-permute-done((f32[328,128]{1,0:T(8,128)S(1)}, f32[328,128]{1,0:T(8,128)S(1)}, u32[]{:S(2)}, u32[]{:S(2)}) %collective-permute-start.27) | collective-permute-done | bytes 167968 | tf_op jit(solution)/shard_map/ppermute | solution.py:534
  93.9 0.1 spread.3
  94.0 0.8 reshape.21
  (20 shorter events, 0.2 us)
Async XLA Ops:
  0.6 1.0 %copy-start.1 = (s32[4,1,128]{2,1,0:T(1,128)S(1)}, s32[4,1,128]{2,1,0:T(1,128)}, u32[]{:S(2)}) copy-start(s32[4,1,128]{2,1,0:T(1,128)} %param.6) | copy-start | bytes 6148
  1.6 0.7 copy-start
  2.5 13.6 %collective-permute-start.1 = (f32[328,128]{1,0:T(8,128)S(1)}, f32[328,128]{1,0:T(8,128)S(1)}, u32[]{:S(2)}, u32[]{:S(2)}) collective-permute-start(f32[328,128]{1,0:T(8,128)S(1)} %pack.1), channel_id=1, source_target_pairs={{0,128},{1,129},{2,130},{3,131},{4,132},{5,133},{6,134},{7,135},{8... | collective-permute-start | bytes 503816 | tf_op jit(solution)/shard_map/ppermute | solution.py:534
  9.9 9.7 %collective-permute-start = (f32[328,128]{1,0:T(8,128)S(1)}, f32[328,128]{1,0:T(8,128)S(1)}, u32[]{:S(2)}, u32[]{:S(2)}) collective-permute-start(f32[328,128]{1,0:T(8,128)S(1)} %pack.1), channel_id=1, source_target_pairs={{0,0},{1,1},{2,2},{3,3},{4,4},{5,5},{6,6},{7,7},{8,14},{9,15},{10,... | collective-permute-start | bytes 503816 | tf_op jit(solution)/shard_map/ppermute | solution.py:534
  19.9 1.3 %collective-permute-start.2 = (f32[18,8,128]{2,1,0:T(8,128)S(1)}, f32[18,8,128]{2,1,0:T(8,128)S(1)}, u32[]{:S(2)}, u32[]{:S(2)}) collective-permute-start(f32[18,8,128]{2,1,0:T(8,128)S(1)} %get-tuple-element.46), channel_id=1, source_target_pairs={{0,1},{1,0},{2,3},{3,2},{4,5},{5,4},{6,7},{7,6},{14,15},{15,14},{1... | collective-permute-start | bytes 221192 | tf_op jit(solution)/shard_map/ppermute | solution.py:534
  20.0 3.9 %collective-permute-start.3 = (f32[18,8,128]{2,1,0:T(8,128)S(1)}, f32[18,8,128]{2,1,0:T(8,128)S(1)}, u32[]{:S(2)}, u32[]{:S(2)}) collective-permute-start(f32[18,8,128]{2,1,0:T(8,128)S(1)} %get-tuple-element.47), channel_id=1, source_target_pairs={{0,128},{1,2},{2,1},{3,4},{4,3},{5,6},{6,5},{7,14},{14,7},{15,12},... | collective-permute-start | bytes 221192 | tf_op jit(solution)/shard_map/ppermute | solution.py:534
  24.4 1.4 %collective-permute-start.4 = (f32[17,8,128]{2,1,0:T(8,128)S(1)}, f32[17,8,128]{2,1,0:T(8,128)S(1)}, u32[]{:S(2)}, u32[]{:S(2)}) collective-permute-start(f32[17,8,128]{2,1,0:T(8,128)S(1)} %get-tuple-element.52), channel_id=1, source_target_pairs={{0,1},{1,0},{2,3},{3,2},{4,5},{5,4},{6,7},{7,6},{14,15},{15,14},{1... | collective-permute-start | bytes 208904 | tf_op jit(solution)/shard_map/ppermute | solution.py:534
  24.8 3.7 %collective-permute-start.5 = (f32[17,8,128]{2,1,0:T(8,128)S(1)}, f32[17,8,128]{2,1,0:T(8,128)S(1)}, u32[]{:S(2)}, u32[]{:S(2)}) collective-permute-start(f32[17,8,128]{2,1,0:T(8,128)S(1)} %get-tuple-element.53), channel_id=1, source_target_pairs={{0,128},{1,2},{2,1},{3,4},{4,3},{5,6},{6,5},{7,14},{14,7},{15,12},... | collective-permute-start | bytes 208904 | tf_op jit(solution)/shard_map/ppermute | solution.py:534
  29.1 1.4 %collective-permute-start.6 = (f32[22,8,128]{2,1,0:T(8,128)S(1)}, f32[22,8,128]{2,1,0:T(8,128)S(1)}, u32[]{:S(2)}, u32[]{:S(2)}) collective-permute-start(f32[22,8,128]{2,1,0:T(8,128)S(1)} %get-tuple-element.55), channel_id=1, source_target_pairs={{0,1},{1,0},{2,3},{3,2},{4,5},{5,4},{6,7},{7,6},{14,15},{15,14},{1... | collective-permute-start | bytes 270344 | tf_op jit(solution)/shard_map/ppermute | solution.py:534
  30.5 10.0 %collective-permute-start.7 = (f32[27,8,128]{2,1,0:T(8,128)S(1)}, f32[27,8,128]{2,1,0:T(8,128)S(1)}, u32[]{:S(2)}, u32[]{:S(2)}) collective-permute-start(f32[27,8,128]{2,1,0:T(8,128)S(1)} %get-tuple-element.58), channel_id=1, source_target_pairs={{0,128},{1,2},{2,1},{3,4},{4,3},{5,6},{6,5},{7,14},{14,7},{15,12},... | collective-permute-start | bytes 331784 | tf_op jit(solution)/shard_map/ppermute | solution.py:534
  31.0 6.3 %collective-permute-start.9 = (f32[10,8,128]{2,1,0:T(8,128)S(1)}, f32[10,8,128]{2,1,0:T(8,128)S(1)}, u32[]{:S(2)}, u32[]{:S(2)}) collective-permute-start(f32[10,8,128]{2,1,0:T(8,128)S(1)} %get-tuple-element.59.chip_ref), channel_id=1, source_target_pairs={{0,128},{1,6},{2,130},{3,14},{4,132},{5,12},{6,1},{7,10},{14,3},{1... | collective-permute-start | bytes 122888 | tf_op jit(solution)/shard_map/ppermute | solution.py:534
  35.6 4.9 %collective-permute-start.8 = (f32[10,8,128]{2,1,0:T(8,128)S(1)}, f32[10,8,128]{2,1,0:T(8,128)S(1)}, u32[]{:S(2)}, u32[]{:S(2)}) collective-permute-start(f32[10,8,128]{2,1,0:T(8,128)S(1)} %get-tuple-element.59.chip_ref), channel_id=1, source_target_pairs={{0,128},{1,4},{2,130},{3,6},{4,1},{5,14},{6,3},{7,12},{14,5},{15,1... | collective-permute-start | bytes 122888 | tf_op jit(solution)/shard_map/ppermute | solution.py:534
  40.6 1.4 %collective-permute-start.10 = (f32[30,8,128]{2,1,0:T(8,128)S(1)}, f32[30,8,128]{2,1,0:T(8,128)S(1)}, u32[]{:S(2)}, u32[]{:S(2)}) collective-permute-start(f32[30,8,128]{2,1,0:T(8,128)S(1)} %side.2.mine_ref), channel_id=1, source_target_pairs={{0,1},{1,0},{2,3},{3,2},{4,5},{5,4},{6,7},{7,6},{14,15},{15,14},{1... | collective-permute-start | bytes 368648 | tf_op jit(solution)/shard_map/ppermute | solution.py:534
  43.6 3.6 %collective-permute-start.11 = (f32[17,8,128]{2,1,0:T(8,128)S(1)}, f32[17,8,128]{2,1,0:T(8,128)S(1)}, u32[]{:S(2)}, u32[]{:S(2)}) collective-permute-start(f32[17,8,128]{2,1,0:T(8,128)S(1)} %get-tuple-element.62), channel_id=1, source_target_pairs={{0,1},{1,0},{2,3},{3,2},{4,5},{5,4},{6,7},{7,6},{14,15},{15,14},{1... | collective-permute-start | bytes 208904 | tf_op jit(solution)/shard_map/ppermute | solution.py:534
  43.8 5.3 %collective-permute-start.12 = (f32[17,8,128]{2,1,0:T(8,128)S(1)}, f32[17,8,128]{2,1,0:T(8,128)S(1)}, u32[]{:S(2)}, u32[]{:S(2)}) collective-permute-start(f32[17,8,128]{2,1,0:T(8,128)S(1)} %get-tuple-element.63), channel_id=1, source_target_pairs={{0,128},{1,2},{2,1},{3,4},{4,3},{5,6},{6,5},{7,14},{14,7},{15,12},... | collective-permute-start | bytes 208904 | tf_op jit(solution)/shard_map/ppermute | solution.py:534
  49.7 2.0 %collective-permute-start.13 = (f32[17,8,128]{2,1,0:T(8,128)S(1)}, f32[17,8,128]{2,1,0:T(8,128)S(1)}, u32[]{:S(2)}, u32[]{:S(2)}) collective-permute-start(f32[17,8,128]{2,1,0:T(8,128)S(1)} %get-tuple-element.66), channel_id=1, source_target_pairs={{0,1},{1,0},{2,3},{3,2},{4,5},{5,4},{6,7},{7,6},{14,15},{15,14},{1... | collective-permute-start | bytes 208904 | tf_op jit(solution)/shard_map/ppermute | solution.py:534
  49.8 3.9 %collective-permute-start.14 = (f32[17,8,128]{2,1,0:T(8,128)S(1)}, f32[17,8,128]{2,1,0:T(8,128)S(1)}, u32[]{:S(2)}, u32[]{:S(2)}) collective-permute-start(f32[17,8,128]{2,1,0:T(8,128)S(1)} %get-tuple-element.67), channel_id=1, source_target_pairs={{0,128},{1,2},{2,1},{3,4},{4,3},{5,6},{6,5},{7,14},{14,7},{15,12},... | collective-permute-start | bytes 208904 | tf_op jit(solution)/shard_map/ppermute | solution.py:534
  54.1 2.4 %collective-permute-start.15 = (f32[17,8,128]{2,1,0:T(8,128)S(1)}, f32[17,8,128]{2,1,0:T(8,128)S(1)}, u32[]{:S(2)}, u32[]{:S(2)}) collective-permute-start(f32[17,8,128]{2,1,0:T(8,128)S(1)} %get-tuple-element.70), channel_id=1, source_target_pairs={{0,1},{1,0},{2,3},{3,2},{4,5},{5,4},{6,7},{7,6},{14,15},{15,14},{1... | collective-permute-start | bytes 208904 | tf_op jit(solution)/shard_map/ppermute | solution.py:534
  54.8 3.7 %collective-permute-start.16 = (f32[17,8,128]{2,1,0:T(8,128)S(1)}, f32[17,8,128]{2,1,0:T(8,128)S(1)}, u32[]{:S(2)}, u32[]{:S(2)}) collective-permute-start(f32[17,8,128]{2,1,0:T(8,128)S(1)} %get-tuple-element.71), channel_id=1, source_target_pairs={{0,128},{1,2},{2,1},{3,4},{4,3},{5,6},{6,5},{7,14},{14,7},{15,12},... | collective-permute-start | bytes 208904 | tf_op jit(solution)/shard_map/ppermute | solution.py:534
  59.0 1.4 %collective-permute-start.17 = (f32[22,8,128]{2,1,0:T(8,128)S(1)}, f32[22,8,128]{2,1,0:T(8,128)S(1)}, u32[]{:S(2)}, u32[]{:S(2)}) collective-permute-start(f32[22,8,128]{2,1,0:T(8,128)S(1)} %get-tuple-element.73), channel_id=1, source_target_pairs={{0,1},{1,0},{2,3},{3,2},{4,5},{5,4},{6,7},{7,6},{14,15},{15,14},{1... | collective-permute-start | bytes 270344 | tf_op jit(solution)/shard_map/ppermute | solution.py:534
  60.4 10.1 %collective-permute-start.18 = (f32[27,8,128]{2,1,0:T(8,128)S(1)}, f32[27,8,128]{2,1,0:T(8,128)S(1)}, u32[]{:S(2)}, u32[]{:S(2)}) collective-permute-start(f32[27,8,128]{2,1,0:T(8,128)S(1)} %get-tuple-element.76), channel_id=1, source_target_pairs={{0,128},{1,2},{2,1},{3,4},{4,3},{5,6},{6,5},{7,14},{14,7},{15,12},... | collective-permute-start | bytes 331784 | tf_op jit(solution)/shard_map/ppermute | solution.py:534
  62.3 5.0 %collective-permute-start.20 = (f32[10,8,128]{2,1,0:T(8,128)S(1)}, f32[10,8,128]{2,1,0:T(8,128)S(1)}, u32[]{:S(2)}, u32[]{:S(2)}) collective-permute-start(f32[10,8,128]{2,1,0:T(8,128)S(1)} %get-tuple-element.77.chip_ref), channel_id=1, source_target_pairs={{0,128},{1,6},{2,130},{3,14},{4,132},{5,12},{6,1},{7,10},{14,3},{1... | collective-permute-start | bytes 122888 | tf_op jit(solution)/shard_map/ppermute | solution.py:534
  65.6 4.9 %collective-permute-start.19 = (f32[10,8,128]{2,1,0:T(8,128)S(1)}, f32[10,8,128]{2,1,0:T(8,128)S(1)}, u32[]{:S(2)}, u32[]{:S(2)}) collective-permute-start(f32[10,8,128]{2,1,0:T(8,128)S(1)} %get-tuple-element.77.chip_ref), channel_id=1, source_target_pairs={{0,128},{1,4},{2,130},{3,6},{4,1},{5,14},{6,3},{7,12},{14,5},{15,1... | collective-permute-start | bytes 122888 | tf_op jit(solution)/shard_map/ppermute | solution.py:534
  70.5 1.4 %collective-permute-start.21 = (f32[30,8,128]{2,1,0:T(8,128)S(1)}, f32[30,8,128]{2,1,0:T(8,128)S(1)}, u32[]{:S(2)}, u32[]{:S(2)}) collective-permute-start(f32[30,8,128]{2,1,0:T(8,128)S(1)} %side.3.mine_ref), channel_id=1, source_target_pairs={{0,1},{1,0},{2,3},{3,2},{4,5},{5,4},{6,7},{7,6},{14,15},{15,14},{1... | collective-permute-start | bytes 368648 | tf_op jit(solution)/shard_map/ppermute | solution.py:534
  73.6 3.7 %collective-permute-start.22 = (f32[17,8,128]{2,1,0:T(8,128)S(1)}, f32[17,8,128]{2,1,0:T(8,128)S(1)}, u32[]{:S(2)}, u32[]{:S(2)}) collective-permute-start(f32[17,8,128]{2,1,0:T(8,128)S(1)} %get-tuple-element.80), channel_id=1, source_target_pairs={{0,1},{1,0},{2,3},{3,2},{4,5},{5,4},{6,7},{7,6},{14,15},{15,14},{1... | collective-permute-start | bytes 208904 | tf_op jit(solution)/shard_map/ppermute | solution.py:534
  73.8 5.5 %collective-permute-start.23 = (f32[17,8,128]{2,1,0:T(8,128)S(1)}, f32[17,8,128]{2,1,0:T(8,128)S(1)}, u32[]{:S(2)}, u32[]{:S(2)}) collective-permute-start(f32[17,8,128]{2,1,0:T(8,128)S(1)} %get-tuple-element.81), channel_id=1, source_target_pairs={{0,128},{1,2},{2,1},{3,4},{4,3},{5,6},{6,5},{7,14},{14,7},{15,12},... | collective-permute-start | bytes 208904 | tf_op jit(solution)/shard_map/ppermute | solution.py:534
  79.8 3.9 %collective-permute-start.25 = (f32[17,8,128]{2,1,0:T(8,128)S(1)}, f32[17,8,128]{2,1,0:T(8,128)S(1)}, u32[]{:S(2)}, u32[]{:S(2)}) collective-permute-start(f32[17,8,128]{2,1,0:T(8,128)S(1)} %get-tuple-element.84), channel_id=1, source_target_pairs={{0,1},{1,0},{2,3},{3,2},{4,5},{5,4},{6,7},{7,6},{14,15},{15,14},{1... | collective-permute-start | bytes 208904 | tf_op jit(solution)/shard_map/ppermute | solution.py:534
  79.9 3.9 %collective-permute-start.26 = (f32[17,8,128]{2,1,0:T(8,128)S(1)}, f32[17,8,128]{2,1,0:T(8,128)S(1)}, u32[]{:S(2)}, u32[]{:S(2)}) collective-permute-start(f32[17,8,128]{2,1,0:T(8,128)S(1)} %get-tuple-element.85), channel_id=1, source_target_pairs={{0,128},{1,2},{2,1},{3,4},{4,3},{5,6},{6,5},{7,14},{14,7},{15,12},... | collective-permute-start | bytes 208904 | tf_op jit(solution)/shard_map/ppermute | solution.py:534
  81.8 8.6 %collective-permute-start.24 = (f32[328,128]{1,0:T(8,128)S(1)}, f32[328,128]{1,0:T(8,128)S(1)}, u32[]{:S(2)}, u32[]{:S(2)}) collective-permute-start(f32[328,128]{1,0:T(8,128)S(1)} %get-tuple-element.82), channel_id=1, source_target_pairs={{0,0},{1,1},{2,2},{3,3},{4,4},{5,5},{6,6},{7,7},{14,8},{15,9},{12,... | collective-permute-start | bytes 503816 | tf_op jit(solution)/shard_map/ppermute | solution.py:534
  84.0 9.8 %collective-permute-start.27 = (f32[328,128]{1,0:T(8,128)S(1)}, f32[328,128]{1,0:T(8,128)S(1)}, u32[]{:S(2)}, u32[]{:S(2)}) collective-permute-start(f32[328,128]{1,0:T(8,128)S(1)} %residual.1), channel_id=1, source_target_pairs={{0,0},{1,1},{2,2},{3,3},{4,4},{5,5},{6,6},{7,7},{14,8},{15,9},{12,... | collective-permute-start | bytes 503816 | tf_op jit(solution)/shard_map/ppermute | solution.py:534

commit v4 on v3

--- a/solution.py
+++ b/solution.py
@@ -268,7 +268,7 @@
     half_rows(Moves(marks), un_ref, half_ref)
 
 
-def restrict_kernel(marks, u_ref, y_ref, f_ref, inv_ref, coeff_ref, ga_ref, gb_ref, part_ref, un_ref, own_ref, a_ref, b_ref, yn_ref, acc_ref, up_ref):
+def restrict_kernel(marks, u_ref, y_ref, f_ref, inv_ref, coeff_ref, ga_ref, gb_ref, part_ref, un_ref, yn_ref, own_ref, a_ref, b_ref, acc_ref, up_ref):
     mv = Moves(marks)
     left, right = got_faces(mv, ga_ref, gb_ref, 17)
     smooth(mv, u_ref, f_ref, y_ref, left, right, inv_ref, un_ref)
@@ -423,7 +423,40 @@
     return out
 
 
-def correct_kernel(marks, u_ref, f_ref, inv_ref, coeff_ref, ga_ref, near_ref, chip_ref, mine_ref, other_ref, un_ref, yn_ref, a_ref, b_ref, ua_ref, ya_ref, face_ref, acc_ref, up_ref):
+def add_correction(mv, low, high, coeff, u_ref, y_ref, ua_ref, ya_ref):
+    half = coeff * 0.5
+    found = {}
+
+    def v(a, b, c):
+        if (a, b, c) not in found:
+            lo, hi = low[a][c], high[a][c]
+            found[a, b, c] = lo if b == 0 else hi if b == 4 else float(INTERP[b, 0]) * lo + float(INTERP[b, 1]) * hi
+        return found[a, b, c]
+
+    def share(a, b, c):
+        parts = []
+        if a in (0, 4):
+            parts.append((v(a, b, c) - v(4 - a, b, c)) * weight(b, c))
+        if b in (0, 4):
+            parts.append((v(a, b, c) - v(a, 4 - b, c)) * weight(a, c))
+        if c in (0, 4):
+            parts.append((v(a, b, c) - v(a, b, 4 - c)) * weight(a, b))
+        return sum(parts[1:], parts[0]) * half if parts else None
+
+    for a in range(4):
+        for b in range(N):
+            row = [share(a, b, c) for c in range(N)]
+            if a == 0:
+                for c in range(N):
+                    under = share(4, b, c)
+                    row[c] = row[c] + mv.below(under)
+            row[0] = row[0] + mv.before(row[4])
+            for c in range(N):
+                ua_ref[at(a, b, c)] = u_ref[at(a, b, c)] + v(a, b, c)
+                ya_ref[at(a, b, c)] = y_ref[at(a, b, c)] if row[c] is None else y_ref[at(a, b, c)] + row[c]
+
+
+def correct_kernel(marks, u_ref, y_ref, f_ref, inv_ref, coeff_ref, ga_ref, near_ref, chip_ref, mine_ref, other_ref, un_ref, yn_ref, a_ref, b_ref, ua_ref, ya_ref, face_ref, acc_ref, up_ref):
     mv = Moves(marks)
     coeff = coeff_ref[...]
     lines, coeff_left, coeff_right = coarse_solve(mv, chip_ref, mine_ref, other_ref)
@@ -431,18 +464,8 @@
         face_ref[k] = v
     for k, v in enumerate(neighbour_face(mv, lines[2], lines[3], coeff_right)):
         face_ref[20 + k] = v
-    low, high = nodal(mv, lines[1], 4), nodal(mv, lines[2], 4)
-    for a in range(4):
-        for b in range(N):
-            for c in range(N):
-                if b == 0:
-                    v = low[a][c]
-                elif b == 4:
-                    v = high[a][c]
-                else:
-                    v = float(INTERP[b, 0]) * low[a][c] + float(INTERP[b, 1]) * high[a][c]
-                ua_ref[at(a, b, c)] = u_ref[at(a, b, c)] + v
-    apply_operator(mv, ua_ref, coeff, ya_ref, acc_ref, up_ref)
+    low, high = nodal(mv, lines[1], N), nodal(mv, lines[2], N)
+    add_correction(mv, low, high, coeff, u_ref, y_ref, ua_ref, ya_ref)
     left, right = got_faces(mv, ga_ref, near_ref, 17, 5, 10)
     left = [left[k] + face_ref[k] for k in range(20)]
     right = [right[k] + face_ref[20 + k] for k in range(20)]
@@ -558,13 +581,13 @@
 
         def sweep_and_correct(u, y, a, b):
             a, b = trade(a, b)
-            u, own, a, b = call("restrict", restrict_kernel, [FIELD, (5, 8, 128), (22, 8, 128), (22, 8, 128)], [FIELD, *WORK], marks, u, y, f, inv, coeff, a, b, part)
+            u, y, own, a, b = call("restrict", restrict_kernel, [FIELD, FIELD, (5, 8, 128), (22, 8, 128), (22, 8, 128)], WORK, marks, u, y, f, inv, coeff, a, b, part)
             a = swap(a, within)
             chip, near = call("chip", chip_kernel, [(10, 8, 128), (27, 8, 128)], [], marks, own, a, b)
             near, second, third = swap(near, beyond[1]), swap(chip, beyond[2]), swap(chip, beyond[3])
             (mine,) = call("side", side_kernel, [(30, 8, 128)], [], near, second, third)
             theirs = swap(mine, within)
-            return call("correct", correct_kernel, [FIELD, FIELD, *faces], [FIELD, FIELD, (40, 8, 128), *WORK], marks, u, f, inv, coeff, a, near, chip, mine, theirs)
+            return call("correct", correct_kernel, [FIELD, FIELD, *faces], [FIELD, FIELD, (40, 8, 128), *WORK], marks, u, y, f, inv, coeff, a, near, chip, mine, theirs)
 
         u, y, a, b = sweep_and_correct(u, y, a, b)
         u, y, a, b = sweep(u, y, a, b)

time: 95.9 us -> 95.4 us (level)
  no operation moved by 1% of the time
where the time goes in v4:
time: 95.4 us; the launch traced here: 94.2 us
  starting transfers between devices  42.4 us (44%)
  waiting for transfers between devices  40.5 us (42%)
  Pallas kernels  6.59 us (7%)
  local copies, waits for them, and re-layouts  3.95 us (4%)
    ppermute x28, starting transfers between devices, swap(): return lax.ppermute(x, AXES, pairs)  42.4 us
    ppermute x28, waiting for transfers between devices, swap(): return lax.ppermute(x, AXES, pairs)  40.5 us
    pallas_call x17, Pallas kernels, call(): pl.pallas_call(kernel, out_shape=[jax.ShapeDtypeStruct(s, F32) for s in o...  6.59 us
  transfers between devices with their start and end apart: 28, of which 20 were waited for; matrix products, arithmetic and copies ran while one was open for 2% of the time, Pallas kernels for 0%

profile of v4, /device:TPU:2, one launch (start us, length us, event | category | flops | bytes accessed | tf_op | source)
XLA Modules:
  0.0 94.2 jit_solution(1610663915486342877)
XLA Ops:
  0.6 1.0 %copy.12 = f32[500,1,128]{2,0,1:T(8,128)S(1)} copy(f32[500,1,128]{2,1,0:T(1,128)} %bitcast.9) | data formatting | bytes 512000 | tf_op jit(solution)/shard_map/reshape | solution.py:566
  1.6 0.7 copy-done
  2.3 0.1 pack.1
  2.5 7.5 %collective-permute-start.1 = (f32[328,128]{1,0:T(8,128)S(1)}, f32[328,128]{1,0:T(8,128)S(1)}, u32[]{:S(2)}, u32[]{:S(2)}) collective-permute-start(f32[328,128]{1,0:T(8,128)S(1)} %pack.1), channel_id=1, source_target_pairs={{0,128},{1,129},{2,130},{3,131},{4,132},{5,133},{6,134},{7,135},{8... | collective-permute-start | bytes 503816 | tf_op jit(solution)/shard_map/ppermute | solution.py:557
  9.9 5.4 %collective-permute-start = (f32[328,128]{1,0:T(8,128)S(1)}, f32[328,128]{1,0:T(8,128)S(1)}, u32[]{:S(2)}, u32[]{:S(2)}) collective-permute-start(f32[328,128]{1,0:T(8,128)S(1)} %pack.1), channel_id=1, source_target_pairs={{0,0},{1,1},{2,2},{3,3},{4,4},{5,5},{6,6},{7,7},{8,14},{9,15},{10,... | collective-permute-start | bytes 503816 | tf_op jit(solution)/shard_map/ppermute | solution.py:557
  15.3 0.7 dynamic-slice_bitcast_fusion
  16.0 3.7 %collective-permute-done.same_ref = f32[328,128]{1,0:T(8,128)S(1)} collective-permute-done((f32[328,128]{1,0:T(8,128)S(1)}, f32[328,128]{1,0:T(8,128)S(1)}, u32[]{:S(2)}, u32[]{:S(2)}) %collective-permute-start) | collective-permute-done | bytes 167968 | tf_op jit(solution)/shard_map/ppermute | solution.py:557
  19.7 0.1 broadcast_in_dim.17.marks
  19.8 0.2 unpack.1
  20.0 0.5 collective-permute-start.3
  20.4 0.8 collective-permute-done.2.ga_ref
  21.2 2.6 %collective-permute-done.3.gb_ref = f32[18,8,128]{2,1,0:T(8,128)S(1)} collective-permute-done((f32[18,8,128]{2,1,0:T(8,128)S(1)}, f32[18,8,128]{2,1,0:T(8,128)S(1)}, u32[]{:S(2)}, u32[]{:S(2)}) %collective-permute-start.3) | collective-permute-done | bytes 73760 | tf_op jit(solution)/shard_map/ppermute | solution.py:557
  23.8 0.5 first.1
  24.3 0.5 collective-permute-start.4
  24.8 0.1 collective-permute-start.5
  24.9 0.8 collective-permute-done.4.ga_ref
  25.8 2.8 %collective-permute-done.5.gb_ref = f32[17,8,128]{2,1,0:T(8,128)S(1)} collective-permute-done((f32[17,8,128]{2,1,0:T(8,128)S(1)}, f32[17,8,128]{2,1,0:T(8,128)S(1)}, u32[]{:S(2)}, u32[]{:S(2)}) %collective-permute-start.5) | collective-permute-done | bytes 69664 | tf_op jit(solution)/shard_map/ppermute | solution.py:557
  28.6 0.5 restrict.2
  29.1 0.2 collective-permute-start.6
  29.3 1.2 %collective-permute-done.6.ga_ref = f32[22,8,128]{2,1,0:T(8,128)S(1)} collective-permute-done((f32[22,8,128]{2,1,0:T(8,128)S(1)}, f32[22,8,128]{2,1,0:T(8,128)S(1)}, u32[]{:S(2)}, u32[]{:S(2)}) %collective-permute-start.6) | collective-permute-done | bytes 90144 | tf_op jit(solution)/shard_map/ppermute | solution.py:557
  30.5 0.5 collective-permute-start.7
  31.0 4.6 %collective-permute-start.9 = (f32[10,8,128]{2,1,0:T(8,128)S(1)}, f32[10,8,128]{2,1,0:T(8,128)S(1)}, u32[]{:S(2)}, u32[]{:S(2)}) collective-permute-start(f32[10,8,128]{2,1,0:T(8,128)S(1)} %get-tuple-element.62.chip_ref), channel_id=1, source_target_pairs={{0,128},{1,6},{2,130},{3,14},{4,132},{5,12},{6,1},{7,10},{14,3},{1... | collective-permute-start | bytes 122888 | tf_op jit(solution)/shard_map/ppermute | solution.py:557
  35.6 1.7 %collective-permute-done.9.third_ref = f32[10,8,128]{2,1,0:T(8,128)S(1)} collective-permute-done((f32[10,8,128]{2,1,0:T(8,128)S(1)}, f32[10,8,128]{2,1,0:T(8,128)S(1)}, u32[]{:S(2)}, u32[]{:S(2)}) %collective-permute-start.9) | collective-permute-done | bytes 40992 | tf_op jit(solution)/shard_map/ppermute | solution.py:557
  37.3 3.2 %collective-permute-done.8.second_ref = f32[10,8,128]{2,1,0:T(8,128)S(1)} collective-permute-done((f32[10,8,128]{2,1,0:T(8,128)S(1)}, f32[10,8,128]{2,1,0:T(8,128)S(1)}, u32[]{:S(2)}, u32[]{:S(2)}) %collective-permute-start.8) | collective-permute-done | bytes 40992 | tf_op jit(solution)/shard_map/ppermute | solution.py:557
  40.5 0.1 collective-permute-start.10
  40.6 1.3 %collective-permute-done.10.other_ref = f32[30,8,128]{2,1,0:T(8,128)S(1)} collective-permute-done((f32[30,8,128]{2,1,0:T(8,128)S(1)}, f32[30,8,128]{2,1,0:T(8,128)S(1)}, u32[]{:S(2)}, u32[]{:S(2)}) %collective-permute-start.10) | collective-permute-done | bytes 122912 | tf_op jit(solution)/shard_map/ppermute | solution.py:557
  42.0 1.4 %correct.2 = (f32[100,8,128]{2,1,0:T(8,128)S(1)}, f32[100,8,128]{2,1,0:T(8,128)S(1)}, f32[17,8,128]{2,1,0:T(8,128)S(1)}, f32[17,8,128]{2,1,0:T(8,128)S(1)}) custom-call(f32[18,8,128]{2,1,0:T(8,128)S(1)} %broadcast_in_dim.17.marks, f32[100,8,128]{2,1,0:T(8,128)S(1)} %get-tuple-element.56.u_ref, f32[100,8,128]{2,1,0:T(8,128)S(1)} %get-tuple-element.57.y_ref, ...), custom_call_target="tpu_custom_call" | custom-call | tf_op jit(solution)/shard_map/correct/pallas_call | solution.py:506
  43.3 0.2 collective-permute-start.11
  43.6 3.4 %collective-permute-start.12 = (f32[17,8,128]{2,1,0:T(8,128)S(1)}, f32[17,8,128]{2,1,0:T(8,128)S(1)}, u32[]{:S(2)}, u32[]{:S(2)}) collective-permute-start(f32[17,8,128]{2,1,0:T(8,128)S(1)} %get-tuple-element.66), channel_id=1, source_target_pairs={{0,128},{1,2},{2,1},{3,4},{4,3},{5,6},{6,5},{7,14},{14,7},{15,12},... | collective-permute-start | bytes 208904 | tf_op jit(solution)/shard_map/ppermute | solution.py:557
  46.9 2.0 %collective-permute-done.12.gb_ref = f32[17,8,128]{2,1,0:T(8,128)S(1)} collective-permute-done((f32[17,8,128]{2,1,0:T(8,128)S(1)}, f32[17,8,128]{2,1,0:T(8,128)S(1)}, u32[]{:S(2)}, u32[]{:S(2)}) %collective-permute-start.12) | collective-permute-done | bytes 69664 | tf_op jit(solution)/shard_map/ppermute | solution.py:557
  48.9 0.5 sweep.2
  49.4 0.1 collective-permute-start.13
  49.5 1.9 %collective-permute-start.14 = (f32[17,8,128]{2,1,0:T(8,128)S(1)}, f32[17,8,128]{2,1,0:T(8,128)S(1)}, u32[]{:S(2)}, u32[]{:S(2)}) collective-permute-start(f32[17,8,128]{2,1,0:T(8,128)S(1)} %get-tuple-element.70), channel_id=1, source_target_pairs={{0,128},{1,2},{2,1},{3,4},{4,3},{5,6},{6,5},{7,14},{14,7},{15,12},... | collective-permute-start | bytes 208904 | tf_op jit(solution)/shard_map/ppermute | solution.py:557
  51.4 2.0 %collective-permute-done.14.gb_ref = f32[17,8,128]{2,1,0:T(8,128)S(1)} collective-permute-done((f32[17,8,128]{2,1,0:T(8,128)S(1)}, f32[17,8,128]{2,1,0:T(8,128)S(1)}, u32[]{:S(2)}, u32[]{:S(2)}) %collective-permute-start.14) | collective-permute-done | bytes 69664 | tf_op jit(solution)/shard_map/ppermute | solution.py:557
  53.4 0.5 sweep.3
  53.9 0.4 collective-permute-start.15
  54.3 1.7 %collective-permute-start.16 = (f32[17,8,128]{2,1,0:T(8,128)S(1)}, f32[17,8,128]{2,1,0:T(8,128)S(1)}, u32[]{:S(2)}, u32[]{:S(2)}) collective-permute-start(f32[17,8,128]{2,1,0:T(8,128)S(1)} %get-tuple-element.74), channel_id=1, source_target_pairs={{0,128},{1,2},{2,1},{3,4},{4,3},{5,6},{6,5},{7,14},{14,7},{15,12},... | collective-permute-start | bytes 208904 | tf_op jit(solution)/shard_map/ppermute | solution.py:557
  56.1 2.0 %collective-permute-done.16.gb_ref = f32[17,8,128]{2,1,0:T(8,128)S(1)} collective-permute-done((f32[17,8,128]{2,1,0:T(8,128)S(1)}, f32[17,8,128]{2,1,0:T(8,128)S(1)}, u32[]{:S(2)}, u32[]{:S(2)}) %collective-permute-start.16) | collective-permute-done | bytes 69664 | tf_op jit(solution)/shard_map/ppermute | solution.py:557
  58.1 0.6 restrict.3
  58.6 0.4 collective-permute-start.17
  59.0 1.0 %collective-permute-done.17.ga_ref = f32[22,8,128]{2,1,0:T(8,128)S(1)} collective-permute-done((f32[22,8,128]{2,1,0:T(8,128)S(1)}, f32[22,8,128]{2,1,0:T(8,128)S(1)}, u32[]{:S(2)}, u32[]{:S(2)}) %collective-permute-start.17) | collective-permute-done | bytes 90144 | tf_op jit(solution)/shard_map/ppermute | solution.py:557
  60.0 1.8 %collective-permute-start.18 = (f32[27,8,128]{2,1,0:T(8,128)S(1)}, f32[27,8,128]{2,1,0:T(8,128)S(1)}, u32[]{:S(2)}, u32[]{:S(2)}) collective-permute-start(f32[27,8,128]{2,1,0:T(8,128)S(1)} %get-tuple-element.80), channel_id=1, source_target_pairs={{0,128},{1,2},{2,1},{3,4},{4,3},{5,6},{6,5},{7,14},{14,7},{15,12},... | collective-permute-start | bytes 331784 | tf_op jit(solution)/shard_map/ppermute | solution.py:557
  61.8 3.5 %collective-permute-start.20 = (f32[10,8,128]{2,1,0:T(8,128)S(1)}, f32[10,8,128]{2,1,0:T(8,128)S(1)}, u32[]{:S(2)}, u32[]{:S(2)}) collective-permute-start(f32[10,8,128]{2,1,0:T(8,128)S(1)} %get-tuple-element.81.chip_ref), channel_id=1, source_target_pairs={{0,128},{1,6},{2,130},{3,14},{4,132},{5,12},{6,1},{7,10},{14,3},{1... | collective-permute-start | bytes 122888 | tf_op jit(solution)/shard_map/ppermute | solution.py:557
  65.3 1.7 %collective-permute-done.20.third_ref = f32[10,8,128]{2,1,0:T(8,128)S(1)} collective-permute-done((f32[10,8,128]{2,1,0:T(8,128)S(1)}, f32[10,8,128]{2,1,0:T(8,128)S(1)}, u32[]{:S(2)}, u32[]{:S(2)}) %collective-permute-start.20) | collective-permute-done | bytes 40992 | tf_op jit(solution)/shard_map/ppermute | solution.py:557
  67.0 3.2 %collective-permute-done.19.second_ref = f32[10,8,128]{2,1,0:T(8,128)S(1)} collective-permute-done((f32[10,8,128]{2,1,0:T(8,128)S(1)}, f32[10,8,128]{2,1,0:T(8,128)S(1)}, u32[]{:S(2)}, u32[]{:S(2)}) %collective-permute-start.19) | collective-permute-done | bytes 40992 | tf_op jit(solution)/shard_map/ppermute | solution.py:557
  70.3 0.1 collective-permute-start.21
  70.4 1.3 %collective-permute-done.21.other_ref = f32[30,8,128]{2,1,0:T(8,128)S(1)} collective-permute-done((f32[30,8,128]{2,1,0:T(8,128)S(1)}, f32[30,8,128]{2,1,0:T(8,128)S(1)}, u32[]{:S(2)}, u32[]{:S(2)}) %collective-permute-start.21) | collective-permute-done | bytes 122912 | tf_op jit(solution)/shard_map/ppermute | solution.py:557
  71.7 1.4 %correct.3 = (f32[100,8,128]{2,1,0:T(8,128)S(1)}, f32[100,8,128]{2,1,0:T(8,128)S(1)}, f32[17,8,128]{2,1,0:T(8,128)S(1)}, f32[17,8,128]{2,1,0:T(8,128)S(1)}) custom-call(f32[18,8,128]{2,1,0:T(8,128)S(1)} %broadcast_in_dim.17.marks, f32[100,8,128]{2,1,0:T(8,128)S(1)} %get-tuple-element.75.u_ref, f32[100,8,128]{2,1,0:T(8,128)S(1)} %get-tuple-element.76.y_ref, ...), custom_call_target="tpu_custom_call" | custom-call | tf_op jit(solution)/shard_map/correct/pallas_call | solution.py:506
  73.1 0.2 collective-permute-start.22
  73.3 3.5 %collective-permute-start.23 = (f32[17,8,128]{2,1,0:T(8,128)S(1)}, f32[17,8,128]{2,1,0:T(8,128)S(1)}, u32[]{:S(2)}, u32[]{:S(2)}) collective-permute-start(f32[17,8,128]{2,1,0:T(8,128)S(1)} %get-tuple-element.85), channel_id=1, source_target_pairs={{0,128},{1,2},{2,1},{3,4},{4,3},{5,6},{6,5},{7,14},{14,7},{15,12},... | collective-permute-start | bytes 208904 | tf_op jit(solution)/shard_map/ppermute | solution.py:557
  76.8 2.0 %collective-permute-done.23.gb_ref = f32[17,8,128]{2,1,0:T(8,128)S(1)} collective-permute-done((f32[17,8,128]{2,1,0:T(8,128)S(1)}, f32[17,8,128]{2,1,0:T(8,128)S(1)}, u32[]{:S(2)}, u32[]{:S(2)}) %collective-permute-start.23) | collective-permute-done | bytes 69664 | tf_op jit(solution)/shard_map/ppermute | solution.py:557
  78.8 0.5 last.1
  79.3 0.1 collective-permute-start.25
  79.4 1.9 %collective-permute-start.26 = (f32[17,8,128]{2,1,0:T(8,128)S(1)}, f32[17,8,128]{2,1,0:T(8,128)S(1)}, u32[]{:S(2)}, u32[]{:S(2)}) collective-permute-start(f32[17,8,128]{2,1,0:T(8,128)S(1)} %get-tuple-element.89), channel_id=1, source_target_pairs={{0,128},{1,2},{2,1},{3,4},{4,3},{5,6},{6,5},{7,14},{14,7},{15,12},... | collective-permute-start | bytes 208904 | tf_op jit(solution)/shard_map/ppermute | solution.py:557
  81.3 1.9 %collective-permute-start.24 = (f32[328,128]{1,0:T(8,128)S(1)}, f32[328,128]{1,0:T(8,128)S(1)}, u32[]{:S(2)}, u32[]{:S(2)}) collective-permute-start(f32[328,128]{1,0:T(8,128)S(1)} %get-tuple-element.86), channel_id=1, source_target_pairs={{0,0},{1,1},{2,2},{3,3},{4,4},{5,5},{6,6},{7,7},{14,8},{15,9},{12,... | collective-permute-start | bytes 503816 | tf_op jit(solution)/shard_map/ppermute | solution.py:557
  83.2 0.1 collective-permute-done.26.gb_ref
  83.3 0.2 residual.1
  83.5 1.9 %collective-permute-start.27 = (f32[328,128]{1,0:T(8,128)S(1)}, f32[328,128]{1,0:T(8,128)S(1)}, u32[]{:S(2)}, u32[]{:S(2)}) collective-permute-start(f32[328,128]{1,0:T(8,128)S(1)} %residual.1), channel_id=1, source_target_pairs={{0,0},{1,1},{2,2},{3,3},{4,4},{5,5},{6,6},{7,7},{14,8},{15,9},{12,... | collective-permute-start | bytes 503816 | tf_op jit(solution)/shard_map/ppermute | solution.py:557
  85.4 4.4 %collective-permute-done.24.half_ref = f32[328,128]{1,0:T(8,128)S(1)} collective-permute-done((f32[328,128]{1,0:T(8,128)S(1)}, f32[328,128]{1,0:T(8,128)S(1)}, u32[]{:S(2)}, u32[]{:S(2)}) %collective-permute-start.24) | collective-permute-done | bytes 167968 | tf_op jit(solution)/shard_map/ppermute | solution.py:557
  89.9 0.1 spread.2
  90.0 0.8 reshape.20
  90.8 2.6 %collective-permute-done.27.half_ref = f32[328,128]{1,0:T(8,128)S(1)} collective-permute-done((f32[328,128]{1,0:T(8,128)S(1)}, f32[328,128]{1,0:T(8,128)S(1)}, u32[]{:S(2)}, u32[]{:S(2)}) %collective-permute-start.27) | collective-permute-done | bytes 167968 | tf_op jit(solution)/shard_map/ppermute | solution.py:557
  93.3 0.1 spread.3
  93.5 0.8 reshape.21
  (20 shorter events, 0.2 us)
Async XLA Ops:
  0.6 1.0 %copy-start.1 = (s32[4,1,128]{2,1,0:T(1,128)S(1)}, s32[4,1,128]{2,1,0:T(1,128)}, u32[]{:S(2)}) copy-start(s32[4,1,128]{2,1,0:T(1,128)} %param.6) | copy-start | bytes 6148
  1.6 0.7 copy-start
  2.5 13.6 %collective-permute-start.1 = (f32[328,128]{1,0:T(8,128)S(1)}, f32[328,128]{1,0:T(8,128)S(1)}, u32[]{:S(2)}, u32[]{:S(2)}) collective-permute-start(f32[328,128]{1,0:T(8,128)S(1)} %pack.1), channel_id=1, source_target_pairs={{0,128},{1,129},{2,130},{3,131},{4,132},{5,133},{6,134},{7,135},{8... | collective-permute-start | bytes 503816 | tf_op jit(solution)/shard_map/ppermute | solution.py:557
  9.9 9.7 %collective-permute-start = (f32[328,128]{1,0:T(8,128)S(1)}, f32[328,128]{1,0:T(8,128)S(1)}, u32[]{:S(2)}, u32[]{:S(2)}) collective-permute-start(f32[328,128]{1,0:T(8,128)S(1)} %pack.1), channel_id=1, source_target_pairs={{0,0},{1,1},{2,2},{3,3},{4,4},{5,5},{6,6},{7,7},{8,14},{9,15},{10,... | collective-permute-start | bytes 503816 | tf_op jit(solution)/shard_map/ppermute | solution.py:557
  19.9 1.3 %collective-permute-start.2 = (f32[18,8,128]{2,1,0:T(8,128)S(1)}, f32[18,8,128]{2,1,0:T(8,128)S(1)}, u32[]{:S(2)}, u32[]{:S(2)}) collective-permute-start(f32[18,8,128]{2,1,0:T(8,128)S(1)} %get-tuple-element.48), channel_id=1, source_target_pairs={{0,1},{1,0},{2,3},{3,2},{4,5},{5,4},{6,7},{7,6},{14,15},{15,14},{1... | collective-permute-start | bytes 221192 | tf_op jit(solution)/shard_map/ppermute | solution.py:557
  20.0 3.9 %collective-permute-start.3 = (f32[18,8,128]{2,1,0:T(8,128)S(1)}, f32[18,8,128]{2,1,0:T(8,128)S(1)}, u32[]{:S(2)}, u32[]{:S(2)}) collective-permute-start(f32[18,8,128]{2,1,0:T(8,128)S(1)} %get-tuple-element.49), channel_id=1, source_target_pairs={{0,128},{1,2},{2,1},{3,4},{4,3},{5,6},{6,5},{7,14},{14,7},{15,12},... | collective-permute-start | bytes 221192 | tf_op jit(solution)/shard_map/ppermute | solution.py:557
  24.3 1.4 %collective-permute-start.4 = (f32[17,8,128]{2,1,0:T(8,128)S(1)}, f32[17,8,128]{2,1,0:T(8,128)S(1)}, u32[]{:S(2)}, u32[]{:S(2)}) collective-permute-start(f32[17,8,128]{2,1,0:T(8,128)S(1)} %get-tuple-element.54), channel_id=1, source_target_pairs={{0,1},{1,0},{2,3},{3,2},{4,5},{5,4},{6,7},{7,6},{14,15},{15,14},{1... | collective-permute-start | bytes 208904 | tf_op jit(solution)/shard_map/ppermute | solution.py:557
  24.8 3.7 %collective-permute-start.5 = (f32[17,8,128]{2,1,0:T(8,128)S(1)}, f32[17,8,128]{2,1,0:T(8,128)S(1)}, u32[]{:S(2)}, u32[]{:S(2)}) collective-permute-start(f32[17,8,128]{2,1,0:T(8,128)S(1)} %get-tuple-element.55), channel_id=1, source_target_pairs={{0,128},{1,2},{2,1},{3,4},{4,3},{5,6},{6,5},{7,14},{14,7},{15,12},... | collective-permute-start | bytes 208904 | tf_op jit(solution)/shard_map/ppermute | solution.py:557
  29.1 1.4 %collective-permute-start.6 = (f32[22,8,128]{2,1,0:T(8,128)S(1)}, f32[22,8,128]{2,1,0:T(8,128)S(1)}, u32[]{:S(2)}, u32[]{:S(2)}) collective-permute-start(f32[22,8,128]{2,1,0:T(8,128)S(1)} %get-tuple-element.58), channel_id=1, source_target_pairs={{0,1},{1,0},{2,3},{3,2},{4,5},{5,4},{6,7},{7,6},{14,15},{15,14},{1... | collective-permute-start | bytes 270344 | tf_op jit(solution)/shard_map/ppermute | solution.py:557
  30.5 10.0 %collective-permute-start.7 = (f32[27,8,128]{2,1,0:T(8,128)S(1)}, f32[27,8,128]{2,1,0:T(8,128)S(1)}, u32[]{:S(2)}, u32[]{:S(2)}) collective-permute-start(f32[27,8,128]{2,1,0:T(8,128)S(1)} %get-tuple-element.61), channel_id=1, source_target_pairs={{0,128},{1,2},{2,1},{3,4},{4,3},{5,6},{6,5},{7,14},{14,7},{15,12},... | collective-permute-start | bytes 331784 | tf_op jit(solution)/shard_map/ppermute | solution.py:557
  31.0 6.3 %collective-permute-start.9 = (f32[10,8,128]{2,1,0:T(8,128)S(1)}, f32[10,8,128]{2,1,0:T(8,128)S(1)}, u32[]{:S(2)}, u32[]{:S(2)}) collective-permute-start(f32[10,8,128]{2,1,0:T(8,128)S(1)} %get-tuple-element.62.chip_ref), channel_id=1, source_target_pairs={{0,128},{1,6},{2,130},{3,14},{4,132},{5,12},{6,1},{7,10},{14,3},{1... | collective-permute-start | bytes 122888 | tf_op jit(solution)/shard_map/ppermute | solution.py:557
  35.6 4.9 %collective-permute-start.8 = (f32[10,8,128]{2,1,0:T(8,128)S(1)}, f32[10,8,128]{2,1,0:T(8,128)S(1)}, u32[]{:S(2)}, u32[]{:S(2)}) collective-permute-start(f32[10,8,128]{2,1,0:T(8,128)S(1)} %get-tuple-element.62.chip_ref), channel_id=1, source_target_pairs={{0,128},{1,4},{2,130},{3,6},{4,1},{5,14},{6,3},{7,12},{14,5},{15,1... | collective-permute-start | bytes 122888 | tf_op jit(solution)/shard_map/ppermute | solution.py:557
  40.5 1.4 %collective-permute-start.10 = (f32[30,8,128]{2,1,0:T(8,128)S(1)}, f32[30,8,128]{2,1,0:T(8,128)S(1)}, u32[]{:S(2)}, u32[]{:S(2)}) collective-permute-start(f32[30,8,128]{2,1,0:T(8,128)S(1)} %side.2.mine_ref), channel_id=1, source_target_pairs={{0,1},{1,0},{2,3},{3,2},{4,5},{5,4},{6,7},{7,6},{14,15},{15,14},{1... | collective-permute-start | bytes 368648 | tf_op jit(solution)/shard_map/ppermute | solution.py:557
  43.3 3.6 %collective-permute-start.11 = (f32[17,8,128]{2,1,0:T(8,128)S(1)}, f32[17,8,128]{2,1,0:T(8,128)S(1)}, u32[]{:S(2)}, u32[]{:S(2)}) collective-permute-start(f32[17,8,128]{2,1,0:T(8,128)S(1)} %get-tuple-element.65), channel_id=1, source_target_pairs={{0,1},{1,0},{2,3},{3,2},{4,5},{5,4},{6,7},{7,6},{14,15},{15,14},{1... | collective-permute-start | bytes 208904 | tf_op jit(solution)/shard_map/ppermute | solution.py:557
  43.6 5.3 %collective-permute-start.12 = (f32[17,8,128]{2,1,0:T(8,128)S(1)}, f32[17,8,128]{2,1,0:T(8,128)S(1)}, u32[]{:S(2)}, u32[]{:S(2)}) collective-permute-start(f32[17,8,128]{2,1,0:T(8,128)S(1)} %get-tuple-element.66), channel_id=1, source_target_pairs={{0,128},{1,2},{2,1},{3,4},{4,3},{5,6},{6,5},{7,14},{14,7},{15,12},... | collective-permute-start | bytes 208904 | tf_op jit(solution)/shard_map/ppermute | solution.py:557
  49.4 2.0 %collective-permute-start.13 = (f32[17,8,128]{2,1,0:T(8,128)S(1)}, f32[17,8,128]{2,1,0:T(8,128)S(1)}, u32[]{:S(2)}, u32[]{:S(2)}) collective-permute-start(f32[17,8,128]{2,1,0:T(8,128)S(1)} %get-tuple-element.69), channel_id=1, source_target_pairs={{0,1},{1,0},{2,3},{3,2},{4,5},{5,4},{6,7},{7,6},{14,15},{15,14},{1... | collective-permute-start | bytes 208904 | tf_op jit(solution)/shard_map/ppermute | solution.py:557
  49.5 3.9 %collective-permute-start.14 = (f32[17,8,128]{2,1,0:T(8,128)S(1)}, f32[17,8,128]{2,1,0:T(8,128)S(1)}, u32[]{:S(2)}, u32[]{:S(2)}) collective-permute-start(f32[17,8,128]{2,1,0:T(8,128)S(1)} %get-tuple-element.70), channel_id=1, source_target_pairs={{0,128},{1,2},{2,1},{3,4},{4,3},{5,6},{6,5},{7,14},{14,7},{15,12},... | collective-permute-start | bytes 208904 | tf_op jit(solution)/shard_map/ppermute | solution.py:557
  53.9 2.2 %collective-permute-start.15 = (f32[17,8,128]{2,1,0:T(8,128)S(1)}, f32[17,8,128]{2,1,0:T(8,128)S(1)}, u32[]{:S(2)}, u32[]{:S(2)}) collective-permute-start(f32[17,8,128]{2,1,0:T(8,128)S(1)} %get-tuple-element.73), channel_id=1, source_target_pairs={{0,1},{1,0},{2,3},{3,2},{4,5},{5,4},{6,7},{7,6},{14,15},{15,14},{1... | collective-permute-start | bytes 208904 | tf_op jit(solution)/shard_map/ppermute | solution.py:557
  54.3 3.7 %collective-permute-start.16 = (f32[17,8,128]{2,1,0:T(8,128)S(1)}, f32[17,8,128]{2,1,0:T(8,128)S(1)}, u32[]{:S(2)}, u32[]{:S(2)}) collective-permute-start(f32[17,8,128]{2,1,0:T(8,128)S(1)} %get-tuple-element.74), channel_id=1, source_target_pairs={{0,128},{1,2},{2,1},{3,4},{4,3},{5,6},{6,5},{7,14},{14,7},{15,12},... | collective-permute-start | bytes 208904 | tf_op jit(solution)/shard_map/ppermute | solution.py:557
  58.6 1.4 %collective-permute-start.17 = (f32[22,8,128]{2,1,0:T(8,128)S(1)}, f32[22,8,128]{2,1,0:T(8,128)S(1)}, u32[]{:S(2)}, u32[]{:S(2)}) collective-permute-start(f32[22,8,128]{2,1,0:T(8,128)S(1)} %get-tuple-element.77), channel_id=1, source_target_pairs={{0,1},{1,0},{2,3},{3,2},{4,5},{5,4},{6,7},{7,6},{14,15},{15,14},{1... | collective-permute-start | bytes 270344 | tf_op jit(solution)/shard_map/ppermute | solution.py:557
  60.0 10.2 %collective-permute-start.18 = (f32[27,8,128]{2,1,0:T(8,128)S(1)}, f32[27,8,128]{2,1,0:T(8,128)S(1)}, u32[]{:S(2)}, u32[]{:S(2)}) collective-permute-start(f32[27,8,128]{2,1,0:T(8,128)S(1)} %get-tuple-element.80), channel_id=1, source_target_pairs={{0,128},{1,2},{2,1},{3,4},{4,3},{5,6},{6,5},{7,14},{14,7},{15,12},... | collective-permute-start | bytes 331784 | tf_op jit(solution)/shard_map/ppermute | solution.py:557
  61.8 5.2 %collective-permute-start.20 = (f32[10,8,128]{2,1,0:T(8,128)S(1)}, f32[10,8,128]{2,1,0:T(8,128)S(1)}, u32[]{:S(2)}, u32[]{:S(2)}) collective-permute-start(f32[10,8,128]{2,1,0:T(8,128)S(1)} %get-tuple-element.81.chip_ref), channel_id=1, source_target_pairs={{0,128},{1,6},{2,130},{3,14},{4,132},{5,12},{6,1},{7,10},{14,3},{1... | collective-permute-start | bytes 122888 | tf_op jit(solution)/shard_map/ppermute | solution.py:557
  65.3 4.9 %collective-permute-start.19 = (f32[10,8,128]{2,1,0:T(8,128)S(1)}, f32[10,8,128]{2,1,0:T(8,128)S(1)}, u32[]{:S(2)}, u32[]{:S(2)}) collective-permute-start(f32[10,8,128]{2,1,0:T(8,128)S(1)} %get-tuple-element.81.chip_ref), channel_id=1, source_target_pairs={{0,128},{1,4},{2,130},{3,6},{4,1},{5,14},{6,3},{7,12},{14,5},{15,1... | collective-permute-start | bytes 122888 | tf_op jit(solution)/shard_map/ppermute | solution.py:557
  70.3 1.4 %collective-permute-start.21 = (f32[30,8,128]{2,1,0:T(8,128)S(1)}, f32[30,8,128]{2,1,0:T(8,128)S(1)}, u32[]{:S(2)}, u32[]{:S(2)}) collective-permute-start(f32[30,8,128]{2,1,0:T(8,128)S(1)} %side.3.mine_ref), channel_id=1, source_target_pairs={{0,1},{1,0},{2,3},{3,2},{4,5},{5,4},{6,7},{7,6},{14,15},{15,14},{1... | collective-permute-start | bytes 368648 | tf_op jit(solution)/shard_map/ppermute | solution.py:557
  73.1 3.7 %collective-permute-start.22 = (f32[17,8,128]{2,1,0:T(8,128)S(1)}, f32[17,8,128]{2,1,0:T(8,128)S(1)}, u32[]{:S(2)}, u32[]{:S(2)}) collective-permute-start(f32[17,8,128]{2,1,0:T(8,128)S(1)} %get-tuple-element.84), channel_id=1, source_target_pairs={{0,1},{1,0},{2,3},{3,2},{4,5},{5,4},{6,7},{7,6},{14,15},{15,14},{1... | collective-permute-start | bytes 208904 | tf_op jit(solution)/shard_map/ppermute | solution.py:557
  73.3 5.5 %collective-permute-start.23 = (f32[17,8,128]{2,1,0:T(8,128)S(1)}, f32[17,8,128]{2,1,0:T(8,128)S(1)}, u32[]{:S(2)}, u32[]{:S(2)}) collective-permute-start(f32[17,8,128]{2,1,0:T(8,128)S(1)} %get-tuple-element.85), channel_id=1, source_target_pairs={{0,128},{1,2},{2,1},{3,4},{4,3},{5,6},{6,5},{7,14},{14,7},{15,12},... | collective-permute-start | bytes 208904 | tf_op jit(solution)/shard_map/ppermute | solution.py:557
  79.3 3.9 %collective-permute-start.25 = (f32[17,8,128]{2,1,0:T(8,128)S(1)}, f32[17,8,128]{2,1,0:T(8,128)S(1)}, u32[]{:S(2)}, u32[]{:S(2)}) collective-permute-start(f32[17,8,128]{2,1,0:T(8,128)S(1)} %get-tuple-element.88), channel_id=1, source_target_pairs={{0,1},{1,0},{2,3},{3,2},{4,5},{5,4},{6,7},{7,6},{14,15},{15,14},{1... | collective-permute-start | bytes 208904 | tf_op jit(solution)/shard_map/ppermute | solution.py:557
  79.4 3.9 %collective-permute-start.26 = (f32[17,8,128]{2,1,0:T(8,128)S(1)}, f32[17,8,128]{2,1,0:T(8,128)S(1)}, u32[]{:S(2)}, u32[]{:S(2)}) collective-permute-start(f32[17,8,128]{2,1,0:T(8,128)S(1)} %get-tuple-element.89), channel_id=1, source_target_pairs={{0,128},{1,2},{2,1},{3,4},{4,3},{5,6},{6,5},{7,14},{14,7},{15,12},... | collective-permute-start | bytes 208904 | tf_op jit(solution)/shard_map/ppermute | solution.py:557
  81.3 8.6 %collective-permute-start.24 = (f32[328,128]{1,0:T(8,128)S(1)}, f32[328,128]{1,0:T(8,128)S(1)}, u32[]{:S(2)}, u32[]{:S(2)}) collective-permute-start(f32[328,128]{1,0:T(8,128)S(1)} %get-tuple-element.86), channel_id=1, source_target_pairs={{0,0},{1,1},{2,2},{3,3},{4,4},{5,5},{6,6},{7,7},{14,8},{15,9},{12,... | collective-permute-start | bytes 503816 | tf_op jit(solution)/shard_map/ppermute | solution.py:557
  83.5 9.8 %collective-permute-start.27 = (f32[328,128]{1,0:T(8,128)S(1)}, f32[328,128]{1,0:T(8,128)S(1)}, u32[]{:S(2)}, u32[]{:S(2)}) collective-permute-start(f32[328,128]{1,0:T(8,128)S(1)} %residual.1), channel_id=1, source_target_pairs={{0,0},{1,1},{2,2},{3,3},{4,4},{5,5},{6,6},{7,7},{14,8},{15,9},{12,... | collective-permute-start | bytes 503816 | tf_op jit(solution)/shard_map/ppermute | solution.py:557

commit v5 on v4

--- a/solution.py
+++ b/solution.py
@@ -94,9 +94,15 @@
         return jnp.where(self.even, x, y)
 
 
-def apply_operator(mv, u_ref, coeff, y_ref, acc_ref, up_ref):
+INNER = (1, 2, 3)
+
+
+def apply_operator(mv, u_ref, coeff, y_ref, acc_ref, up_ref, ready_ref=None):
     for b in range(N):
         for c in range(N):
+            if ready_ref is not None and b in INNER:
+                up_ref[b * 5 + c] = mv.above(u_ref[at(0, b, c)])
+                continue
             u = [u_ref[at(a, b, c)] for a in range(4)]
             u.append(mv.above(u[0]))
             up_ref[b * 5 + c] = u[4]
@@ -110,8 +116,12 @@
         u = [[up_ref[b * 5 + c] if a == 4 else u_ref[at(a, b, c)] for c in range(N)] for b in range(N)]
         across = [line([u[b][c] for b in range(N)]) for c in range(N)]
         for b in range(N):
-            along = line(u[b])
-            y = [(acc_ref[at(a, b, c)] + along[c] + across[c][b]) * scale[SYM[b], SYM[c]] for c in range(N)]
+            if ready_ref is not None and b in INNER:
+                base = [ready_ref[at(a, b, c)] for c in range(N)]
+            else:
+                along = line(u[b])
+                base = [acc_ref[at(a, b, c)] + along[c] for c in range(N)]
+            y = [(base[c] + across[c][b]) * scale[SYM[b], SYM[c]] for c in range(N)]
             if a == 4:
                 for c in range(N):
                     up_ref[b * 5 + c] = y[c]
@@ -170,9 +180,13 @@
     return row
 
 
-def smooth(mv, u_ref, f_ref, y_ref, left, right, inv_ref, out_ref):
+def smooth(mv, u_ref, f_ref, y_ref, left, right, inv_ref, out_ref, mid_ref=None, rows=range(N)):
     for a in range(4):
-        for b in range(N):
+        for b in rows:
+            if mid_ref is not None and b in INNER:
+                for c in range(N):
+                    out_ref[at(a, b, c)] = mid_ref[at(a, b, c)]
+                continue
             r = residual_row(mv, f_ref, y_ref, left, right, a, b)
             u = [u_ref[at(a, b, c)] + r[c] * inverse_at(inv_ref, a, b, c) for c in range(N)]
             u[4] = mv.after(u[0], u[4])
@@ -255,24 +269,40 @@
     put_faces(mv, y_ref, a_ref, b_ref)
 
 
-def sweep_kernel(marks, u_ref, y_ref, f_ref, inv_ref, coeff_ref, ga_ref, gb_ref, un_ref, yn_ref, a_ref, b_ref, acc_ref, up_ref):
+def inner_kernel(u_ref, y_ref, f_ref, inv_ref, mid_ref, ready_ref):
+    mv = Moves()
+    smooth(mv, u_ref, f_ref, y_ref, None, None, inv_ref, mid_ref, None, INNER)
+    for b in INNER:
+        planes = []
+        for c in range(N):
+            u = [mid_ref[at(a, b, c)] for a in range(4)]
+            u.append(mv.above(u[0]))
+            planes.append(u[4])
+            for a, value in enumerate(line(u)):
+                ready_ref[at(a, b, c)] = value
+        for a in range(N):
+            for c, value in enumerate(line(planes if a == 4 else [mid_ref[at(a, b, c)] for c in range(N)])):
+                ready_ref[at(a, b, c)] = ready_ref[at(a, b, c)] + value
+
+
+def sweep_kernel(marks, u_ref, y_ref, f_ref, inv_ref, coeff_ref, mid_ref, ready_ref, ga_ref, gb_ref, un_ref, yn_ref, a_ref, b_ref, acc_ref, up_ref):
     mv = Moves(marks)
     left, right = got_faces(mv, ga_ref, gb_ref, 17)
-    smooth(mv, u_ref, f_ref, y_ref, left, right, inv_ref, un_ref)
-    apply_operator(mv, un_ref, coeff_ref[...], yn_ref, acc_ref, up_ref)
+    smooth(mv, u_ref, f_ref, y_ref, left, right, inv_ref, un_ref, mid_ref)
+    apply_operator(mv, un_ref, coeff_ref[...], yn_ref, acc_ref, up_ref, ready_ref)
     put_faces(mv, yn_ref, a_ref, b_ref)
 
 
-def last_sweep_kernel(marks, u_ref, y_ref, f_ref, inv_ref, coeff_ref, ga_ref, gb_ref, yn_ref, a_ref, b_ref, half_ref, un_ref, acc_ref, up_ref):
-    sweep_kernel(marks, u_ref, y_ref, f_ref, inv_ref, coeff_ref, ga_ref, gb_ref, un_ref, yn_ref, a_ref, b_ref, acc_ref, up_ref)
+def last_sweep_kernel(marks, u_ref, y_ref, f_ref, inv_ref, coeff_ref, mid_ref, ready_ref, ga_ref, gb_ref, yn_ref, a_ref, b_ref, half_ref, un_ref, acc_ref, up_ref):
+    sweep_kernel(marks, u_ref, y_ref, f_ref, inv_ref, coeff_ref, mid_ref, ready_ref, ga_ref, gb_ref, un_ref, yn_ref, a_ref, b_ref, acc_ref, up_ref)
     half_rows(Moves(marks), un_ref, half_ref)
 
 
-def restrict_kernel(marks, u_ref, y_ref, f_ref, inv_ref, coeff_ref, ga_ref, gb_ref, part_ref, un_ref, yn_ref, own_ref, a_ref, b_ref, acc_ref, up_ref):
+def restrict_kernel(marks, u_ref, y_ref, f_ref, inv_ref, coeff_ref, mid_ref, ready_ref, ga_ref, gb_ref, part_ref, un_ref, yn_ref, own_ref, a_ref, b_ref, acc_ref, up_ref):
     mv = Moves(marks)
     left, right = got_faces(mv, ga_ref, gb_ref, 17)
-    smooth(mv, u_ref, f_ref, y_ref, left, right, inv_ref, un_ref)
-    apply_operator(mv, un_ref, coeff_ref[...], yn_ref, acc_ref, up_ref)
+    smooth(mv, u_ref, f_ref, y_ref, left, right, inv_ref, un_ref, mid_ref)
+    apply_operator(mv, un_ref, coeff_ref[...], yn_ref, acc_ref, up_ref, ready_ref)
     put_faces(mv, yn_ref, a_ref, b_ref, 5)
     z = [[], []]
     for c in range(N):
@@ -502,7 +532,7 @@
 WORK = [(125, 8, 128), (25, 8, 128)]
 
 
-def call(name, kernel, outs, scratch, *args):
+def call(name, kernel, outs, scratch, *args, cost=None):
     return pl.pallas_call(
         kernel,
         out_shape=[jax.ShapeDtypeStruct(s, F32) for s in outs],
@@ -511,6 +541,7 @@
         scratch_shapes=[pltpu.VMEM(s, F32) for s in scratch],
         compiler_params=pltpu.CompilerParams(vmem_limit_bytes=12 * 1024 * 1024),
         name=name,
+        cost_estimate=cost,
     )(*args)
 
 
@@ -575,13 +606,17 @@
         a, b = trade(a, b)
         u, y, f, inv, a, b = call("first", first_kernel, [FIELD, FIELD, FIELD, (12, 8, 128), *faces], WORK, marks, part, coeff, a, b)
 
+        def inner(u, y):
+            cost = pl.CostEstimate(flops=2000000, bytes_accessed=1500000, transcendentals=0)
+            return call("inner", inner_kernel, [FIELD, (125, 8, 128)], [], u, y, f, inv, cost=cost)
+
         def sweep(u, y, a, b):
             a, b = trade(a, b)
-            return call("sweep", sweep_kernel, [FIELD, FIELD, *faces], WORK, marks, u, y, f, inv, coeff, a, b)
+            return call("sweep", sweep_kernel, [FIELD, FIELD, *faces], WORK, marks, u, y, f, inv, coeff, *inner(u, y), a, b)
 
         def sweep_and_correct(u, y, a, b):
             a, b = trade(a, b)
-            u, y, own, a, b = call("restrict", restrict_kernel, [FIELD, FIELD, (5, 8, 128), (22, 8, 128), (22, 8, 128)], WORK, marks, u, y, f, inv, coeff, a, b, part)
+            u, y, own, a, b = call("restrict", restrict_kernel, [FIELD, FIELD, (5, 8, 128), (22, 8, 128), (22, 8, 128)], WORK, marks, u, y, f, inv, coeff, *inner(u, y), a, b, part)
             a = swap(a, within)
             chip, near = call("chip", chip_kernel, [(10, 8, 128), (27, 8, 128)], [], marks, own, a, b)
             near, second, third = swap(near, beyond[1]), swap(chip, beyond[2]), swap(chip, beyond[3])
@@ -594,7 +629,7 @@
         u, y, a, b = sweep(u, y, a, b)
         u, y, a, b = sweep_and_correct(u, y, a, b)
         a, b = trade(a, b)
-        y, a, b, half = call("last", last_sweep_kernel, [FIELD, *faces, (328, 128)], [FIELD, *WORK], marks, u, y, f, inv, coeff, a, b)
+        y, a, b, half = call("last", last_sweep_kernel, [FIELD, *faces, (328, 128)], [FIELD, *WORK], marks, u, y, f, inv, coeff, *inner(u, y), a, b)
         a, b = trade(a, b)
         half = restore(half)
         (left_half,) = call("residual", residual_kernel, [(328, 128)], [FIELD], marks, y, f, a, b)

time: 95.4 us -> 94.7 us (level)
  waiting for transfers between devices: 40.5 us -> 39.5 us
    pallas_call x17 -> x22, Pallas kernels: 6.59 us -> 6.81 us  [call(): pl.pallas_call(kernel, out_shape=[jax.ShapeDtypeStruct(s, F32) for s in o...]
  transfers between devices with their start and end apart: 28 -> 28, of which waited for: 20 -> 20; matrix products, arithmetic and copies ran while one was open for 2% -> 2% of each run, Pallas kernels for 0% -> 1%
where the time goes in v5:
time: 94.7 us; the launch traced here: 93.5 us
  starting transfers between devices  42.4 us (45%)
  waiting for transfers between devices  39.5 us (42%)
  Pallas kernels  6.81 us (7%)
  local copies, waits for them, and re-layouts  3.95 us (4%)
    ppermute x28, starting transfers between devices, swap(): return lax.ppermute(x, AXES, pairs)  42.4 us
    ppermute x28, waiting for transfers between devices, swap(): return lax.ppermute(x, AXES, pairs)  39.5 us
    pallas_call x22, Pallas kernels, call(): pl.pallas_call(kernel, out_shape=[jax.ShapeDtypeStruct(s, F32) for s in o...  6.81 us
  transfers between devices with their start and end apart: 28, of which 20 were waited for; matrix products, arithmetic and copies ran while one was open for 2% of the time, Pallas kernels for 1%

profile of v5, /device:TPU:2, one launch (start us, length us, event | category | flops | bytes accessed | tf_op | source)
XLA Modules:
  0.0 93.5 jit_solution(8901306155696615421)
XLA Ops:
  0.6 1.0 %copy.12 = f32[500,1,128]{2,0,1:T(8,128)S(1)} copy(f32[500,1,128]{2,1,0:T(1,128)} %bitcast.9) | data formatting | bytes 512000 | tf_op jit(solution)/shard_map/reshape | solution.py:597
  1.6 0.7 copy-done
  2.3 0.1 pack.1
  2.5 7.5 %collective-permute-start.1 = (f32[328,128]{1,0:T(8,128)S(1)}, f32[328,128]{1,0:T(8,128)S(1)}, u32[]{:S(2)}, u32[]{:S(2)}) collective-permute-start(f32[328,128]{1,0:T(8,128)S(1)} %pack.1), channel_id=1, source_target_pairs={{0,128},{1,129},{2,130},{3,131},{4,132},{5,133},{6,134},{7,135},{8... | collective-permute-start | bytes 503816 | tf_op jit(solution)/shard_map/ppermute | solution.py:588
  9.9 5.4 %collective-permute-start = (f32[328,128]{1,0:T(8,128)S(1)}, f32[328,128]{1,0:T(8,128)S(1)}, u32[]{:S(2)}, u32[]{:S(2)}) collective-permute-start(f32[328,128]{1,0:T(8,128)S(1)} %pack.1), channel_id=1, source_target_pairs={{0,0},{1,1},{2,2},{3,3},{4,4},{5,5},{6,6},{7,7},{8,14},{9,15},{10,... | collective-permute-start | bytes 503816 | tf_op jit(solution)/shard_map/ppermute | solution.py:588
  15.3 0.7 dynamic-slice_bitcast_fusion
  16.0 3.7 %collective-permute-done.same_ref = f32[328,128]{1,0:T(8,128)S(1)} collective-permute-done((f32[328,128]{1,0:T(8,128)S(1)}, f32[328,128]{1,0:T(8,128)S(1)}, u32[]{:S(2)}, u32[]{:S(2)}) %collective-permute-start) | collective-permute-done | bytes 167968 | tf_op jit(solution)/shard_map/ppermute | solution.py:588
  19.8 0.2 unpack.1
  20.0 0.5 collective-permute-start.3
  20.4 0.8 collective-permute-done.2.ga_ref
  21.2 2.6 %collective-permute-done.3.gb_ref = f32[18,8,128]{2,1,0:T(8,128)S(1)} collective-permute-done((f32[18,8,128]{2,1,0:T(8,128)S(1)}, f32[18,8,128]{2,1,0:T(8,128)S(1)}, u32[]{:S(2)}, u32[]{:S(2)}) %collective-permute-start.3) | collective-permute-done | bytes 73760 | tf_op jit(solution)/shard_map/ppermute | solution.py:588
  23.8 0.5 first.1
  24.4 0.5 collective-permute-start.4
  24.9 0.2 inner.5
  25.1 0.7 collective-permute-done.4.ga_ref
  25.8 2.8 %collective-permute-done.5.gb_ref = f32[17,8,128]{2,1,0:T(8,128)S(1)} collective-permute-done((f32[17,8,128]{2,1,0:T(8,128)S(1)}, f32[17,8,128]{2,1,0:T(8,128)S(1)}, u32[]{:S(2)}, u32[]{:S(2)}) %collective-permute-start.5) | collective-permute-done | bytes 69664 | tf_op jit(solution)/shard_map/ppermute | solution.py:588
  28.6 0.4 restrict.2
  29.0 0.2 collective-permute-start.6
  29.2 1.2 %collective-permute-done.6.ga_ref = f32[22,8,128]{2,1,0:T(8,128)S(1)} collective-permute-done((f32[22,8,128]{2,1,0:T(8,128)S(1)}, f32[22,8,128]{2,1,0:T(8,128)S(1)}, u32[]{:S(2)}, u32[]{:S(2)}) %collective-permute-start.6) | collective-permute-done | bytes 90144 | tf_op jit(solution)/shard_map/ppermute | solution.py:588
  30.4 0.5 collective-permute-start.7
  30.9 4.6 %collective-permute-start.9 = (f32[10,8,128]{2,1,0:T(8,128)S(1)}, f32[10,8,128]{2,1,0:T(8,128)S(1)}, u32[]{:S(2)}, u32[]{:S(2)}) collective-permute-start(f32[10,8,128]{2,1,0:T(8,128)S(1)} %get-tuple-element.74.chip_ref), channel_id=1, source_target_pairs={{0,128},{1,6},{2,130},{3,14},{4,132},{5,12},{6,1},{7,10},{14,3},{1... | collective-permute-start | bytes 122888 | tf_op jit(solution)/shard_map/ppermute | solution.py:588
  35.5 1.7 %collective-permute-done.9.third_ref = f32[10,8,128]{2,1,0:T(8,128)S(1)} collective-permute-done((f32[10,8,128]{2,1,0:T(8,128)S(1)}, f32[10,8,128]{2,1,0:T(8,128)S(1)}, u32[]{:S(2)}, u32[]{:S(2)}) %collective-permute-start.9) | collective-permute-done | bytes 40992 | tf_op jit(solution)/shard_map/ppermute | solution.py:588
  37.2 3.2 %collective-permute-done.8.second_ref = f32[10,8,128]{2,1,0:T(8,128)S(1)} collective-permute-done((f32[10,8,128]{2,1,0:T(8,128)S(1)}, f32[10,8,128]{2,1,0:T(8,128)S(1)}, u32[]{:S(2)}, u32[]{:S(2)}) %collective-permute-start.8) | collective-permute-done | bytes 40992 | tf_op jit(solution)/shard_map/ppermute | solution.py:588
  40.4 0.1 collective-permute-start.10
  40.5 1.3 %collective-permute-done.10.other_ref = f32[30,8,128]{2,1,0:T(8,128)S(1)} collective-permute-done((f32[30,8,128]{2,1,0:T(8,128)S(1)}, f32[30,8,128]{2,1,0:T(8,128)S(1)}, u32[]{:S(2)}, u32[]{:S(2)}) %collective-permute-start.10) | collective-permute-done | bytes 122912 | tf_op jit(solution)/shard_map/ppermute | solution.py:588
  41.8 1.4 %correct.2 = (f32[100,8,128]{2,1,0:T(8,128)S(1)}, f32[100,8,128]{2,1,0:T(8,128)S(1)}, f32[17,8,128]{2,1,0:T(8,128)S(1)}, f32[17,8,128]{2,1,0:T(8,128)S(1)}) custom-call(f32[18,8,128]{2,1,0:T(8,128)S(1)} %broadcast_in_dim.17.marks, f32[100,8,128]{2,1,0:T(8,128)S(1)} %get-tuple-element.68.u_ref, f32[100,8,128]{2,1,0:T(8,128)S(1)} %get-tuple-element.69.y_ref, ...), custom_call_target="tpu_custom_call" | custom-call | tf_op jit(solution)/shard_map/correct/pallas_call | solution.py:536
  43.2 0.2 collective-permute-start.11
  43.5 3.4 %collective-permute-start.12 = (f32[17,8,128]{2,1,0:T(8,128)S(1)}, f32[17,8,128]{2,1,0:T(8,128)S(1)}, u32[]{:S(2)}, u32[]{:S(2)}) collective-permute-start(f32[17,8,128]{2,1,0:T(8,128)S(1)} %get-tuple-element.80), channel_id=1, source_target_pairs={{0,128},{1,2},{2,1},{3,4},{4,3},{5,6},{6,5},{7,14},{14,7},{15,12},... | collective-permute-start | bytes 208904 | tf_op jit(solution)/shard_map/ppermute | solution.py:588
  46.8 0.2 inner.6
  47.0 1.8 %collective-permute-done.12.gb_ref = f32[17,8,128]{2,1,0:T(8,128)S(1)} collective-permute-done((f32[17,8,128]{2,1,0:T(8,128)S(1)}, f32[17,8,128]{2,1,0:T(8,128)S(1)}, u32[]{:S(2)}, u32[]{:S(2)}) %collective-permute-start.12) | collective-permute-done | bytes 69664 | tf_op jit(solution)/shard_map/ppermute | solution.py:588
  48.8 0.3 sweep.2
  49.2 1.9 %collective-permute-start.14 = (f32[17,8,128]{2,1,0:T(8,128)S(1)}, f32[17,8,128]{2,1,0:T(8,128)S(1)}, u32[]{:S(2)}, u32[]{:S(2)}) collective-permute-start(f32[17,8,128]{2,1,0:T(8,128)S(1)} %get-tuple-element.86), channel_id=1, source_target_pairs={{0,128},{1,2},{2,1},{3,4},{4,3},{5,6},{6,5},{7,14},{14,7},{15,12},... | collective-permute-start | bytes 208904 | tf_op jit(solution)/shard_map/ppermute | solution.py:588
  51.1 0.2 inner.7
  51.3 1.8 %collective-permute-done.14.gb_ref = f32[17,8,128]{2,1,0:T(8,128)S(1)} collective-permute-done((f32[17,8,128]{2,1,0:T(8,128)S(1)}, f32[17,8,128]{2,1,0:T(8,128)S(1)}, u32[]{:S(2)}, u32[]{:S(2)}) %collective-permute-start.14) | collective-permute-done | bytes 69664 | tf_op jit(solution)/shard_map/ppermute | solution.py:588
  53.1 0.3 sweep.3
  53.5 0.4 collective-permute-start.15
  53.9 1.7 %collective-permute-start.16 = (f32[17,8,128]{2,1,0:T(8,128)S(1)}, f32[17,8,128]{2,1,0:T(8,128)S(1)}, u32[]{:S(2)}, u32[]{:S(2)}) collective-permute-start(f32[17,8,128]{2,1,0:T(8,128)S(1)} %get-tuple-element.92), channel_id=1, source_target_pairs={{0,128},{1,2},{2,1},{3,4},{4,3},{5,6},{6,5},{7,14},{14,7},{15,12},... | collective-permute-start | bytes 208904 | tf_op jit(solution)/shard_map/ppermute | solution.py:588
  55.6 0.2 inner.8
  55.8 1.8 %collective-permute-done.16.gb_ref = f32[17,8,128]{2,1,0:T(8,128)S(1)} collective-permute-done((f32[17,8,128]{2,1,0:T(8,128)S(1)}, f32[17,8,128]{2,1,0:T(8,128)S(1)}, u32[]{:S(2)}, u32[]{:S(2)}) %collective-permute-start.16) | collective-permute-done | bytes 69664 | tf_op jit(solution)/shard_map/ppermute | solution.py:588
  57.6 0.4 restrict.3
  58.0 0.4 collective-permute-start.17
  58.4 1.0 %collective-permute-done.17.ga_ref = f32[22,8,128]{2,1,0:T(8,128)S(1)} collective-permute-done((f32[22,8,128]{2,1,0:T(8,128)S(1)}, f32[22,8,128]{2,1,0:T(8,128)S(1)}, u32[]{:S(2)}, u32[]{:S(2)}) %collective-permute-start.17) | collective-permute-done | bytes 90144 | tf_op jit(solution)/shard_map/ppermute | solution.py:588
  59.4 1.8 %collective-permute-start.18 = (f32[27,8,128]{2,1,0:T(8,128)S(1)}, f32[27,8,128]{2,1,0:T(8,128)S(1)}, u32[]{:S(2)}, u32[]{:S(2)}) collective-permute-start(f32[27,8,128]{2,1,0:T(8,128)S(1)} %get-tuple-element.98), channel_id=1, source_target_pairs={{0,128},{1,2},{2,1},{3,4},{4,3},{5,6},{6,5},{7,14},{14,7},{15,12},... | collective-permute-start | bytes 331784 | tf_op jit(solution)/shard_map/ppermute | solution.py:588
  61.3 3.5 %collective-permute-start.20 = (f32[10,8,128]{2,1,0:T(8,128)S(1)}, f32[10,8,128]{2,1,0:T(8,128)S(1)}, u32[]{:S(2)}, u32[]{:S(2)}) collective-permute-start(f32[10,8,128]{2,1,0:T(8,128)S(1)} %get-tuple-element.99.chip_ref), channel_id=1, source_target_pairs={{0,128},{1,6},{2,130},{3,14},{4,132},{5,12},{6,1},{7,10},{14,3},{1... | collective-permute-start | bytes 122888 | tf_op jit(solution)/shard_map/ppermute | solution.py:588
  64.7 1.7 %collective-permute-done.20.third_ref = f32[10,8,128]{2,1,0:T(8,128)S(1)} collective-permute-done((f32[10,8,128]{2,1,0:T(8,128)S(1)}, f32[10,8,128]{2,1,0:T(8,128)S(1)}, u32[]{:S(2)}, u32[]{:S(2)}) %collective-permute-start.20) | collective-permute-done | bytes 40992 | tf_op jit(solution)/shard_map/ppermute | solution.py:588
  66.4 3.2 %collective-permute-done.19.second_ref = f32[10,8,128]{2,1,0:T(8,128)S(1)} collective-permute-done((f32[10,8,128]{2,1,0:T(8,128)S(1)}, f32[10,8,128]{2,1,0:T(8,128)S(1)}, u32[]{:S(2)}, u32[]{:S(2)}) %collective-permute-start.19) | collective-permute-done | bytes 40992 | tf_op jit(solution)/shard_map/ppermute | solution.py:588
  69.7 0.1 collective-permute-start.21
  69.8 1.3 %collective-permute-done.21.other_ref = f32[30,8,128]{2,1,0:T(8,128)S(1)} collective-permute-done((f32[30,8,128]{2,1,0:T(8,128)S(1)}, f32[30,8,128]{2,1,0:T(8,128)S(1)}, u32[]{:S(2)}, u32[]{:S(2)}) %collective-permute-start.21) | collective-permute-done | bytes 122912 | tf_op jit(solution)/shard_map/ppermute | solution.py:588
  71.1 1.4 %correct.3 = (f32[100,8,128]{2,1,0:T(8,128)S(1)}, f32[100,8,128]{2,1,0:T(8,128)S(1)}, f32[17,8,128]{2,1,0:T(8,128)S(1)}, f32[17,8,128]{2,1,0:T(8,128)S(1)}) custom-call(f32[18,8,128]{2,1,0:T(8,128)S(1)} %broadcast_in_dim.17.marks, f32[100,8,128]{2,1,0:T(8,128)S(1)} %get-tuple-element.93.u_ref, f32[100,8,128]{2,1,0:T(8,128)S(1)} %get-tuple-element.94.y_ref, ...), custom_call_target="tpu_custom_call" | custom-call | tf_op jit(solution)/shard_map/correct/pallas_call | solution.py:536
  72.5 0.2 collective-permute-start.22
  72.7 3.5 %collective-permute-start.23 = (f32[17,8,128]{2,1,0:T(8,128)S(1)}, f32[17,8,128]{2,1,0:T(8,128)S(1)}, u32[]{:S(2)}, u32[]{:S(2)}) collective-permute-start(f32[17,8,128]{2,1,0:T(8,128)S(1)} %get-tuple-element.105), channel_id=1, source_target_pairs={{0,128},{1,2},{2,1},{3,4},{4,3},{5,6},{6,5},{7,14},{14,7},{15,12},... | collective-permute-start | bytes 208904 | tf_op jit(solution)/shard_map/ppermute | solution.py:588
  76.3 0.2 inner.9
  76.5 1.8 %collective-permute-done.23.gb_ref = f32[17,8,128]{2,1,0:T(8,128)S(1)} collective-permute-done((f32[17,8,128]{2,1,0:T(8,128)S(1)}, f32[17,8,128]{2,1,0:T(8,128)S(1)}, u32[]{:S(2)}, u32[]{:S(2)}) %collective-permute-start.23) | collective-permute-done | bytes 69664 | tf_op jit(solution)/shard_map/ppermute | solution.py:588
  78.2 0.4 last.1
  78.7 1.9 %collective-permute-start.26 = (f32[17,8,128]{2,1,0:T(8,128)S(1)}, f32[17,8,128]{2,1,0:T(8,128)S(1)}, u32[]{:S(2)}, u32[]{:S(2)}) collective-permute-start(f32[17,8,128]{2,1,0:T(8,128)S(1)} %get-tuple-element.109), channel_id=1, source_target_pairs={{0,128},{1,2},{2,1},{3,4},{4,3},{5,6},{6,5},{7,14},{14,7},{15,12},... | collective-permute-start | bytes 208904 | tf_op jit(solution)/shard_map/ppermute | solution.py:588
  80.6 1.9 %collective-permute-start.24 = (f32[328,128]{1,0:T(8,128)S(1)}, f32[328,128]{1,0:T(8,128)S(1)}, u32[]{:S(2)}, u32[]{:S(2)}) collective-permute-start(f32[328,128]{1,0:T(8,128)S(1)} %get-tuple-element.106), channel_id=1, source_target_pairs={{0,0},{1,1},{2,2},{3,3},{4,4},{5,5},{6,6},{7,7},{14,8},{15,9},{12,... | collective-permute-start | bytes 503816 | tf_op jit(solution)/shard_map/ppermute | solution.py:588
  82.6 0.2 residual.1
  82.8 1.9 %collective-permute-start.27 = (f32[328,128]{1,0:T(8,128)S(1)}, f32[328,128]{1,0:T(8,128)S(1)}, u32[]{:S(2)}, u32[]{:S(2)}) collective-permute-start(f32[328,128]{1,0:T(8,128)S(1)} %residual.1), channel_id=1, source_target_pairs={{0,0},{1,1},{2,2},{3,3},{4,4},{5,5},{6,6},{7,7},{14,8},{15,9},{12,... | collective-permute-start | bytes 503816 | tf_op jit(solution)/shard_map/ppermute | solution.py:588
  84.7 4.4 %collective-permute-done.24.half_ref = f32[328,128]{1,0:T(8,128)S(1)} collective-permute-done((f32[328,128]{1,0:T(8,128)S(1)}, f32[328,128]{1,0:T(8,128)S(1)}, u32[]{:S(2)}, u32[]{:S(2)}) %collective-permute-start.24) | collective-permute-done | bytes 167968 | tf_op jit(solution)/shard_map/ppermute | solution.py:588
  89.2 0.1 spread.2
  89.3 0.8 reshape.20
  90.1 2.6 %collective-permute-done.27.half_ref = f32[328,128]{1,0:T(8,128)S(1)} collective-permute-done((f32[328,128]{1,0:T(8,128)S(1)}, f32[328,128]{1,0:T(8,128)S(1)}, u32[]{:S(2)}, u32[]{:S(2)}) %collective-permute-start.27) | collective-permute-done | bytes 167968 | tf_op jit(solution)/shard_map/ppermute | solution.py:588
  92.7 0.1 spread.3
  92.8 0.8 reshape.21
  (25 shorter events, 0.5 us)
Async XLA Ops:
  0.6 1.0 %copy-start.1 = (s32[4,1,128]{2,1,0:T(1,128)S(1)}, s32[4,1,128]{2,1,0:T(1,128)}, u32[]{:S(2)}) copy-start(s32[4,1,128]{2,1,0:T(1,128)} %param.6) | copy-start | bytes 6148
  1.6 0.7 copy-start
  2.5 13.6 %collective-permute-start.1 = (f32[328,128]{1,0:T(8,128)S(1)}, f32[328,128]{1,0:T(8,128)S(1)}, u32[]{:S(2)}, u32[]{:S(2)}) collective-permute-start(f32[328,128]{1,0:T(8,128)S(1)} %pack.1), channel_id=1, source_target_pairs={{0,128},{1,129},{2,130},{3,131},{4,132},{5,133},{6,134},{7,135},{8... | collective-permute-start | bytes 503816 | tf_op jit(solution)/shard_map/ppermute | solution.py:588
  9.9 9.7 %collective-permute-start = (f32[328,128]{1,0:T(8,128)S(1)}, f32[328,128]{1,0:T(8,128)S(1)}, u32[]{:S(2)}, u32[]{:S(2)}) collective-permute-start(f32[328,128]{1,0:T(8,128)S(1)} %pack.1), channel_id=1, source_target_pairs={{0,0},{1,1},{2,2},{3,3},{4,4},{5,5},{6,6},{7,7},{8,14},{9,15},{10,... | collective-permute-start | bytes 503816 | tf_op jit(solution)/shard_map/ppermute | solution.py:588
  19.9 1.3 %collective-permute-start.2 = (f32[18,8,128]{2,1,0:T(8,128)S(1)}, f32[18,8,128]{2,1,0:T(8,128)S(1)}, u32[]{:S(2)}, u32[]{:S(2)}) collective-permute-start(f32[18,8,128]{2,1,0:T(8,128)S(1)} %get-tuple-element.58), channel_id=1, source_target_pairs={{0,1},{1,0},{2,3},{3,2},{4,5},{5,4},{6,7},{7,6},{14,15},{15,14},{1... | collective-permute-start | bytes 221192 | tf_op jit(solution)/shard_map/ppermute | solution.py:588
  20.0 3.9 %collective-permute-start.3 = (f32[18,8,128]{2,1,0:T(8,128)S(1)}, f32[18,8,128]{2,1,0:T(8,128)S(1)}, u32[]{:S(2)}, u32[]{:S(2)}) collective-permute-start(f32[18,8,128]{2,1,0:T(8,128)S(1)} %get-tuple-element.59), channel_id=1, source_target_pairs={{0,128},{1,2},{2,1},{3,4},{4,3},{5,6},{6,5},{7,14},{14,7},{15,12},... | collective-permute-start | bytes 221192 | tf_op jit(solution)/shard_map/ppermute | solution.py:588
  24.4 1.4 %collective-permute-start.4 = (f32[17,8,128]{2,1,0:T(8,128)S(1)}, f32[17,8,128]{2,1,0:T(8,128)S(1)}, u32[]{:S(2)}, u32[]{:S(2)}) collective-permute-start(f32[17,8,128]{2,1,0:T(8,128)S(1)} %get-tuple-element.66), channel_id=1, source_target_pairs={{0,1},{1,0},{2,3},{3,2},{4,5},{5,4},{6,7},{7,6},{14,15},{15,14},{1... | collective-permute-start | bytes 208904 | tf_op jit(solution)/shard_map/ppermute | solution.py:588
  24.8 3.7 %collective-permute-start.5 = (f32[17,8,128]{2,1,0:T(8,128)S(1)}, f32[17,8,128]{2,1,0:T(8,128)S(1)}, u32[]{:S(2)}, u32[]{:S(2)}) collective-permute-start(f32[17,8,128]{2,1,0:T(8,128)S(1)} %get-tuple-element.67), channel_id=1, source_target_pairs={{0,128},{1,2},{2,1},{3,4},{4,3},{5,6},{6,5},{7,14},{14,7},{15,12},... | collective-permute-start | bytes 208904 | tf_op jit(solution)/shard_map/ppermute | solution.py:588
  29.0 1.4 %collective-permute-start.6 = (f32[22,8,128]{2,1,0:T(8,128)S(1)}, f32[22,8,128]{2,1,0:T(8,128)S(1)}, u32[]{:S(2)}, u32[]{:S(2)}) collective-permute-start(f32[22,8,128]{2,1,0:T(8,128)S(1)} %get-tuple-element.70), channel_id=1, source_target_pairs={{0,1},{1,0},{2,3},{3,2},{4,5},{5,4},{6,7},{7,6},{14,15},{15,14},{1... | collective-permute-start | bytes 270344 | tf_op jit(solution)/shard_map/ppermute | solution.py:588
  30.4 10.0 %collective-permute-start.7 = (f32[27,8,128]{2,1,0:T(8,128)S(1)}, f32[27,8,128]{2,1,0:T(8,128)S(1)}, u32[]{:S(2)}, u32[]{:S(2)}) collective-permute-start(f32[27,8,128]{2,1,0:T(8,128)S(1)} %get-tuple-element.73), channel_id=1, source_target_pairs={{0,128},{1,2},{2,1},{3,4},{4,3},{5,6},{6,5},{7,14},{14,7},{15,12},... | collective-permute-start | bytes 331784 | tf_op jit(solution)/shard_map/ppermute | solution.py:588
  30.9 6.3 %collective-permute-start.9 = (f32[10,8,128]{2,1,0:T(8,128)S(1)}, f32[10,8,128]{2,1,0:T(8,128)S(1)}, u32[]{:S(2)}, u32[]{:S(2)}) collective-permute-start(f32[10,8,128]{2,1,0:T(8,128)S(1)} %get-tuple-element.74.chip_ref), channel_id=1, source_target_pairs={{0,128},{1,6},{2,130},{3,14},{4,132},{5,12},{6,1},{7,10},{14,3},{1... | collective-permute-start | bytes 122888 | tf_op jit(solution)/shard_map/ppermute | solution.py:588
  35.5 4.9 %collective-permute-start.8 = (f32[10,8,128]{2,1,0:T(8,128)S(1)}, f32[10,8,128]{2,1,0:T(8,128)S(1)}, u32[]{:S(2)}, u32[]{:S(2)}) collective-permute-start(f32[10,8,128]{2,1,0:T(8,128)S(1)} %get-tuple-element.74.chip_ref), channel_id=1, source_target_pairs={{0,128},{1,4},{2,130},{3,6},{4,1},{5,14},{6,3},{7,12},{14,5},{15,1... | collective-permute-start | bytes 122888 | tf_op jit(solution)/shard_map/ppermute | solution.py:588
  40.4 1.4 %collective-permute-start.10 = (f32[30,8,128]{2,1,0:T(8,128)S(1)}, f32[30,8,128]{2,1,0:T(8,128)S(1)}, u32[]{:S(2)}, u32[]{:S(2)}) collective-permute-start(f32[30,8,128]{2,1,0:T(8,128)S(1)} %side.2.mine_ref), channel_id=1, source_target_pairs={{0,1},{1,0},{2,3},{3,2},{4,5},{5,4},{6,7},{7,6},{14,15},{15,14},{1... | collective-permute-start | bytes 368648 | tf_op jit(solution)/shard_map/ppermute | solution.py:588
  43.2 3.8 %collective-permute-start.11 = (f32[17,8,128]{2,1,0:T(8,128)S(1)}, f32[17,8,128]{2,1,0:T(8,128)S(1)}, u32[]{:S(2)}, u32[]{:S(2)}) collective-permute-start(f32[17,8,128]{2,1,0:T(8,128)S(1)} %get-tuple-element.79), channel_id=1, source_target_pairs={{0,1},{1,0},{2,3},{3,2},{4,5},{5,4},{6,7},{7,6},{14,15},{15,14},{1... | collective-permute-start | bytes 208904 | tf_op jit(solution)/shard_map/ppermute | solution.py:588
  43.5 5.3 %collective-permute-start.12 = (f32[17,8,128]{2,1,0:T(8,128)S(1)}, f32[17,8,128]{2,1,0:T(8,128)S(1)}, u32[]{:S(2)}, u32[]{:S(2)}) collective-permute-start(f32[17,8,128]{2,1,0:T(8,128)S(1)} %get-tuple-element.80), channel_id=1, source_target_pairs={{0,128},{1,2},{2,1},{3,4},{4,3},{5,6},{6,5},{7,14},{14,7},{15,12},... | collective-permute-start | bytes 208904 | tf_op jit(solution)/shard_map/ppermute | solution.py:588
  49.2 2.2 %collective-permute-start.13 = (f32[17,8,128]{2,1,0:T(8,128)S(1)}, f32[17,8,128]{2,1,0:T(8,128)S(1)}, u32[]{:S(2)}, u32[]{:S(2)}) collective-permute-start(f32[17,8,128]{2,1,0:T(8,128)S(1)} %get-tuple-element.85), channel_id=1, source_target_pairs={{0,1},{1,0},{2,3},{3,2},{4,5},{5,4},{6,7},{7,6},{14,15},{15,14},{1... | collective-permute-start | bytes 208904 | tf_op jit(solution)/shard_map/ppermute | solution.py:588
  49.2 3.9 %collective-permute-start.14 = (f32[17,8,128]{2,1,0:T(8,128)S(1)}, f32[17,8,128]{2,1,0:T(8,128)S(1)}, u32[]{:S(2)}, u32[]{:S(2)}) collective-permute-start(f32[17,8,128]{2,1,0:T(8,128)S(1)} %get-tuple-element.86), channel_id=1, source_target_pairs={{0,128},{1,2},{2,1},{3,4},{4,3},{5,6},{6,5},{7,14},{14,7},{15,12},... | collective-permute-start | bytes 208904 | tf_op jit(solution)/shard_map/ppermute | solution.py:588
  53.5 2.4 %collective-permute-start.15 = (f32[17,8,128]{2,1,0:T(8,128)S(1)}, f32[17,8,128]{2,1,0:T(8,128)S(1)}, u32[]{:S(2)}, u32[]{:S(2)}) collective-permute-start(f32[17,8,128]{2,1,0:T(8,128)S(1)} %get-tuple-element.91), channel_id=1, source_target_pairs={{0,1},{1,0},{2,3},{3,2},{4,5},{5,4},{6,7},{7,6},{14,15},{15,14},{1... | collective-permute-start | bytes 208904 | tf_op jit(solution)/shard_map/ppermute | solution.py:588
  53.9 3.7 %collective-permute-start.16 = (f32[17,8,128]{2,1,0:T(8,128)S(1)}, f32[17,8,128]{2,1,0:T(8,128)S(1)}, u32[]{:S(2)}, u32[]{:S(2)}) collective-permute-start(f32[17,8,128]{2,1,0:T(8,128)S(1)} %get-tuple-element.92), channel_id=1, source_target_pairs={{0,128},{1,2},{2,1},{3,4},{4,3},{5,6},{6,5},{7,14},{14,7},{15,12},... | collective-permute-start | bytes 208904 | tf_op jit(solution)/shard_map/ppermute | solution.py:588
  58.0 1.4 %collective-permute-start.17 = (f32[22,8,128]{2,1,0:T(8,128)S(1)}, f32[22,8,128]{2,1,0:T(8,128)S(1)}, u32[]{:S(2)}, u32[]{:S(2)}) collective-permute-start(f32[22,8,128]{2,1,0:T(8,128)S(1)} %get-tuple-element.95), channel_id=1, source_target_pairs={{0,1},{1,0},{2,3},{3,2},{4,5},{5,4},{6,7},{7,6},{14,15},{15,14},{1... | collective-permute-start | bytes 270344 | tf_op jit(solution)/shard_map/ppermute | solution.py:588
  59.4 10.2 %collective-permute-start.18 = (f32[27,8,128]{2,1,0:T(8,128)S(1)}, f32[27,8,128]{2,1,0:T(8,128)S(1)}, u32[]{:S(2)}, u32[]{:S(2)}) collective-permute-start(f32[27,8,128]{2,1,0:T(8,128)S(1)} %get-tuple-element.98), channel_id=1, source_target_pairs={{0,128},{1,2},{2,1},{3,4},{4,3},{5,6},{6,5},{7,14},{14,7},{15,12},... | collective-permute-start | bytes 331784 | tf_op jit(solution)/shard_map/ppermute | solution.py:588
  61.3 5.2 %collective-permute-start.20 = (f32[10,8,128]{2,1,0:T(8,128)S(1)}, f32[10,8,128]{2,1,0:T(8,128)S(1)}, u32[]{:S(2)}, u32[]{:S(2)}) collective-permute-start(f32[10,8,128]{2,1,0:T(8,128)S(1)} %get-tuple-element.99.chip_ref), channel_id=1, source_target_pairs={{0,128},{1,6},{2,130},{3,14},{4,132},{5,12},{6,1},{7,10},{14,3},{1... | collective-permute-start | bytes 122888 | tf_op jit(solution)/shard_map/ppermute | solution.py:588
  64.7 4.9 %collective-permute-start.19 = (f32[10,8,128]{2,1,0:T(8,128)S(1)}, f32[10,8,128]{2,1,0:T(8,128)S(1)}, u32[]{:S(2)}, u32[]{:S(2)}) collective-permute-start(f32[10,8,128]{2,1,0:T(8,128)S(1)} %get-tuple-element.99.chip_ref), channel_id=1, source_target_pairs={{0,128},{1,4},{2,130},{3,6},{4,1},{5,14},{6,3},{7,12},{14,5},{15,1... | collective-permute-start | bytes 122888 | tf_op jit(solution)/shard_map/ppermute | solution.py:588
  69.7 1.4 %collective-permute-start.21 = (f32[30,8,128]{2,1,0:T(8,128)S(1)}, f32[30,8,128]{2,1,0:T(8,128)S(1)}, u32[]{:S(2)}, u32[]{:S(2)}) collective-permute-start(f32[30,8,128]{2,1,0:T(8,128)S(1)} %side.3.mine_ref), channel_id=1, source_target_pairs={{0,1},{1,0},{2,3},{3,2},{4,5},{5,4},{6,7},{7,6},{14,15},{15,14},{1... | collective-permute-start | bytes 368648 | tf_op jit(solution)/shard_map/ppermute | solution.py:588
  72.5 3.9 %collective-permute-start.22 = (f32[17,8,128]{2,1,0:T(8,128)S(1)}, f32[17,8,128]{2,1,0:T(8,128)S(1)}, u32[]{:S(2)}, u32[]{:S(2)}) collective-permute-start(f32[17,8,128]{2,1,0:T(8,128)S(1)} %get-tuple-element.104), channel_id=1, source_target_pairs={{0,1},{1,0},{2,3},{3,2},{4,5},{5,4},{6,7},{7,6},{14,15},{15,14},{1... | collective-permute-start | bytes 208904 | tf_op jit(solution)/shard_map/ppermute | solution.py:588
  72.7 5.5 %collective-permute-start.23 = (f32[17,8,128]{2,1,0:T(8,128)S(1)}, f32[17,8,128]{2,1,0:T(8,128)S(1)}, u32[]{:S(2)}, u32[]{:S(2)}) collective-permute-start(f32[17,8,128]{2,1,0:T(8,128)S(1)} %get-tuple-element.105), channel_id=1, source_target_pairs={{0,128},{1,2},{2,1},{3,4},{4,3},{5,6},{6,5},{7,14},{14,7},{15,12},... | collective-permute-start | bytes 208904 | tf_op jit(solution)/shard_map/ppermute | solution.py:588
  78.6 3.9 %collective-permute-start.25 = (f32[17,8,128]{2,1,0:T(8,128)S(1)}, f32[17,8,128]{2,1,0:T(8,128)S(1)}, u32[]{:S(2)}, u32[]{:S(2)}) collective-permute-start(f32[17,8,128]{2,1,0:T(8,128)S(1)} %get-tuple-element.108), channel_id=1, source_target_pairs={{0,1},{1,0},{2,3},{3,2},{4,5},{5,4},{6,7},{7,6},{14,15},{15,14},{1... | collective-permute-start | bytes 208904 | tf_op jit(solution)/shard_map/ppermute | solution.py:588
  78.7 3.9 %collective-permute-start.26 = (f32[17,8,128]{2,1,0:T(8,128)S(1)}, f32[17,8,128]{2,1,0:T(8,128)S(1)}, u32[]{:S(2)}, u32[]{:S(2)}) collective-permute-start(f32[17,8,128]{2,1,0:T(8,128)S(1)} %get-tuple-element.109), channel_id=1, source_target_pairs={{0,128},{1,2},{2,1},{3,4},{4,3},{5,6},{6,5},{7,14},{14,7},{15,12},... | collective-permute-start | bytes 208904 | tf_op jit(solution)/shard_map/ppermute | solution.py:588
  80.6 8.6 %collective-permute-start.24 = (f32[328,128]{1,0:T(8,128)S(1)}, f32[328,128]{1,0:T(8,128)S(1)}, u32[]{:S(2)}, u32[]{:S(2)}) collective-permute-start(f32[328,128]{1,0:T(8,128)S(1)} %get-tuple-element.106), channel_id=1, source_target_pairs={{0,0},{1,1},{2,2},{3,3},{4,4},{5,5},{6,6},{7,7},{14,8},{15,9},{12,... | collective-permute-start | bytes 503816 | tf_op jit(solution)/shard_map/ppermute | solution.py:588
  82.8 9.8 %collective-permute-start.27 = (f32[328,128]{1,0:T(8,128)S(1)}, f32[328,128]{1,0:T(8,128)S(1)}, u32[]{:S(2)}, u32[]{:S(2)}) collective-permute-start(f32[328,128]{1,0:T(8,128)S(1)} %residual.1), channel_id=1, source_target_pairs={{0,0},{1,1},{2,2},{3,3},{4,4},{5,5},{6,6},{7,7},{14,8},{15,9},{12,... | collective-permute-start | bytes 503816 | tf_op jit(solution)/shard_map/ppermute | solution.py:588

commit v6 on v5

--- a/solution.py
+++ b/solution.py
@@ -631,6 +631,7 @@
         a, b = trade(a, b)
         y, a, b, half = call("last", last_sweep_kernel, [FIELD, *faces, (328, 128)], [FIELD, *WORK], marks, u, y, f, inv, coeff, *inner(u, y), a, b)
         a, b = trade(a, b)
+        a, b, half = lax.optimization_barrier((a, b, half))
         half = restore(half)
         (left_half,) = call("residual", residual_kernel, [(328, 128)], [FIELD], marks, y, f, a, b)
         (solved,) = call("spread", spread_kernel, [(500, 128)], [], half)

time: 94.7 us -> 97.7 us (1.032)
  waiting for transfers between devices: 39.5 us -> 42.7 us
    ppermute x28, waiting for transfers between devices: 39.5 us -> 42.7 us  [swap(): return lax.ppermute(x, AXES, pairs)]
where the time goes in v6:
time: 97.7 us; the launch traced here: 96.7 us
  waiting for transfers between devices  42.7 us (44%)
  starting transfers between devices  42.4 us (43%)
  Pallas kernels  6.82 us (7%)
  local copies, waits for them, and re-layouts  3.95 us (4%)
    ppermute x28, waiting for transfers between devices, swap(): return lax.ppermute(x, AXES, pairs)  42.7 us
    ppermute x28, starting transfers between devices, swap(): return lax.ppermute(x, AXES, pairs)  42.4 us
    pallas_call x22, Pallas kernels, call(): pl.pallas_call(kernel, out_shape=[jax.ShapeDtypeStruct(s, F32) for s in o...  6.82 us
  transfers between devices with their start and end apart: 28, of which 20 were waited for; matrix products, arithmetic and copies ran while one was open for 2% of the time, Pallas kernels for 1%

profile of v6, /device:TPU:2, one launch (start us, length us, event | category | flops | bytes accessed | tf_op | source)
XLA Modules:
  0.0 96.7 jit_solution(4881278445325038649)
XLA Ops:
  0.6 1.0 %copy.12 = f32[500,1,128]{2,0,1:T(8,128)S(1)} copy(f32[500,1,128]{2,1,0:T(1,128)} %bitcast.9) | data formatting | bytes 512000 | tf_op jit(solution)/shard_map/reshape | solution.py:597
  1.6 0.7 copy-done
  2.3 0.1 pack.1
  2.5 7.5 %collective-permute-start.1 = (f32[328,128]{1,0:T(8,128)S(1)}, f32[328,128]{1,0:T(8,128)S(1)}, u32[]{:S(2)}, u32[]{:S(2)}) collective-permute-start(f32[328,128]{1,0:T(8,128)S(1)} %pack.1), channel_id=1, source_target_pairs={{0,128},{1,129},{2,130},{3,131},{4,132},{5,133},{6,134},{7,135},{8... | collective-permute-start | bytes 503816 | tf_op jit(solution)/shard_map/ppermute | solution.py:588
  9.9 5.4 %collective-permute-start = (f32[328,128]{1,0:T(8,128)S(1)}, f32[328,128]{1,0:T(8,128)S(1)}, u32[]{:S(2)}, u32[]{:S(2)}) collective-permute-start(f32[328,128]{1,0:T(8,128)S(1)} %pack.1), channel_id=1, source_target_pairs={{0,0},{1,1},{2,2},{3,3},{4,4},{5,5},{6,6},{7,7},{8,14},{9,15},{10,... | collective-permute-start | bytes 503816 | tf_op jit(solution)/shard_map/ppermute | solution.py:588
  15.3 0.7 dynamic-slice_bitcast_fusion
  16.0 3.7 %collective-permute-done.same_ref = f32[328,128]{1,0:T(8,128)S(1)} collective-permute-done((f32[328,128]{1,0:T(8,128)S(1)}, f32[328,128]{1,0:T(8,128)S(1)}, u32[]{:S(2)}, u32[]{:S(2)}) %collective-permute-start) | collective-permute-done | bytes 167968 | tf_op jit(solution)/shard_map/ppermute | solution.py:588
  19.8 0.2 unpack.1
  20.0 0.5 collective-permute-start.3
  20.4 0.8 collective-permute-done.2.ga_ref
  21.2 2.6 %collective-permute-done.3.gb_ref = f32[18,8,128]{2,1,0:T(8,128)S(1)} collective-permute-done((f32[18,8,128]{2,1,0:T(8,128)S(1)}, f32[18,8,128]{2,1,0:T(8,128)S(1)}, u32[]{:S(2)}, u32[]{:S(2)}) %collective-permute-start.3) | collective-permute-done | bytes 73760 | tf_op jit(solution)/shard_map/ppermute | solution.py:588
  23.8 0.5 first.1
  24.4 0.5 collective-permute-start.4
  24.9 0.2 inner.5
  25.1 0.7 collective-permute-done.4.ga_ref
  25.8 2.8 %collective-permute-done.5.gb_ref = f32[17,8,128]{2,1,0:T(8,128)S(1)} collective-permute-done((f32[17,8,128]{2,1,0:T(8,128)S(1)}, f32[17,8,128]{2,1,0:T(8,128)S(1)}, u32[]{:S(2)}, u32[]{:S(2)}) %collective-permute-start.5) | collective-permute-done | bytes 69664 | tf_op jit(solution)/shard_map/ppermute | solution.py:588
  28.6 0.4 restrict.2
  29.0 0.2 collective-permute-start.6
  29.2 1.2 %collective-permute-done.6.ga_ref = f32[22,8,128]{2,1,0:T(8,128)S(1)} collective-permute-done((f32[22,8,128]{2,1,0:T(8,128)S(1)}, f32[22,8,128]{2,1,0:T(8,128)S(1)}, u32[]{:S(2)}, u32[]{:S(2)}) %collective-permute-start.6) | collective-permute-done | bytes 90144 | tf_op jit(solution)/shard_map/ppermute | solution.py:588
  30.4 0.5 collective-permute-start.7
  30.9 4.6 %collective-permute-start.9 = (f32[10,8,128]{2,1,0:T(8,128)S(1)}, f32[10,8,128]{2,1,0:T(8,128)S(1)}, u32[]{:S(2)}, u32[]{:S(2)}) collective-permute-start(f32[10,8,128]{2,1,0:T(8,128)S(1)} %get-tuple-element.77.chip_ref), channel_id=1, source_target_pairs={{0,128},{1,6},{2,130},{3,14},{4,132},{5,12},{6,1},{7,10},{14,3},{1... | collective-permute-start | bytes 122888 | tf_op jit(solution)/shard_map/ppermute | solution.py:588
  35.5 1.7 %collective-permute-done.9.third_ref = f32[10,8,128]{2,1,0:T(8,128)S(1)} collective-permute-done((f32[10,8,128]{2,1,0:T(8,128)S(1)}, f32[10,8,128]{2,1,0:T(8,128)S(1)}, u32[]{:S(2)}, u32[]{:S(2)}) %collective-permute-start.9) | collective-permute-done | bytes 40992 | tf_op jit(solution)/shard_map/ppermute | solution.py:588
  37.2 3.2 %collective-permute-done.8.second_ref = f32[10,8,128]{2,1,0:T(8,128)S(1)} collective-permute-done((f32[10,8,128]{2,1,0:T(8,128)S(1)}, f32[10,8,128]{2,1,0:T(8,128)S(1)}, u32[]{:S(2)}, u32[]{:S(2)}) %collective-permute-start.8) | collective-permute-done | bytes 40992 | tf_op jit(solution)/shard_map/ppermute | solution.py:588
  40.4 0.1 collective-permute-start.10
  40.5 1.3 %collective-permute-done.10.other_ref = f32[30,8,128]{2,1,0:T(8,128)S(1)} collective-permute-done((f32[30,8,128]{2,1,0:T(8,128)S(1)}, f32[30,8,128]{2,1,0:T(8,128)S(1)}, u32[]{:S(2)}, u32[]{:S(2)}) %collective-permute-start.10) | collective-permute-done | bytes 122912 | tf_op jit(solution)/shard_map/ppermute | solution.py:588
  41.8 1.4 %correct.2 = (f32[100,8,128]{2,1,0:T(8,128)S(1)}, f32[100,8,128]{2,1,0:T(8,128)S(1)}, f32[17,8,128]{2,1,0:T(8,128)S(1)}, f32[17,8,128]{2,1,0:T(8,128)S(1)}) custom-call(f32[18,8,128]{2,1,0:T(8,128)S(1)} %broadcast_in_dim.17.marks, f32[100,8,128]{2,1,0:T(8,128)S(1)} %get-tuple-element.71.u_ref, f32[100,8,128]{2,1,0:T(8,128)S(1)} %get-tuple-element.72.y_ref, ...), custom_call_target="tpu_custom_call" | custom-call | tf_op jit(solution)/shard_map/correct/pallas_call | solution.py:536
  43.2 0.2 collective-permute-start.11
  43.5 3.4 %collective-permute-start.12 = (f32[17,8,128]{2,1,0:T(8,128)S(1)}, f32[17,8,128]{2,1,0:T(8,128)S(1)}, u32[]{:S(2)}, u32[]{:S(2)}) collective-permute-start(f32[17,8,128]{2,1,0:T(8,128)S(1)} %get-tuple-element.83), channel_id=1, source_target_pairs={{0,128},{1,2},{2,1},{3,4},{4,3},{5,6},{6,5},{7,14},{14,7},{15,12},... | collective-permute-start | bytes 208904 | tf_op jit(solution)/shard_map/ppermute | solution.py:588
  46.8 0.2 inner.6
  47.0 1.8 %collective-permute-done.12.gb_ref = f32[17,8,128]{2,1,0:T(8,128)S(1)} collective-permute-done((f32[17,8,128]{2,1,0:T(8,128)S(1)}, f32[17,8,128]{2,1,0:T(8,128)S(1)}, u32[]{:S(2)}, u32[]{:S(2)}) %collective-permute-start.12) | collective-permute-done | bytes 69664 | tf_op jit(solution)/shard_map/ppermute | solution.py:588
  48.8 0.3 sweep.2
  49.2 1.9 %collective-permute-start.14 = (f32[17,8,128]{2,1,0:T(8,128)S(1)}, f32[17,8,128]{2,1,0:T(8,128)S(1)}, u32[]{:S(2)}, u32[]{:S(2)}) collective-permute-start(f32[17,8,128]{2,1,0:T(8,128)S(1)} %get-tuple-element.89), channel_id=1, source_target_pairs={{0,128},{1,2},{2,1},{3,4},{4,3},{5,6},{6,5},{7,14},{14,7},{15,12},... | collective-permute-start | bytes 208904 | tf_op jit(solution)/shard_map/ppermute | solution.py:588
  51.1 0.2 inner.7
  51.3 1.8 %collective-permute-done.14.gb_ref = f32[17,8,128]{2,1,0:T(8,128)S(1)} collective-permute-done((f32[17,8,128]{2,1,0:T(8,128)S(1)}, f32[17,8,128]{2,1,0:T(8,128)S(1)}, u32[]{:S(2)}, u32[]{:S(2)}) %collective-permute-start.14) | collective-permute-done | bytes 69664 | tf_op jit(solution)/shard_map/ppermute | solution.py:588
  53.1 0.3 sweep.3
  53.5 0.4 collective-permute-start.15
  53.9 1.7 %collective-permute-start.16 = (f32[17,8,128]{2,1,0:T(8,128)S(1)}, f32[17,8,128]{2,1,0:T(8,128)S(1)}, u32[]{:S(2)}, u32[]{:S(2)}) collective-permute-start(f32[17,8,128]{2,1,0:T(8,128)S(1)} %get-tuple-element.95), channel_id=1, source_target_pairs={{0,128},{1,2},{2,1},{3,4},{4,3},{5,6},{6,5},{7,14},{14,7},{15,12},... | collective-permute-start | bytes 208904 | tf_op jit(solution)/shard_map/ppermute | solution.py:588
  55.6 0.2 inner.8
  55.8 1.8 %collective-permute-done.16.gb_ref = f32[17,8,128]{2,1,0:T(8,128)S(1)} collective-permute-done((f32[17,8,128]{2,1,0:T(8,128)S(1)}, f32[17,8,128]{2,1,0:T(8,128)S(1)}, u32[]{:S(2)}, u32[]{:S(2)}) %collective-permute-start.16) | collective-permute-done | bytes 69664 | tf_op jit(solution)/shard_map/ppermute | solution.py:588
  57.6 0.4 restrict.3
  58.0 0.4 collective-permute-start.17
  58.4 1.0 %collective-permute-done.17.ga_ref = f32[22,8,128]{2,1,0:T(8,128)S(1)} collective-permute-done((f32[22,8,128]{2,1,0:T(8,128)S(1)}, f32[22,8,128]{2,1,0:T(8,128)S(1)}, u32[]{:S(2)}, u32[]{:S(2)}) %collective-permute-start.17) | collective-permute-done | bytes 90144 | tf_op jit(solution)/shard_map/ppermute | solution.py:588
  59.4 1.8 %collective-permute-start.18 = (f32[27,8,128]{2,1,0:T(8,128)S(1)}, f32[27,8,128]{2,1,0:T(8,128)S(1)}, u32[]{:S(2)}, u32[]{:S(2)}) collective-permute-start(f32[27,8,128]{2,1,0:T(8,128)S(1)} %get-tuple-element.101), channel_id=1, source_target_pairs={{0,128},{1,2},{2,1},{3,4},{4,3},{5,6},{6,5},{7,14},{14,7},{15,12},... | collective-permute-start | bytes 331784 | tf_op jit(solution)/shard_map/ppermute | solution.py:588
  61.3 3.5 %collective-permute-start.20 = (f32[10,8,128]{2,1,0:T(8,128)S(1)}, f32[10,8,128]{2,1,0:T(8,128)S(1)}, u32[]{:S(2)}, u32[]{:S(2)}) collective-permute-start(f32[10,8,128]{2,1,0:T(8,128)S(1)} %get-tuple-element.102.chip_ref), channel_id=1, source_target_pairs={{0,128},{1,6},{2,130},{3,14},{4,132},{5,12},{6,1},{7,10},{14,3},{1... | collective-permute-start | bytes 122888 | tf_op jit(solution)/shard_map/ppermute | solution.py:588
  64.7 1.7 %collective-permute-done.20.third_ref = f32[10,8,128]{2,1,0:T(8,128)S(1)} collective-permute-done((f32[10,8,128]{2,1,0:T(8,128)S(1)}, f32[10,8,128]{2,1,0:T(8,128)S(1)}, u32[]{:S(2)}, u32[]{:S(2)}) %collective-permute-start.20) | collective-permute-done | bytes 40992 | tf_op jit(solution)/shard_map/ppermute | solution.py:588
  66.4 3.2 %collective-permute-done.19.second_ref = f32[10,8,128]{2,1,0:T(8,128)S(1)} collective-permute-done((f32[10,8,128]{2,1,0:T(8,128)S(1)}, f32[10,8,128]{2,1,0:T(8,128)S(1)}, u32[]{:S(2)}, u32[]{:S(2)}) %collective-permute-start.19) | collective-permute-done | bytes 40992 | tf_op jit(solution)/shard_map/ppermute | solution.py:588
  69.8 1.3 %collective-permute-done.21.other_ref = f32[30,8,128]{2,1,0:T(8,128)S(1)} collective-permute-done((f32[30,8,128]{2,1,0:T(8,128)S(1)}, f32[30,8,128]{2,1,0:T(8,128)S(1)}, u32[]{:S(2)}, u32[]{:S(2)}) %collective-permute-start.21) | collective-permute-done | bytes 122912 | tf_op jit(solution)/shard_map/ppermute | solution.py:588
  71.1 1.4 %correct.3 = (f32[100,8,128]{2,1,0:T(8,128)S(1)}, f32[100,8,128]{2,1,0:T(8,128)S(1)}, f32[17,8,128]{2,1,0:T(8,128)S(1)}, f32[17,8,128]{2,1,0:T(8,128)S(1)}) custom-call(f32[18,8,128]{2,1,0:T(8,128)S(1)} %broadcast_in_dim.17.marks, f32[100,8,128]{2,1,0:T(8,128)S(1)} %get-tuple-element.96.u_ref, f32[100,8,128]{2,1,0:T(8,128)S(1)} %get-tuple-element.97.y_ref, ...), custom_call_target="tpu_custom_call" | custom-call | tf_op jit(solution)/shard_map/correct/pallas_call | solution.py:536
  72.5 0.2 collective-permute-start.22
  72.7 3.5 %collective-permute-start.23 = (f32[17,8,128]{2,1,0:T(8,128)S(1)}, f32[17,8,128]{2,1,0:T(8,128)S(1)}, u32[]{:S(2)}, u32[]{:S(2)}) collective-permute-start(f32[17,8,128]{2,1,0:T(8,128)S(1)} %get-tuple-element.108), channel_id=1, source_target_pairs={{0,128},{1,2},{2,1},{3,4},{4,3},{5,6},{6,5},{7,14},{14,7},{15,12},... | collective-permute-start | bytes 208904 | tf_op jit(solution)/shard_map/ppermute | solution.py:588
  76.3 0.2 inner.9
  76.5 1.8 %collective-permute-done.23.gb_ref = f32[17,8,128]{2,1,0:T(8,128)S(1)} collective-permute-done((f32[17,8,128]{2,1,0:T(8,128)S(1)}, f32[17,8,128]{2,1,0:T(8,128)S(1)}, u32[]{:S(2)}, u32[]{:S(2)}) %collective-permute-start.23) | collective-permute-done | bytes 69664 | tf_op jit(solution)/shard_map/ppermute | solution.py:588
  78.2 0.4 last.1
  78.7 1.9 %collective-permute-start.25 = (f32[17,8,128]{2,1,0:T(8,128)S(1)}, f32[17,8,128]{2,1,0:T(8,128)S(1)}, u32[]{:S(2)}, u32[]{:S(2)}) collective-permute-start(f32[17,8,128]{2,1,0:T(8,128)S(1)} %get-tuple-element.110), channel_id=1, source_target_pairs={{0,128},{1,2},{2,1},{3,4},{4,3},{5,6},{6,5},{7,14},{14,7},{15,12},... | collective-permute-start | bytes 208904 | tf_op jit(solution)/shard_map/ppermute | solution.py:588
  80.6 2.0 %collective-permute-done.25.gb_ref = f32[17,8,128]{2,1,0:T(8,128)S(1)} collective-permute-done((f32[17,8,128]{2,1,0:T(8,128)S(1)}, f32[17,8,128]{2,1,0:T(8,128)S(1)}, u32[]{:S(2)}, u32[]{:S(2)}) %collective-permute-start.25) | collective-permute-done | bytes 69664 | tf_op jit(solution)/shard_map/ppermute | solution.py:588
  82.6 1.9 %collective-permute-start.26 = (f32[328,128]{1,0:T(8,128)S(1)}, f32[328,128]{1,0:T(8,128)S(1)}, u32[]{:S(2)}, u32[]{:S(2)}) collective-permute-start(f32[328,128]{1,0:T(8,128)S(1)} %get-tuple-element.112), channel_id=1, source_target_pairs={{0,0},{1,1},{2,2},{3,3},{4,4},{5,5},{6,6},{7,7},{14,8},{15,9},{12,... | collective-permute-start | bytes 503816 | tf_op jit(solution)/shard_map/ppermute | solution.py:588
  84.5 0.2 residual.1
  84.7 1.9 %collective-permute-start.27 = (f32[328,128]{1,0:T(8,128)S(1)}, f32[328,128]{1,0:T(8,128)S(1)}, u32[]{:S(2)}, u32[]{:S(2)}) collective-permute-start(f32[328,128]{1,0:T(8,128)S(1)} %residual.1), channel_id=1, source_target_pairs={{0,0},{1,1},{2,2},{3,3},{4,4},{5,5},{6,6},{7,7},{14,8},{15,9},{12,... | collective-permute-start | bytes 503816 | tf_op jit(solution)/shard_map/ppermute | solution.py:588
  86.7 6.1 %collective-permute-done.26.half_ref = f32[328,128]{1,0:T(8,128)S(1)} collective-permute-done((f32[328,128]{1,0:T(8,128)S(1)}, f32[328,128]{1,0:T(8,128)S(1)}, u32[]{:S(2)}, u32[]{:S(2)}) %collective-permute-start.26) | collective-permute-done | bytes 167968 | tf_op jit(solution)/shard_map/ppermute | solution.py:588
  92.8 0.1 spread.2
  92.9 0.8 reshape.20
  93.7 2.1 %collective-permute-done.27.half_ref = f32[328,128]{1,0:T(8,128)S(1)} collective-permute-done((f32[328,128]{1,0:T(8,128)S(1)}, f32[328,128]{1,0:T(8,128)S(1)}, u32[]{:S(2)}, u32[]{:S(2)}) %collective-permute-start.27) | collective-permute-done | bytes 167968 | tf_op jit(solution)/shard_map/ppermute | solution.py:588
  95.8 0.1 spread.3
  96.0 0.8 reshape.21
  (25 shorter events, 0.6 us)
Async XLA Ops:
  0.6 1.0 %copy-start.1 = (s32[4,1,128]{2,1,0:T(1,128)S(1)}, s32[4,1,128]{2,1,0:T(1,128)}, u32[]{:S(2)}) copy-start(s32[4,1,128]{2,1,0:T(1,128)} %param.6) | copy-start | bytes 6148
  1.6 0.7 copy-start
  2.5 13.6 %collective-permute-start.1 = (f32[328,128]{1,0:T(8,128)S(1)}, f32[328,128]{1,0:T(8,128)S(1)}, u32[]{:S(2)}, u32[]{:S(2)}) collective-permute-start(f32[328,128]{1,0:T(8,128)S(1)} %pack.1), channel_id=1, source_target_pairs={{0,128},{1,129},{2,130},{3,131},{4,132},{5,133},{6,134},{7,135},{8... | collective-permute-start | bytes 503816 | tf_op jit(solution)/shard_map/ppermute | solution.py:588
  9.9 9.7 %collective-permute-start = (f32[328,128]{1,0:T(8,128)S(1)}, f32[328,128]{1,0:T(8,128)S(1)}, u32[]{:S(2)}, u32[]{:S(2)}) collective-permute-start(f32[328,128]{1,0:T(8,128)S(1)} %pack.1), channel_id=1, source_target_pairs={{0,0},{1,1},{2,2},{3,3},{4,4},{5,5},{6,6},{7,7},{8,14},{9,15},{10,... | collective-permute-start | bytes 503816 | tf_op jit(solution)/shard_map/ppermute | solution.py:588
  19.9 1.3 %collective-permute-start.2 = (f32[18,8,128]{2,1,0:T(8,128)S(1)}, f32[18,8,128]{2,1,0:T(8,128)S(1)}, u32[]{:S(2)}, u32[]{:S(2)}) collective-permute-start(f32[18,8,128]{2,1,0:T(8,128)S(1)} %get-tuple-element.61), channel_id=1, source_target_pairs={{0,1},{1,0},{2,3},{3,2},{4,5},{5,4},{6,7},{7,6},{14,15},{15,14},{1... | collective-permute-start | bytes 221192 | tf_op jit(solution)/shard_map/ppermute | solution.py:588
  20.0 3.9 %collective-permute-start.3 = (f32[18,8,128]{2,1,0:T(8,128)S(1)}, f32[18,8,128]{2,1,0:T(8,128)S(1)}, u32[]{:S(2)}, u32[]{:S(2)}) collective-permute-start(f32[18,8,128]{2,1,0:T(8,128)S(1)} %get-tuple-element.62), channel_id=1, source_target_pairs={{0,128},{1,2},{2,1},{3,4},{4,3},{5,6},{6,5},{7,14},{14,7},{15,12},... | collective-permute-start | bytes 221192 | tf_op jit(solution)/shard_map/ppermute | solution.py:588
  24.4 1.4 %collective-permute-start.4 = (f32[17,8,128]{2,1,0:T(8,128)S(1)}, f32[17,8,128]{2,1,0:T(8,128)S(1)}, u32[]{:S(2)}, u32[]{:S(2)}) collective-permute-start(f32[17,8,128]{2,1,0:T(8,128)S(1)} %get-tuple-element.69), channel_id=1, source_target_pairs={{0,1},{1,0},{2,3},{3,2},{4,5},{5,4},{6,7},{7,6},{14,15},{15,14},{1... | collective-permute-start | bytes 208904 | tf_op jit(solution)/shard_map/ppermute | solution.py:588
  24.8 3.7 %collective-permute-start.5 = (f32[17,8,128]{2,1,0:T(8,128)S(1)}, f32[17,8,128]{2,1,0:T(8,128)S(1)}, u32[]{:S(2)}, u32[]{:S(2)}) collective-permute-start(f32[17,8,128]{2,1,0:T(8,128)S(1)} %get-tuple-element.70), channel_id=1, source_target_pairs={{0,128},{1,2},{2,1},{3,4},{4,3},{5,6},{6,5},{7,14},{14,7},{15,12},... | collective-permute-start | bytes 208904 | tf_op jit(solution)/shard_map/ppermute | solution.py:588
  29.0 1.4 %collective-permute-start.6 = (f32[22,8,128]{2,1,0:T(8,128)S(1)}, f32[22,8,128]{2,1,0:T(8,128)S(1)}, u32[]{:S(2)}, u32[]{:S(2)}) collective-permute-start(f32[22,8,128]{2,1,0:T(8,128)S(1)} %get-tuple-element.73), channel_id=1, source_target_pairs={{0,1},{1,0},{2,3},{3,2},{4,5},{5,4},{6,7},{7,6},{14,15},{15,14},{1... | collective-permute-start | bytes 270344 | tf_op jit(solution)/shard_map/ppermute | solution.py:588
  30.4 10.0 %collective-permute-start.7 = (f32[27,8,128]{2,1,0:T(8,128)S(1)}, f32[27,8,128]{2,1,0:T(8,128)S(1)}, u32[]{:S(2)}, u32[]{:S(2)}) collective-permute-start(f32[27,8,128]{2,1,0:T(8,128)S(1)} %get-tuple-element.76), channel_id=1, source_target_pairs={{0,128},{1,2},{2,1},{3,4},{4,3},{5,6},{6,5},{7,14},{14,7},{15,12},... | collective-permute-start | bytes 331784 | tf_op jit(solution)/shard_map/ppermute | solution.py:588
  30.9 6.3 %collective-permute-start.9 = (f32[10,8,128]{2,1,0:T(8,128)S(1)}, f32[10,8,128]{2,1,0:T(8,128)S(1)}, u32[]{:S(2)}, u32[]{:S(2)}) collective-permute-start(f32[10,8,128]{2,1,0:T(8,128)S(1)} %get-tuple-element.77.chip_ref), channel_id=1, source_target_pairs={{0,128},{1,6},{2,130},{3,14},{4,132},{5,12},{6,1},{7,10},{14,3},{1... | collective-permute-start | bytes 122888 | tf_op jit(solution)/shard_map/ppermute | solution.py:588
  35.5 4.9 %collective-permute-start.8 = (f32[10,8,128]{2,1,0:T(8,128)S(1)}, f32[10,8,128]{2,1,0:T(8,128)S(1)}, u32[]{:S(2)}, u32[]{:S(2)}) collective-permute-start(f32[10,8,128]{2,1,0:T(8,128)S(1)} %get-tuple-element.77.chip_ref), channel_id=1, source_target_pairs={{0,128},{1,4},{2,130},{3,6},{4,1},{5,14},{6,3},{7,12},{14,5},{15,1... | collective-permute-start | bytes 122888 | tf_op jit(solution)/shard_map/ppermute | solution.py:588
  40.4 1.4 %collective-permute-start.10 = (f32[30,8,128]{2,1,0:T(8,128)S(1)}, f32[30,8,128]{2,1,0:T(8,128)S(1)}, u32[]{:S(2)}, u32[]{:S(2)}) collective-permute-start(f32[30,8,128]{2,1,0:T(8,128)S(1)} %side.2.mine_ref), channel_id=1, source_target_pairs={{0,1},{1,0},{2,3},{3,2},{4,5},{5,4},{6,7},{7,6},{14,15},{15,14},{1... | collective-permute-start | bytes 368648 | tf_op jit(solution)/shard_map/ppermute | solution.py:588
  43.2 3.8 %collective-permute-start.11 = (f32[17,8,128]{2,1,0:T(8,128)S(1)}, f32[17,8,128]{2,1,0:T(8,128)S(1)}, u32[]{:S(2)}, u32[]{:S(2)}) collective-permute-start(f32[17,8,128]{2,1,0:T(8,128)S(1)} %get-tuple-element.82), channel_id=1, source_target_pairs={{0,1},{1,0},{2,3},{3,2},{4,5},{5,4},{6,7},{7,6},{14,15},{15,14},{1... | collective-permute-start | bytes 208904 | tf_op jit(solution)/shard_map/ppermute | solution.py:588
  43.5 5.3 %collective-permute-start.12 = (f32[17,8,128]{2,1,0:T(8,128)S(1)}, f32[17,8,128]{2,1,0:T(8,128)S(1)}, u32[]{:S(2)}, u32[]{:S(2)}) collective-permute-start(f32[17,8,128]{2,1,0:T(8,128)S(1)} %get-tuple-element.83), channel_id=1, source_target_pairs={{0,128},{1,2},{2,1},{3,4},{4,3},{5,6},{6,5},{7,14},{14,7},{15,12},... | collective-permute-start | bytes 208904 | tf_op jit(solution)/shard_map/ppermute | solution.py:588
  49.2 2.2 %collective-permute-start.13 = (f32[17,8,128]{2,1,0:T(8,128)S(1)}, f32[17,8,128]{2,1,0:T(8,128)S(1)}, u32[]{:S(2)}, u32[]{:S(2)}) collective-permute-start(f32[17,8,128]{2,1,0:T(8,128)S(1)} %get-tuple-element.88), channel_id=1, source_target_pairs={{0,1},{1,0},{2,3},{3,2},{4,5},{5,4},{6,7},{7,6},{14,15},{15,14},{1... | collective-permute-start | bytes 208904 | tf_op jit(solution)/shard_map/ppermute | solution.py:588
  49.2 3.9 %collective-permute-start.14 = (f32[17,8,128]{2,1,0:T(8,128)S(1)}, f32[17,8,128]{2,1,0:T(8,128)S(1)}, u32[]{:S(2)}, u32[]{:S(2)}) collective-permute-start(f32[17,8,128]{2,1,0:T(8,128)S(1)} %get-tuple-element.89), channel_id=1, source_target_pairs={{0,128},{1,2},{2,1},{3,4},{4,3},{5,6},{6,5},{7,14},{14,7},{15,12},... | collective-permute-start | bytes 208904 | tf_op jit(solution)/shard_map/ppermute | solution.py:588
  53.5 2.4 %collective-permute-start.15 = (f32[17,8,128]{2,1,0:T(8,128)S(1)}, f32[17,8,128]{2,1,0:T(8,128)S(1)}, u32[]{:S(2)}, u32[]{:S(2)}) collective-permute-start(f32[17,8,128]{2,1,0:T(8,128)S(1)} %get-tuple-element.94), channel_id=1, source_target_pairs={{0,1},{1,0},{2,3},{3,2},{4,5},{5,4},{6,7},{7,6},{14,15},{15,14},{1... | collective-permute-start | bytes 208904 | tf_op jit(solution)/shard_map/ppermute | solution.py:588
  53.9 3.7 %collective-permute-start.16 = (f32[17,8,128]{2,1,0:T(8,128)S(1)}, f32[17,8,128]{2,1,0:T(8,128)S(1)}, u32[]{:S(2)}, u32[]{:S(2)}) collective-permute-start(f32[17,8,128]{2,1,0:T(8,128)S(1)} %get-tuple-element.95), channel_id=1, source_target_pairs={{0,128},{1,2},{2,1},{3,4},{4,3},{5,6},{6,5},{7,14},{14,7},{15,12},... | collective-permute-start | bytes 208904 | tf_op jit(solution)/shard_map/ppermute | solution.py:588
  58.0 1.4 %collective-permute-start.17 = (f32[22,8,128]{2,1,0:T(8,128)S(1)}, f32[22,8,128]{2,1,0:T(8,128)S(1)}, u32[]{:S(2)}, u32[]{:S(2)}) collective-permute-start(f32[22,8,128]{2,1,0:T(8,128)S(1)} %get-tuple-element.98), channel_id=1, source_target_pairs={{0,1},{1,0},{2,3},{3,2},{4,5},{5,4},{6,7},{7,6},{14,15},{15,14},{1... | collective-permute-start | bytes 270344 | tf_op jit(solution)/shard_map/ppermute | solution.py:588
  59.4 10.2 %collective-permute-start.18 = (f32[27,8,128]{2,1,0:T(8,128)S(1)}, f32[27,8,128]{2,1,0:T(8,128)S(1)}, u32[]{:S(2)}, u32[]{:S(2)}) collective-permute-start(f32[27,8,128]{2,1,0:T(8,128)S(1)} %get-tuple-element.101), channel_id=1, source_target_pairs={{0,128},{1,2},{2,1},{3,4},{4,3},{5,6},{6,5},{7,14},{14,7},{15,12},... | collective-permute-start | bytes 331784 | tf_op jit(solution)/shard_map/ppermute | solution.py:588
  61.3 5.2 %collective-permute-start.20 = (f32[10,8,128]{2,1,0:T(8,128)S(1)}, f32[10,8,128]{2,1,0:T(8,128)S(1)}, u32[]{:S(2)}, u32[]{:S(2)}) collective-permute-start(f32[10,8,128]{2,1,0:T(8,128)S(1)} %get-tuple-element.102.chip_ref), channel_id=1, source_target_pairs={{0,128},{1,6},{2,130},{3,14},{4,132},{5,12},{6,1},{7,10},{14,3},{1... | collective-permute-start | bytes 122888 | tf_op jit(solution)/shard_map/ppermute | solution.py:588
  64.7 4.9 %collective-permute-start.19 = (f32[10,8,128]{2,1,0:T(8,128)S(1)}, f32[10,8,128]{2,1,0:T(8,128)S(1)}, u32[]{:S(2)}, u32[]{:S(2)}) collective-permute-start(f32[10,8,128]{2,1,0:T(8,128)S(1)} %get-tuple-element.102.chip_ref), channel_id=1, source_target_pairs={{0,128},{1,4},{2,130},{3,6},{4,1},{5,14},{6,3},{7,12},{14,5},{15,1... | collective-permute-start | bytes 122888 | tf_op jit(solution)/shard_map/ppermute | solution.py:588
  69.7 1.4 %collective-permute-start.21 = (f32[30,8,128]{2,1,0:T(8,128)S(1)}, f32[30,8,128]{2,1,0:T(8,128)S(1)}, u32[]{:S(2)}, u32[]{:S(2)}) collective-permute-start(f32[30,8,128]{2,1,0:T(8,128)S(1)} %side.3.mine_ref), channel_id=1, source_target_pairs={{0,1},{1,0},{2,3},{3,2},{4,5},{5,4},{6,7},{7,6},{14,15},{15,14},{1... | collective-permute-start | bytes 368648 | tf_op jit(solution)/shard_map/ppermute | solution.py:588
  72.5 3.9 %collective-permute-start.22 = (f32[17,8,128]{2,1,0:T(8,128)S(1)}, f32[17,8,128]{2,1,0:T(8,128)S(1)}, u32[]{:S(2)}, u32[]{:S(2)}) collective-permute-start(f32[17,8,128]{2,1,0:T(8,128)S(1)} %get-tuple-element.107), channel_id=1, source_target_pairs={{0,1},{1,0},{2,3},{3,2},{4,5},{5,4},{6,7},{7,6},{14,15},{15,14},{1... | collective-permute-start | bytes 208904 | tf_op jit(solution)/shard_map/ppermute | solution.py:588
  72.7 5.5 %collective-permute-start.23 = (f32[17,8,128]{2,1,0:T(8,128)S(1)}, f32[17,8,128]{2,1,0:T(8,128)S(1)}, u32[]{:S(2)}, u32[]{:S(2)}) collective-permute-start(f32[17,8,128]{2,1,0:T(8,128)S(1)} %get-tuple-element.108), channel_id=1, source_target_pairs={{0,128},{1,2},{2,1},{3,4},{4,3},{5,6},{6,5},{7,14},{14,7},{15,12},... | collective-permute-start | bytes 208904 | tf_op jit(solution)/shard_map/ppermute | solution.py:588
  78.6 2.0 %collective-permute-start.24 = (f32[17,8,128]{2,1,0:T(8,128)S(1)}, f32[17,8,128]{2,1,0:T(8,128)S(1)}, u32[]{:S(2)}, u32[]{:S(2)}) collective-permute-start(f32[17,8,128]{2,1,0:T(8,128)S(1)} %get-tuple-element.109), channel_id=1, source_target_pairs={{0,1},{1,0},{2,3},{3,2},{4,5},{5,4},{6,7},{7,6},{14,15},{15,14},{1... | collective-permute-start | bytes 208904 | tf_op jit(solution)/shard_map/ppermute | solution.py:588
  78.7 3.9 %collective-permute-start.25 = (f32[17,8,128]{2,1,0:T(8,128)S(1)}, f32[17,8,128]{2,1,0:T(8,128)S(1)}, u32[]{:S(2)}, u32[]{:S(2)}) collective-permute-start(f32[17,8,128]{2,1,0:T(8,128)S(1)} %get-tuple-element.110), channel_id=1, source_target_pairs={{0,128},{1,2},{2,1},{3,4},{4,3},{5,6},{6,5},{7,14},{14,7},{15,12},... | collective-permute-start | bytes 208904 | tf_op jit(solution)/shard_map/ppermute | solution.py:588
  82.6 10.2 %collective-permute-start.26 = (f32[328,128]{1,0:T(8,128)S(1)}, f32[328,128]{1,0:T(8,128)S(1)}, u32[]{:S(2)}, u32[]{:S(2)}) collective-permute-start(f32[328,128]{1,0:T(8,128)S(1)} %get-tuple-element.112), channel_id=1, source_target_pairs={{0,0},{1,1},{2,2},{3,3},{4,4},{5,5},{6,6},{7,7},{14,8},{15,9},{12,... | collective-permute-start | bytes 503816 | tf_op jit(solution)/shard_map/ppermute | solution.py:588
  84.7 11.1 %collective-permute-start.27 = (f32[328,128]{1,0:T(8,128)S(1)}, f32[328,128]{1,0:T(8,128)S(1)}, u32[]{:S(2)}, u32[]{:S(2)}) collective-permute-start(f32[328,128]{1,0:T(8,128)S(1)} %residual.1), channel_id=1, source_target_pairs={{0,0},{1,1},{2,2},{3,3},{4,4},{5,5},{6,6},{7,7},{14,8},{15,9},{12,... | collective-permute-start | bytes 503816 | tf_op jit(solution)/shard_map/ppermute | solution.py:588
